TPU v7x, 32 devices: a whole 2x2x4 slice. The times are simulated.
32 devices in a mesh: outer: 2 (over core), inner: 16 (over z, y, x).
Axes of the slice: x: 2, y: 2, z: 4, core: 2. Of those that a mesh axis runs over, the one named last changes fastest.
Arguments:
- features: float32 [65536, 1024], P(('outer', 'inner'))
- dest: int32 [512], P(('outer', 'inner')), may hold values from 0 to 15, as said below
- slot: int32 [512], P(('outer', 'inner')), may hold values from 0 to 15, as said below
Outputs:
- standardized: float32 [65536, 1024], P(('outer', 'inner'))
- moments: float32 [2, 1024], replicated
Inputs may be any that keep to these rules, and one draw needn't show every extreme that they name: `dest`: blocks of one device name destinations in the same shuffle domain; from one device at most 1 block go to any one destination, and exactly 1 to each destination it names. Every device of a shuffle domain receives exactly 16 blocks, each with a different slot.
All inputs are finite; a program needn't handle non-finite values.
Results may differ from a plain program's by a relative error of at most 0.000031.
Values sent between devices are 32-bit elements; how exact they have to be, the bound alone decides.
No kernel may reach another device: no remote copies, remote signals or barrier semaphores. Data moves between devices by JAX's collectives and lax.ppermute only.
A program may use at most 128 MiB of HBM per device.

v0:
```python
import jax
import jax.numpy as jnp
from jax import lax
from jax.sharding import PartitionSpec as P

eps_value = 1e-06
clip_value = 3.0


def partner(array, axis, stride):
    return lax.ppermute(array, axis, [(i, i ^ 1 << stride) for i in range(lax.axis_size(axis))])


def merge_pair(center_a, spread_a, center_b, spread_b, half):
    gap = center_b - center_a
    return ((center_a + center_b) * 0.5, spread_a + spread_b + gap * gap * half)


def standardize(block_rows, center, factor):
    return jnp.clip((block_rows - center) * factor, -clip_value, clip_value)


def body(features, dest, slot):
    row_count, feat_width = features.shape
    block_count = dest.shape[0]
    block_rows = row_count // block_count
    peer_count = lax.axis_size("inner")
    outer_count = lax.axis_size("outer")
    capacity = max(1, block_count // peer_count)
    total_rows = row_count * peer_count * outer_count
    local_center = jnp.mean(features, axis=0)
    deviation = features - local_center
    local_spread = jnp.sum(deviation * deviation, axis=0)
    center, spread = (local_center, local_spread)
    level_count = row_count
    for bit_index in range(peer_count.bit_length() - 1):
        other_center, other_spread = partner((center, spread), "inner", bit_index)
        center, spread = merge_pair(center, spread, other_center, other_spread, level_count * 0.5)
        level_count = level_count * 2
    bit_index = 0
    other_center, other_spread = partner((center, spread), "outer", bit_index)
    center, spread = merge_pair(center, spread, other_center, other_spread, level_count * 0.5)
    variance = spread / total_rows
    factor = lax.rsqrt(variance + eps_value)
    peer_ids = jnp.arange(peer_count, dtype=jnp.int32)
    hits = (dest[:, None] == peer_ids[None, :]).astype(jnp.int32)
    earlier = jnp.cumsum(hits, axis=0) - hits
    within = jnp.sum(earlier * hits, axis=1)
    target_cell = dest * capacity + within
    cell_ids = jnp.arange(peer_count * capacity, dtype=jnp.int32)
    matches = target_cell[:, None] == cell_ids[None, :]
    block_ids = jnp.arange(block_count, dtype=jnp.int32)
    source_block = jnp.sum(jnp.where(matches, block_ids[:, None], 0), axis=0)
    occupied = jnp.any(matches, axis=0)
    sent_slot = jnp.where(occupied, slot[source_block], -1).reshape(peer_count, capacity)
    blocks = features.reshape(block_count, block_rows, feat_width)
    picked = jnp.where(occupied[:, None, None], blocks[source_block], 0.0)
    received = lax.all_to_all(
        picked.reshape(peer_count, capacity, block_rows, feat_width),
        "inner",
        split_axis=0,
        concat_axis=0,
        tiled=True,
    )
    got_slot = lax.all_to_all(sent_slot, "inner", split_axis=0, concat_axis=0, tiled=True)
    flat_blocks = received.reshape(peer_count * capacity, block_rows, feat_width)
    slot_hits = got_slot.reshape(-1)[:, None] == block_ids[None, :]
    chosen = jnp.sum(jnp.where(slot_hits, cell_ids[:, None], 0), axis=0)
    standardized = standardize(flat_blocks[chosen].reshape(row_count, feat_width), center, factor)
    return (standardized, jnp.stack([center, variance]))


def solution(mesh):
    in_specs = (P(("outer", "inner"), None), P(("outer", "inner")), P(("outer", "inner")))
    out_specs = (P(("outer", "inner"), None), P())
    return jax.shard_map(body, mesh=mesh, in_specs=in_specs, out_specs=out_specs, check_vma=False)
```

profile of v0, /device:TPU:5, one launch (start us, length us, event | category | flops | bytes accessed | tf_op | source)
XLA Modules:
  0.0 243.2 jit_solution(319188328067751697)
XLA Ops:
  0.6 0.7 fusion.3
  1.4 0.8 select_reduce_fusion.2
  2.3 0.7 add.75
  2.9 0.1 select_reduce_fusion.1
  3.0 0.1 fusion.2
  3.1 0.7 gather_fusion.1
  3.8 0.7 copy.6
  4.5 6.7 %all-to-all-start.1 = ((s32[16,1,1]{2,1,0:T(1,128)}), s32[16,1,1]{2,1,0:T(1,128)S(1)}, u32[]{:S(2)}, u32[]{:S(2)}) async-start(s32[16,1,1]{2,1,0:T(1,128)} %copy.6), calls=%async_computation.1 | async-start | bytes 16384 | tf_op jit(solution)/shard_map/all_to_all | solution.py:65
  11.2 7.9 %gather_fusion = f32[16,128,1024]{2,1,0:T(8,128)} fusion(f32[16,128,1024]{2,1,0:T(8,128)} %bitcast.22, s32[1024]{0:T(1024)S(1)} %pad_clamp_fusion.1), kind=kCustom, calls=%fused_computation | custom fusion | bytes 16777280 | tf_op jit(solution)/shard_map/gather | solution.py:57
  19.1 8.8 %bitcast_select_fusion = f32[16,1,128,1024]{3,2,1,0:T(8,128)} fusion(f32[16,128,1024]{2,1,0:T(8,128)} %gather_fusion, pred[16]{0:T(512)(128)(4,1)S(1)} %fusion.2), kind=kLoop, calls=%fused_computation.6 | loop fusion | flops 2097152 | bytes 16777232 | tf_op jit(solution)/shard_map/jit(_where)/select_n | solution.py:57
  27.9 6.4 %all-to-all-start = ((f32[16,1,128,1024]{3,2,1,0:T(8,128)}), f32[16,1,128,1024]{3,2,1,0:T(8,128)}, u32[]{:S(2)}, u32[]{:S(2)}) async-start(f32[16,1,128,1024]{3,2,1,0:T(8,128)} %bitcast_select_fusion), calls=%async_computation | async-start | bytes 16777216 | tf_op jit(solution)/shard_map/all_to_all | solution.py:58
  34.2 3.9 %reduce_sum.54 = f32[1024]{0:T(1024)S(1)} reduce(f32[2048,1024]{1,0:T(8,128)} %param.3, f32[]{:T(128)} %constant.8.clone.1), dimensions={0}, to_apply=%region_5.6 | reduce | flops 2096128 | bytes 8392708 | tf_op jit(solution)/shard_map/reduce_sum | solution.py:31
  38.1 1.2 collective-permute-start
  39.4 4.3 %multiply_reduce_fusion = f32[1024]{0:T(1024)S(1)} fusion(f32[2048,1024]{1,0:T(8,128)} %param.3, f32[1024]{0:T(1024)S(1)} %broadcast_multiply_fusion), kind=kLoop, calls=%fused_computation.7 | loop fusion | flops 6290432 | bytes 8396800 | tf_op jit(solution)/shard_map/reduce_sum | solution.py:33
  43.7 0.3 collective-permute-start.5
  44.0 17.2 %collective-permute-done = f32[1024]{0:T(1024)S(1)} collective-permute-done((f32[1024]{0:T(1024)S(1)}, f32[1024]{0:T(1024)S(1)}, u32[]{:S(2)}, u32[]{:S(2)}) %collective-permute-start) | collective-permute-done | bytes 4128 | tf_op jit(solution)/shard_map/ppermute | solution.py:11
  61.3 2.7 %collective-permute-start.1 = (f32[1024]{0:T(1024)S(1)}, f32[1024]{0:T(1024)S(1)}, u32[]{:S(2)}, u32[]{:S(2)}) collective-permute-start(f32[1024]{0:T(1024)S(1)} %get-tuple-element.12), channel_id=1, source_target_pairs={{0,2},{1,3},{2,0},{3,1},{4,6},{5,7},{6,4},{7,5},{8,10},{9,11},{10,... | collective-permute-start | bytes 12296 | tf_op jit(solution)/shard_map/ppermute | solution.py:11
  64.0 0.4 reduce
  64.4 4.3 %collective-permute-done.1 = f32[1024]{0:T(1024)S(1)} collective-permute-done((f32[1024]{0:T(1024)S(1)}, f32[1024]{0:T(1024)S(1)}, u32[]{:S(2)}, u32[]{:S(2)}) %collective-permute-start.1) | collective-permute-done | bytes 4128 | tf_op jit(solution)/shard_map/ppermute | solution.py:11
  68.8 1.3 collective-permute-start.2
  70.1 0.2 collective-permute-start.7
  70.2 0.1 select_reduce_fusion
  70.3 102.2 %collective-permute-done.2 = f32[1024]{0:T(1024)S(1)} collective-permute-done((f32[1024]{0:T(1024)S(1)}, f32[1024]{0:T(1024)S(1)}, u32[]{:S(2)}, u32[]{:S(2)}) %collective-permute-start.2) | collective-permute-done | bytes 4128 | tf_op jit(solution)/shard_map/ppermute | solution.py:11
  172.5 9.6 %collective-permute-start.3 = (f32[1024]{0:T(1024)S(1)}, f32[1024]{0:T(1024)S(1)}, u32[]{:S(2)}, u32[]{:S(2)}) collective-permute-start(f32[1024]{0:T(1024)S(1)} %get-tuple-element.8), channel_id=1, source_target_pairs={{0,8},{1,9},{2,10},{3,11},{4,12},{5,13},{6,14},{7,15},{8,0},{9,1},... | collective-permute-start | bytes 12296 | tf_op jit(solution)/shard_map/ppermute | solution.py:11
  182.2 40.8 %collective-permute-done.3 = f32[1024]{0:T(1024)S(1)} collective-permute-done((f32[1024]{0:T(1024)S(1)}, f32[1024]{0:T(1024)S(1)}, u32[]{:S(2)}, u32[]{:S(2)}) %collective-permute-start.3) | collective-permute-done | bytes 4128 | tf_op jit(solution)/shard_map/ppermute | solution.py:11
  223.0 0.1 collective-permute-done.8
  223.1 1.8 collective-permute-start.4
  225.0 0.7 collective-permute-done.4
  225.7 0.3 collective-permute-done.9
  226.1 0.6 pad_maximum_fusion
  226.7 7.7 %gather_fusion.2 = f32[16,128,1024]{2,1,0:T(8,128)} fusion(f32[16,128,1024]{2,1,0:T(8,128)} %bitcast.4, s32[1024]{0:T(1024)S(1)} %pad_clamp_fusion), kind=kCustom, calls=%fused_computation.2 | custom fusion | bytes 16777280 | tf_op jit(solution)/shard_map/gather | solution.py:69
  234.4 8.8 %fusion.1 = f32[2048,1024]{1,0:T(8,128)} fusion(f32[16,128,1024]{2,1,0:T(8,128)} %gather_fusion.2, f32[1024]{0:T(1024)S(1)} %get-tuple-element.2, f32[1024]{0:T(1024)S(1)} %get-tuple-element.4), kind=kLoop, calls=%fused_computation.5 | loop fusion | flops 6291456 | bytes 16785408 | tf_op jit(solution)/shard_map/jit(clip)/min | solution.py:20
  (22 shorter events, 0.6 us)
Async XLA Ops:
  0.6 2.5 %copy-start = (s32[16]{0:T(128)S(1)}, s32[16]{0:T(128)}, u32[]{:S(2)}) copy-start(s32[16]{0:T(128)} %param.5) | copy-start | bytes 196
  4.5 23.4 %all-to-all-start.1 = ((s32[16,1,1]{2,1,0:T(1,128)}), s32[16,1,1]{2,1,0:T(1,128)S(1)}, u32[]{:S(2)}, u32[]{:S(2)}) async-start(s32[16,1,1]{2,1,0:T(1,128)} %copy.6), calls=%async_computation.1 | async-start | bytes 16384 | tf_op jit(solution)/shard_map/all_to_all | solution.py:65
  27.9 198.8 %all-to-all-start = ((f32[16,1,128,1024]{3,2,1,0:T(8,128)}), f32[16,1,128,1024]{3,2,1,0:T(8,128)}, u32[]{:S(2)}, u32[]{:S(2)}) async-start(f32[16,1,128,1024]{3,2,1,0:T(8,128)} %bitcast_select_fusion), calls=%async_computation | async-start | bytes 16777216 | tf_op jit(solution)/shard_map/all_to_all | solution.py:58
  38.1 23.1 %collective-permute-start = (f32[1024]{0:T(1024)S(1)}, f32[1024]{0:T(1024)S(1)}, u32[]{:S(2)}, u32[]{:S(2)}) collective-permute-start(f32[1024]{0:T(1024)S(1)} %broadcast_multiply_fusion), channel_id=1, source_target_pairs={{0,1},{1,0},{2,3},{3,2},{4,5},{5,4},{6,7},{7,6},{8,9},{9,8},{10,11... | collective-permute-start | bytes 12296 | tf_op jit(solution)/shard_map/ppermute | solution.py:11
  43.7 17.6 %collective-permute-start.5 = (f32[1024]{0:T(1024)S(1)}, f32[1024]{0:T(1024)S(1)}, u32[]{:S(2)}, u32[]{:S(2)}) collective-permute-start(f32[1024]{0:T(1024)S(1)} %multiply_reduce_fusion), channel_id=1, source_target_pairs={{0,1},{1,0},{2,3},{3,2},{4,5},{5,4},{6,7},{7,6},{8,9},{9,8},{10,11... | collective-permute-start | bytes 12296 | tf_op jit(solution)/shard_map/ppermute | solution.py:11
  61.3 7.4 %collective-permute-start.1 = (f32[1024]{0:T(1024)S(1)}, f32[1024]{0:T(1024)S(1)}, u32[]{:S(2)}, u32[]{:S(2)}) collective-permute-start(f32[1024]{0:T(1024)S(1)} %get-tuple-element.12), channel_id=1, source_target_pairs={{0,2},{1,3},{2,0},{3,1},{4,6},{5,7},{6,4},{7,5},{8,10},{9,11},{10,... | collective-permute-start | bytes 12296 | tf_op jit(solution)/shard_map/ppermute | solution.py:11
  63.9 4.8 %collective-permute-start.6 = (f32[1024]{0:T(1024)S(1)}, f32[1024]{0:T(1024)S(1)}, u32[]{:S(2)}, u32[]{:S(2)}) collective-permute-start(f32[1024]{0:T(1024)S(1)} %get-tuple-element.11), channel_id=1, source_target_pairs={{0,2},{1,3},{2,0},{3,1},{4,6},{5,7},{6,4},{7,5},{8,10},{9,11},{10,... | collective-permute-start | bytes 12296 | tf_op jit(solution)/shard_map/ppermute | solution.py:11
  68.8 103.7 %collective-permute-start.2 = (f32[1024]{0:T(1024)S(1)}, f32[1024]{0:T(1024)S(1)}, u32[]{:S(2)}, u32[]{:S(2)}) collective-permute-start(f32[1024]{0:T(1024)S(1)} %get-tuple-element.10), channel_id=1, source_target_pairs={{0,4},{1,5},{2,6},{3,7},{4,0},{5,1},{6,2},{7,3},{8,12},{9,13},{10,... | collective-permute-start | bytes 12296 | tf_op jit(solution)/shard_map/ppermute | solution.py:11
  70.1 102.5 %collective-permute-start.7 = (f32[1024]{0:T(1024)S(1)}, f32[1024]{0:T(1024)S(1)}, u32[]{:S(2)}, u32[]{:S(2)}) collective-permute-start(f32[1024]{0:T(1024)S(1)} %get-tuple-element.9), channel_id=1, source_target_pairs={{0,4},{1,5},{2,6},{3,7},{4,0},{5,1},{6,2},{7,3},{8,12},{9,13},{10,... | collective-permute-start | bytes 12296 | tf_op jit(solution)/shard_map/ppermute | solution.py:11
  172.5 50.5 %collective-permute-start.3 = (f32[1024]{0:T(1024)S(1)}, f32[1024]{0:T(1024)S(1)}, u32[]{:S(2)}, u32[]{:S(2)}) collective-permute-start(f32[1024]{0:T(1024)S(1)} %get-tuple-element.8), channel_id=1, source_target_pairs={{0,8},{1,9},{2,10},{3,11},{4,12},{5,13},{6,14},{7,15},{8,0},{9,1},... | collective-permute-start | bytes 12296 | tf_op jit(solution)/shard_map/ppermute | solution.py:11
  182.1 41.0 %collective-permute-start.8 = (f32[1024]{0:T(1024)S(1)}, f32[1024]{0:T(1024)S(1)}, u32[]{:S(2)}, u32[]{:S(2)}) collective-permute-start(f32[1024]{0:T(1024)S(1)} %get-tuple-element.7), channel_id=1, source_target_pairs={{0,8},{1,9},{2,10},{3,11},{4,12},{5,13},{6,14},{7,15},{8,0},{9,1},... | collective-permute-start | bytes 12296 | tf_op jit(solution)/shard_map/ppermute | solution.py:11
  223.1 2.6 %collective-permute-start.4 = (f32[1024]{0:T(1024)S(1)}, f32[1024]{0:T(1024)S(1)}, u32[]{:S(2)}, u32[]{:S(2)}) collective-permute-start(f32[1024]{0:T(1024)S(1)} %get-tuple-element.6), channel_id=1, source_target_pairs={{0,16},{16,0},{1,17},{17,1},{2,18},{18,2},{3,19},{19,3},{4,20},{20... | collective-permute-start | bytes 12296 | tf_op jit(solution)/shard_map/ppermute | solution.py:11
  224.9 1.2 collective-permute-start.9
where the time goes:
time: 244 us; the launch traced here: 243 us
  waiting for transfers between devices  166 us (68%)
  starting transfers between devices  30.4 us (12%)
  other arithmetic  29.4 us (12%)
  local copies, waits for them, and re-layouts  16.9 us (7%)
    ppermute x10, waiting for transfers between devices, partner(): lax.ppermute(array, axis, [(i, i ^ 1 << stride) for i in range(lax.axis_s...  166 us
    ppermute x10, starting transfers between devices, partner(): lax.ppermute(array, axis, [(i, i ^ 1 << stride) for i in range(lax.axis_s...  17.3 us
    min x1, other arithmetic, standardize(): return jnp.clip((block_rows - center) * factor, -clip_value, clip_value)  8.82 us
    select_n x2, other arithmetic, body(): picked = jnp.where(occupied[:, None, None], blocks[source_block], 0.0)  8.79 us
    gather x1, local copies, waits for them, and re-layouts, body(): picked = jnp.where(occupied[:, None, None], blocks[source_block], 0.0)  7.86 us
    gather x1, local copies, waits for them, and re-layouts, body(): flat_blocks[chosen].reshape(row_count, feat_width)  7.67 us
    all_to_all x1, starting transfers between devices, body(): lax.all_to_all(sent_slot, 'inner', split_axis=0, concat_axis=0, tiled=True)  6.72 us
    all_to_all x1, starting transfers between devices, body(): lax.all_to_all(picked.reshape(peer_count, capacity, block_rows, feat_widt...  6.36 us
  transfers between devices with their start and end apart: 12, of which 10 were waited for; matrix products, arithmetic and copies ran while one was open for 11% of the time, Pallas kernels for 0%

commit v1 on v0

v1 whole, which is shorter than its diff:
```python
import functools

import jax
import jax.numpy as jnp
from jax import lax
from jax.experimental import pallas as pl
from jax.experimental.pallas import tpu as pltpu
from jax.sharding import PartitionSpec as P

eps_value = 1e-06
clip_value = 3.0
payload_rows = 4


def merge_pair(center_a, spread_a, center_b, spread_b, half):
    gap = center_b - center_a
    return ((center_a + center_b) * 0.5, spread_a + spread_b + gap * gap * half)


def invert(dest_ref, inverse):
    me = lax.axis_index("inner")

    def step(b, carry):
        inverse[dest_ref[b] ^ me] = b
        return carry

    lax.fori_loop(0, dest_ref.shape[0], step, 0)


def first_kernel(lanes, dest_ref, blocks_ref, *rest):
    outs, (inverse, sems) = rest[: len(lanes)], rest[len(lanes) :]
    invert(dest_ref, inverse)
    copies = [pltpu.make_async_copy(blocks_ref.at[inverse[lane]], out, sems.at[i]) for i, (lane, out) in enumerate(zip(lanes, outs))]
    for copy in copies:
        copy.start()
    for copy in copies:
        copy.wait()


def pick_first(lanes, dest, blocks):
    return pl.pallas_call(
        functools.partial(first_kernel, lanes),
        out_shape=[jax.ShapeDtypeStruct(blocks.shape[1:], blocks.dtype)] * len(lanes),
        in_specs=[pl.BlockSpec(memory_space=pltpu.SMEM), pl.BlockSpec(memory_space=pl.ANY)],
        out_specs=[pl.BlockSpec(memory_space=pl.ANY)] * len(lanes),
        scratch_shapes=[pltpu.SMEM((dest.shape[0],), jnp.int32), pltpu.SemaphoreType.DMA((len(lanes),))],
        name="pick_first",
    )(dest, blocks)


def rest_kernel(order, written, dest_ref, slot_ref, blocks_ref, payload_ref, *rest):
    outs, (held, inverse, in_sems, out_sems) = rest[: len(written)], rest[len(written) :]
    peers, rows, feats = held.shape
    row_count = peers * rows
    invert(dest_ref, inverse)
    for i, lane in enumerate(order):
        pltpu.make_async_copy(blocks_ref.at[inverse[lane]], held.at[i], in_sems.at[i]).start()

    def block_sum(i, fn):
        return jnp.sum(fn(held[i]).reshape(rows // 8, 8, feats), axis=0)

    total = jnp.zeros((8, feats), jnp.float32)
    for i, lane in enumerate(order):
        pltpu.make_async_copy(blocks_ref.at[inverse[lane]], held.at[i], in_sems.at[i]).wait()
        if lane in written:
            j = written.index(lane)
            pltpu.make_async_copy(held.at[i], outs[j], out_sems.at[j]).start()
        total = total + block_sum(i, lambda x: x)
    center = jnp.sum(total, axis=0, keepdims=True) / row_count

    def deviation(x):
        gap = x - center
        return gap * gap

    total = lax.fori_loop(0, peers, lambda i, acc: acc + block_sum(i, deviation), jnp.zeros((8, feats), jnp.float32))
    spread = jnp.sum(total, axis=0, keepdims=True)
    me = lax.axis_index("inner")
    for lane in range(peers):
        mark = jnp.full((payload_rows - 2, feats), slot_ref[inverse[lane]].astype(jnp.float32))
        payload_ref[lane ^ me] = jnp.concatenate([center, spread, mark], axis=0)
    for j in range(len(written)):
        pltpu.make_async_copy(held.at[order.index(written[j])], outs[j], out_sems.at[j]).wait()


def pick_rest(order, written, dest, slot, blocks):
    peers, rows, feats = blocks.shape
    smem, hbm = pl.BlockSpec(memory_space=pltpu.SMEM), pl.BlockSpec(memory_space=pl.ANY)
    res = pl.pallas_call(
        functools.partial(rest_kernel, order, written),
        out_shape=[jax.ShapeDtypeStruct((peers, payload_rows, feats), jnp.float32)]
        + [jax.ShapeDtypeStruct((rows, feats), blocks.dtype)] * len(written),
        in_specs=[smem, smem, hbm],
        out_specs=[pl.BlockSpec(memory_space=pltpu.VMEM)] + [hbm] * len(written),
        scratch_shapes=[
            pltpu.VMEM((peers, rows, feats), jnp.float32),
            pltpu.SMEM((peers,), jnp.int32),
            pltpu.SemaphoreType.DMA((peers,)),
            pltpu.SemaphoreType.DMA((len(written),)),
        ],
        compiler_params=pltpu.CompilerParams(vmem_limit_bytes=32 * 1024 * 1024),
        name="pick_rest",
    )(dest, slot, blocks)
    return res[0], res[1:]


def standardize(block_rows, center, factor):
    return jnp.clip((block_rows - center) * factor, -clip_value, clip_value)


def body(features, dest, slot):
    row_count, feat_width = features.shape
    peers = dest.shape[0]
    rows = row_count // peers
    outer_count = lax.axis_size("outer")
    total_rows = row_count * peers * outer_count
    blocks = features.reshape(peers, rows, feat_width)
    me = lax.axis_index("inner")

    far, near = list(range(peers // 2, peers)), list(range(1, peers // 2))
    lanes = [far[0]]
    for f, n in zip(far[1:], near):
        lanes += [n, f]
    first, later = lanes[:1], lanes[1:]
    picked = dict(zip(first, pick_first(first, dest, blocks)))
    order = later + [0] + first
    payload, rest = pick_rest(order, later + [0], dest, slot, blocks)
    picked.update(zip(later + [0], rest))

    def send(lane, block):
        return lax.ppermute(block, "inner", [(i, i ^ lane) for i in range(peers)])

    received = {lane: send(lane, picked[lane]) for lane in lanes}

    told = lax.all_to_all(payload, "inner", split_axis=0, concat_axis=0, tiled=True)
    got_slot = told[:, 2, 0].astype(jnp.int32)
    level_count = row_count
    centers, spreads = told[:, 0], told[:, 1]
    while centers.shape[0] > 1:
        centers, spreads = merge_pair(centers[0::2], spreads[0::2], centers[1::2], spreads[1::2], level_count * 0.5)
        level_count *= 2
    pair = jnp.concatenate([centers, spreads], axis=0)
    for bit in range(outer_count.bit_length() - 1):
        other = lax.ppermute(pair, "outer", [(i, i ^ 1 << bit) for i in range(outer_count)])
        center, spread = merge_pair(pair[0], pair[1], other[0], other[1], level_count * 0.5)
        level_count *= 2
        pair = jnp.stack([center, spread])
    center, variance = pair[0], pair[1] / total_rows
    factor = lax.rsqrt(variance + eps_value)

    by_lane = got_slot[me ^ jnp.arange(peers, dtype=jnp.int32)]
    out = jnp.zeros((row_count, feat_width), jnp.float32)
    for lane in [0] + lanes:
        block = picked[0] if lane == 0 else received[lane]
        out = lax.dynamic_update_slice(out, standardize(block, center, factor), (by_lane[lane] * rows, 0))
    return (out, jnp.stack([center, variance]))


def solution(mesh):
    in_specs = (P(("outer", "inner"), None), P(("outer", "inner")), P(("outer", "inner")))
    out_specs = (P(("outer", "inner"), None), P())
    return jax.shard_map(body, mesh=mesh, in_specs=in_specs, out_specs=out_specs, check_vma=False)
```

time: 244 us -> 239 us (0.980)
  the two profiles are of different devices: /device:TPU:5 before, /device:TPU:8 now
where the time goes in v1:
time: 239 us; the launch traced here: 236 us
  waiting for transfers between devices  127 us (53%)
  starting transfers between devices  48.3 us (20%)
  Pallas kernels  22.4 us (9%)
  local copies, waits for them, and re-layouts  19.4 us (8%)
  between operations  11.2 us (5%)
  other arithmetic  7.12 us (3%)
    ppermute x15, waiting for transfers between devices, send(): return lax.ppermute(block, 'inner', [(i, i ^ lane) for i in range(peers)])  127 us
    ppermute x15, starting transfers between devices, send(): return lax.ppermute(block, 'inner', [(i, i ^ lane) for i in range(peers)])  41 us
    pallas_call x1, Pallas kernels, pick_first(): pl.pallas_call(functools.partial(first_kernel, lanes), out_shape=[jax.Sha...  17.8 us
    unnamed x36, local copies, waits for them, and re-layouts  15.3 us
    all_to_all x1, starting transfers between devices, body(): lax.all_to_all(payload, 'inner', split_axis=0, concat_axis=0, tiled=True)  7.22 us
    dynamic_update_slice x16, other arithmetic, body(): lax.dynamic_update_slice(out, standardize(block, center, factor), (by_lan...  5.23 us
  transfers between devices with their start and end apart: 17, of which 11 were waited for; matrix products, arithmetic and copies ran while one was open for 5% of the time, Pallas kernels for 8%

profile of v1, /device:TPU:8, one launch (start us, length us, event | category | flops | bytes accessed | tf_op | source)
XLA Modules:
  0.0 235.6 jit_solution(11680424196882123136)
XLA Ops:
  0.6 3.4 %copy-done = f32[2048,1024]{1,0:T(8,128)S(1)} copy-done((f32[2048,1024]{1,0:T(8,128)S(1)}, f32[2048,1024]{1,0:T(8,128)}, u32[]{:S(2)}) %copy-start) | copy-done | bytes 8388632
  5.3 4.6 %pick_rest.1 = (f32[16,4,1024]{2,1,0:T(4,128)}, f32[128,1024]{1,0:T(8,128)S(1)}, f32[128,1024]{1,0:T(8,128)S(1)}, f32[128,1024]{1,0:T(8,128)S(1)}, f32[128,1024]...) custom-call(s32[16]{0:T(128)S(1)} %copy-done.1, ...), custom_call_target="tpu_custom_call" | custom-call | tf_op jit(solution)/shard_map/pick_rest/pallas_call | solution.py:88
  17.2 7.2 %all-to-all-start = ((f32[16,4,1024]{2,1,0:T(4,128)}), f32[16,4,1024]{2,1,0:T(4,128)S(1)}, u32[]{:S(2)}, u32[]{:S(2)}) async-start(f32[16,4,1024]{2,1,0:T(4,128)} %get-tuple-element.19), calls=%async_computation | async-start | bytes 524288 | tf_op jit(solution)/shard_map/all_to_all | solution.py:134
  24.4 17.8 %pick_first.1 = f32[128,1024]{1,0:T(8,128)} custom-call(s32[16]{0:T(128)} %dest_ref.3, f32[16,128,1024]{2,1,0:T(8,128)} %bitcast.25), custom_call_target="tpu_custom_call" | custom-call | tf_op jit(solution)/shard_map/pick_first/pallas_call | solution.py:41
  42.2 2.4 %collective-permute-start.1 = (f32[128,1024]{1,0:T(8,128)}, f32[128,1024]{1,0:T(8,128)}, u32[]{:S(2)}, u32[]{:S(2)}) collective-permute-start(f32[128,1024]{1,0:T(8,128)} %pick_first.1), channel_id=1, source_target_pairs={{0,8},{1,9},{2,10},{3,11},{4,12},{5,13},{6,14},{7,15},{8,0},{9,1},... | collective-permute-start | bytes 1572872 | tf_op jit(solution)/shard_map/ppermute | solution.py:130
  44.7 1.5 collective-permute-start.2
  46.7 1.5 collective-permute-start.4
  62.8 2.4 %collective-permute-start.5 = (f32[128,1024]{1,0:T(8,128)}, f32[128,1024]{1,0:T(8,128)S(1)}, u32[]{:S(2)}, u32[]{:S(2)}) collective-permute-start(f32[128,1024]{1,0:T(8,128)} %copy-done.13), channel_id=1, source_target_pairs={{0,10},{1,11},{2,8},{3,9},{4,14},{5,15},{6,12},{7,13},{8,2},{9,3},... | collective-permute-start | bytes 1572872 | tf_op jit(solution)/shard_map/ppermute | solution.py:130
  67.0 22.4 %collective-permute-done.1 = f32[128,1024]{1,0:T(8,128)} collective-permute-done((f32[128,1024]{1,0:T(8,128)}, f32[128,1024]{1,0:T(8,128)}, u32[]{:S(2)}, u32[]{:S(2)}) %collective-permute-start.1) | collective-permute-done | bytes 524320 | tf_op jit(solution)/shard_map/ppermute | solution.py:130
  89.4 2.4 %collective-permute-start.6 = (f32[128,1024]{1,0:T(8,128)S(1)}, f32[128,1024]{1,0:T(8,128)S(1)}, u32[]{:S(2)}, u32[]{:S(2)}) collective-permute-start(f32[128,1024]{1,0:T(8,128)S(1)} %copy-done.12), channel_id=1, source_target_pairs={{0,3},{1,2},{2,1},{3,0},{4,7},{5,6},{6,5},{7,4},{8,11},{9,10},{10,... | collective-permute-start | bytes 1572872 | tf_op jit(solution)/shard_map/ppermute | solution.py:130
  91.8 1.1 clamp_dynamic-update-slice_fusion.14
  92.9 3.4 %collective-permute-start.7 = (f32[128,1024]{1,0:T(8,128)S(1)}, f32[128,1024]{1,0:T(8,128)S(1)}, u32[]{:S(2)}, u32[]{:S(2)}) collective-permute-start(f32[128,1024]{1,0:T(8,128)S(1)} %copy-done.10), channel_id=1, source_target_pairs={{0,11},{1,10},{2,9},{3,8},{4,15},{5,14},{6,13},{7,12},{8,3},{9,2},... | collective-permute-start | bytes 1572872 | tf_op jit(solution)/shard_map/ppermute | solution.py:130
  96.3 1.1 clamp_dynamic-update-slice_fusion.13
  97.5 14.4 %collective-permute-done.3 = f32[128,1024]{1,0:T(8,128)} collective-permute-done((f32[128,1024]{1,0:T(8,128)}, f32[128,1024]{1,0:T(8,128)}, u32[]{:S(2)}, u32[]{:S(2)}) %collective-permute-start.3) | collective-permute-done | bytes 524320 | tf_op jit(solution)/shard_map/ppermute | solution.py:130
  111.9 3.4 %collective-permute-start.8 = (f32[128,1024]{1,0:T(8,128)S(1)}, f32[128,1024]{1,0:T(8,128)S(1)}, u32[]{:S(2)}, u32[]{:S(2)}) collective-permute-start(f32[128,1024]{1,0:T(8,128)S(1)} %copy-done.8), channel_id=1, source_target_pairs={{0,4},{1,5},{2,6},{3,7},{4,0},{5,1},{6,2},{7,3},{8,12},{9,13},{10,... | collective-permute-start | bytes 1572872 | tf_op jit(solution)/shard_map/ppermute | solution.py:130
  116.5 1.5 collective-permute-start.9
  119.0 4.8 %collective-permute-done.5 = f32[128,1024]{1,0:T(8,128)S(1)} collective-permute-done((f32[128,1024]{1,0:T(8,128)}, f32[128,1024]{1,0:T(8,128)S(1)}, u32[]{:S(2)}, u32[]{:S(2)}) %collective-permute-start.5) | collective-permute-done | bytes 524320 | tf_op jit(solution)/shard_map/ppermute | solution.py:130
  123.8 3.7 %collective-permute-start.10 = (f32[128,1024]{1,0:T(8,128)S(1)}, f32[128,1024]{1,0:T(8,128)S(1)}, u32[]{:S(2)}, u32[]{:S(2)}) collective-permute-start(f32[128,1024]{1,0:T(8,128)S(1)} %copy-done.4), channel_id=1, source_target_pairs={{0,5},{1,4},{2,7},{3,6},{4,1},{5,0},{6,3},{7,2},{8,13},{9,12},{10,... | collective-permute-start | bytes 1572872 | tf_op jit(solution)/shard_map/ppermute | solution.py:130
  127.5 2.4 %collective-permute-start.11 = (f32[128,1024]{1,0:T(8,128)S(1)}, f32[128,1024]{1,0:T(8,128)S(1)}, u32[]{:S(2)}, u32[]{:S(2)}) collective-permute-start(f32[128,1024]{1,0:T(8,128)S(1)} %get-tuple-element.29), channel_id=1, source_target_pairs={{0,13},{1,12},{2,15},{3,14},{4,9},{5,8},{6,11},{7,10},{8,5},{9,4},... | collective-permute-start | bytes 1572872 | tf_op jit(solution)/shard_map/ppermute | solution.py:130
  130.0 16.1 %collective-permute-done.7 = f32[128,1024]{1,0:T(8,128)S(1)} collective-permute-done((f32[128,1024]{1,0:T(8,128)S(1)}, f32[128,1024]{1,0:T(8,128)S(1)}, u32[]{:S(2)}, u32[]{:S(2)}) %collective-permute-start.7) | collective-permute-done | bytes 524320 | tf_op jit(solution)/shard_map/ppermute | solution.py:130
  146.1 3.8 %collective-permute-start.12 = (f32[128,1024]{1,0:T(8,128)S(1)}, f32[128,1024]{1,0:T(8,128)S(1)}, u32[]{:S(2)}, u32[]{:S(2)}) collective-permute-start(f32[128,1024]{1,0:T(8,128)S(1)} %get-tuple-element.30), channel_id=1, source_target_pairs={{0,6},{1,7},{2,4},{3,5},{4,2},{5,3},{6,0},{7,1},{8,14},{9,15},{10,... | collective-permute-start | bytes 1572872 | tf_op jit(solution)/shard_map/ppermute | solution.py:130
  149.9 16.9 %collective-permute-done.8 = f32[128,1024]{1,0:T(8,128)S(1)} collective-permute-done((f32[128,1024]{1,0:T(8,128)S(1)}, f32[128,1024]{1,0:T(8,128)S(1)}, u32[]{:S(2)}, u32[]{:S(2)}) %collective-permute-start.8) | collective-permute-done | bytes 524320 | tf_op jit(solution)/shard_map/ppermute | solution.py:130
  166.9 3.4 %collective-permute-start.13 = (f32[128,1024]{1,0:T(8,128)S(1)}, f32[128,1024]{1,0:T(8,128)S(1)}, u32[]{:S(2)}, u32[]{:S(2)}) collective-permute-start(f32[128,1024]{1,0:T(8,128)S(1)} %get-tuple-element.31), channel_id=1, source_target_pairs={{0,14},{1,15},{2,12},{3,13},{4,10},{5,11},{6,8},{7,9},{8,6},{9,7},... | collective-permute-start | bytes 1572872 | tf_op jit(solution)/shard_map/ppermute | solution.py:130
  170.4 4.3 %collective-permute-start.14 = (f32[128,1024]{1,0:T(8,128)S(1)}, f32[128,1024]{1,0:T(8,128)S(1)}, u32[]{:S(2)}, u32[]{:S(2)}) collective-permute-start(f32[128,1024]{1,0:T(8,128)S(1)} %get-tuple-element.32), channel_id=1, source_target_pairs={{0,7},{1,6},{2,5},{3,4},{4,3},{5,2},{6,1},{7,0},{8,15},{9,14},{10,... | collective-permute-start | bytes 1572872 | tf_op jit(solution)/shard_map/ppermute | solution.py:130
  174.8 14.5 %collective-permute-done.10 = f32[128,1024]{1,0:T(8,128)S(1)} collective-permute-done((f32[128,1024]{1,0:T(8,128)S(1)}, f32[128,1024]{1,0:T(8,128)S(1)}, u32[]{:S(2)}, u32[]{:S(2)}) %collective-permute-start.10) | collective-permute-done | bytes 524320 | tf_op jit(solution)/shard_map/ppermute | solution.py:130
  189.3 4.3 %collective-permute-start.15 = (f32[128,1024]{1,0:T(8,128)S(1)}, f32[128,1024]{1,0:T(8,128)S(1)}, u32[]{:S(2)}, u32[]{:S(2)}) collective-permute-start(f32[128,1024]{1,0:T(8,128)S(1)} %get-tuple-element.33), channel_id=1, source_target_pairs={{0,15},{1,14},{2,13},{3,12},{4,11},{5,10},{6,9},{7,8},{8,7},{9,6},... | collective-permute-start | bytes 1572872 | tf_op jit(solution)/shard_map/ppermute | solution.py:130
  193.8 2.2 collective-permute-done.11
  196.0 4.5 %collective-permute-done.12 = f32[128,1024]{1,0:T(8,128)S(1)} collective-permute-done((f32[128,1024]{1,0:T(8,128)S(1)}, f32[128,1024]{1,0:T(8,128)S(1)}, u32[]{:S(2)}, u32[]{:S(2)}) %collective-permute-start.12) | collective-permute-done | bytes 524320 | tf_op jit(solution)/shard_map/ppermute | solution.py:130
  200.7 20.8 %collective-permute-done.13 = f32[128,1024]{1,0:T(8,128)S(1)} collective-permute-done((f32[128,1024]{1,0:T(8,128)S(1)}, f32[128,1024]{1,0:T(8,128)S(1)}, u32[]{:S(2)}, u32[]{:S(2)}) %collective-permute-start.13) | collective-permute-done | bytes 524320 | tf_op jit(solution)/shard_map/ppermute | solution.py:130
  221.6 1.4 collective-permute-done.14
  223.1 9.0 %collective-permute-done.15 = f32[128,1024]{1,0:T(8,128)S(1)} collective-permute-done((f32[128,1024]{1,0:T(8,128)S(1)}, f32[128,1024]{1,0:T(8,128)S(1)}, u32[]{:S(2)}, u32[]{:S(2)}) %collective-permute-start.15) | collective-permute-done | bytes 524320 | tf_op jit(solution)/shard_map/ppermute | solution.py:130
  232.2 3.4 %copy-done.17 = f32[2048,1024]{1,0:T(8,128)} copy-done((f32[2048,1024]{1,0:T(8,128)}, f32[2048,1024]{1,0:T(8,128)S(1)}, u32[]{:S(2)}) %copy-start.17) | copy-done | bytes 8388632
  (83 shorter events, 18.2 us)
Async XLA Ops:
  0.6 3.4 %copy-start = (f32[2048,1024]{1,0:T(8,128)S(1)}, f32[2048,1024]{1,0:T(8,128)}, u32[]{:S(2)}) copy-start(f32[2048,1024]{1,0:T(8,128)} %param.3) | copy-start | bytes 25165828
  10.7 0.8 copy-start.5
  11.6 0.8 copy-start.7
  12.4 0.8 copy-start.9
  13.2 0.8 copy-start.11
  14.0 0.8 copy-start.13
  14.8 0.8 copy-start.14
  15.6 0.8 copy-start.15
  16.4 0.8 copy-start.16
  17.2 31.0 %all-to-all-start = ((f32[16,4,1024]{2,1,0:T(4,128)}), f32[16,4,1024]{2,1,0:T(4,128)S(1)}, u32[]{:S(2)}, u32[]{:S(2)}) async-start(f32[16,4,1024]{2,1,0:T(4,128)} %get-tuple-element.19), calls=%async_computation | async-start | bytes 524288 | tf_op jit(solution)/shard_map/all_to_all | solution.py:134
  42.2 47.2 %collective-permute-start.1 = (f32[128,1024]{1,0:T(8,128)}, f32[128,1024]{1,0:T(8,128)}, u32[]{:S(2)}, u32[]{:S(2)}) collective-permute-start(f32[128,1024]{1,0:T(8,128)} %pick_first.1), channel_id=1, source_target_pairs={{0,8},{1,9},{2,10},{3,11},{4,12},{5,13},{6,14},{7,15},{8,0},{9,1},... | collective-permute-start | bytes 1572872 | tf_op jit(solution)/shard_map/ppermute | solution.py:130
  44.7 48.2 %collective-permute-start.2 = (f32[128,1024]{1,0:T(8,128)}, f32[128,1024]{1,0:T(8,128)}, u32[]{:S(2)}, u32[]{:S(2)}) collective-permute-start(f32[128,1024]{1,0:T(8,128)} %copy-done.16), channel_id=1, source_target_pairs={{0,1},{1,0},{2,3},{3,2},{4,5},{5,4},{6,7},{7,6},{8,9},{9,8},{10,11... | collective-permute-start | bytes 1572872 | tf_op jit(solution)/shard_map/ppermute | solution.py:130
  46.1 65.7 %collective-permute-start.3 = (f32[128,1024]{1,0:T(8,128)}, f32[128,1024]{1,0:T(8,128)}, u32[]{:S(2)}, u32[]{:S(2)}) collective-permute-start(f32[128,1024]{1,0:T(8,128)} %copy-done.15), channel_id=1, source_target_pairs={{0,9},{1,8},{2,11},{3,10},{4,13},{5,12},{6,15},{7,14},{8,1},{9,0},... | collective-permute-start | bytes 1572872 | tf_op jit(solution)/shard_map/ppermute | solution.py:130
  46.7 69.8 %collective-permute-start.4 = (f32[128,1024]{1,0:T(8,128)}, f32[128,1024]{1,0:T(8,128)}, u32[]{:S(2)}, u32[]{:S(2)}) collective-permute-start(f32[128,1024]{1,0:T(8,128)} %copy-done.14), channel_id=1, source_target_pairs={{0,2},{1,3},{2,0},{3,1},{4,6},{5,7},{6,4},{7,5},{8,10},{9,11},{10,... | collective-permute-start | bytes 1572872 | tf_op jit(solution)/shard_map/ppermute | solution.py:130
  50.7 12.1 %collective-permute-start = (f32[2,1024]{1,0:T(2,128)S(1)}, f32[2,1024]{1,0:T(2,128)S(1)}, u32[]{:S(2)}, u32[]{:S(2)}) collective-permute-start(f32[2,1024]{1,0:T(2,128)S(1)} %pad_maximum_fusion), channel_id=1, source_target_pairs={{0,16},{16,0},{1,17},{17,1},{2,18},{18,2},{3,19},{19,3},{4,20},{20... | collective-permute-start | bytes 24584 | tf_op jit(solution)/shard_map/ppermute | solution.py:143
  62.7 26.7 %copy-start.12 = (f32[128,1024]{1,0:T(8,128)S(1)}, f32[128,1024]{1,0:T(8,128)}, u32[]{:S(2)}) copy-start(f32[128,1024]{1,0:T(8,128)} %copy-done.11) | copy-start | bytes 1572868
  62.8 30.1 %copy-start.10 = (f32[128,1024]{1,0:T(8,128)S(1)}, f32[128,1024]{1,0:T(8,128)}, u32[]{:S(2)}) copy-start(f32[128,1024]{1,0:T(8,128)} %copy-done.9) | copy-start | bytes 1572868
  62.8 49.1 %copy-start.8 = (f32[128,1024]{1,0:T(8,128)S(1)}, f32[128,1024]{1,0:T(8,128)}, u32[]{:S(2)}) copy-start(f32[128,1024]{1,0:T(8,128)} %copy-done.7) | copy-start | bytes 1572868
  62.8 53.7 %copy-start.6 = (f32[128,1024]{1,0:T(8,128)S(1)}, f32[128,1024]{1,0:T(8,128)}, u32[]{:S(2)}) copy-start(f32[128,1024]{1,0:T(8,128)} %copy-done.5) | copy-start | bytes 1572868
  62.8 61.0 %copy-start.4 = (f32[128,1024]{1,0:T(8,128)S(1)}, f32[128,1024]{1,0:T(8,128)}, u32[]{:S(2)}) copy-start(f32[128,1024]{1,0:T(8,128)} %copy-done.3) | copy-start | bytes 1572868
  62.8 61.0 %collective-permute-start.5 = (f32[128,1024]{1,0:T(8,128)}, f32[128,1024]{1,0:T(8,128)S(1)}, u32[]{:S(2)}, u32[]{:S(2)}) collective-permute-start(f32[128,1024]{1,0:T(8,128)} %copy-done.13), channel_id=1, source_target_pairs={{0,10},{1,11},{2,8},{3,9},{4,14},{5,15},{6,12},{7,13},{8,2},{9,3},... | collective-permute-start | bytes 1572872 | tf_op jit(solution)/shard_map/ppermute | solution.py:130
  89.4 38.1 %collective-permute-start.6 = (f32[128,1024]{1,0:T(8,128)S(1)}, f32[128,1024]{1,0:T(8,128)S(1)}, u32[]{:S(2)}, u32[]{:S(2)}) collective-permute-start(f32[128,1024]{1,0:T(8,128)S(1)} %copy-done.12), channel_id=1, source_target_pairs={{0,3},{1,2},{2,1},{3,0},{4,7},{5,6},{6,5},{7,4},{8,11},{9,10},{10,... | collective-permute-start | bytes 1572872 | tf_op jit(solution)/shard_map/ppermute | solution.py:130
  92.9 53.2 %collective-permute-start.7 = (f32[128,1024]{1,0:T(8,128)S(1)}, f32[128,1024]{1,0:T(8,128)S(1)}, u32[]{:S(2)}, u32[]{:S(2)}) collective-permute-start(f32[128,1024]{1,0:T(8,128)S(1)} %copy-done.10), channel_id=1, source_target_pairs={{0,11},{1,10},{2,9},{3,8},{4,15},{5,14},{6,13},{7,12},{8,3},{9,2},... | collective-permute-start | bytes 1572872 | tf_op jit(solution)/shard_map/ppermute | solution.py:130
  111.9 55.0 %collective-permute-start.8 = (f32[128,1024]{1,0:T(8,128)S(1)}, f32[128,1024]{1,0:T(8,128)S(1)}, u32[]{:S(2)}, u32[]{:S(2)}) collective-permute-start(f32[128,1024]{1,0:T(8,128)S(1)} %copy-done.8), channel_id=1, source_target_pairs={{0,4},{1,5},{2,6},{3,7},{4,0},{5,1},{6,2},{7,3},{8,12},{9,13},{10,... | collective-permute-start | bytes 1572872 | tf_op jit(solution)/shard_map/ppermute | solution.py:130
  116.5 53.9 %collective-permute-start.9 = (f32[128,1024]{1,0:T(8,128)S(1)}, f32[128,1024]{1,0:T(8,128)S(1)}, u32[]{:S(2)}, u32[]{:S(2)}) collective-permute-start(f32[128,1024]{1,0:T(8,128)S(1)} %copy-done.6), channel_id=1, source_target_pairs={{0,12},{1,13},{2,14},{3,15},{4,8},{5,9},{6,10},{7,11},{8,4},{9,5},... | collective-permute-start | bytes 1572872 | tf_op jit(solution)/shard_map/ppermute | solution.py:130
  123.8 65.5 %collective-permute-start.10 = (f32[128,1024]{1,0:T(8,128)S(1)}, f32[128,1024]{1,0:T(8,128)S(1)}, u32[]{:S(2)}, u32[]{:S(2)}) collective-permute-start(f32[128,1024]{1,0:T(8,128)S(1)} %copy-done.4), channel_id=1, source_target_pairs={{0,5},{1,4},{2,7},{3,6},{4,1},{5,0},{6,3},{7,2},{8,13},{9,12},{10,... | collective-permute-start | bytes 1572872 | tf_op jit(solution)/shard_map/ppermute | solution.py:130
  127.5 68.4 %collective-permute-start.11 = (f32[128,1024]{1,0:T(8,128)S(1)}, f32[128,1024]{1,0:T(8,128)S(1)}, u32[]{:S(2)}, u32[]{:S(2)}) collective-permute-start(f32[128,1024]{1,0:T(8,128)S(1)} %get-tuple-element.29), channel_id=1, source_target_pairs={{0,13},{1,12},{2,15},{3,14},{4,9},{5,8},{6,11},{7,10},{8,5},{9,4},... | collective-permute-start | bytes 1572872 | tf_op jit(solution)/shard_map/ppermute | solution.py:130
  146.1 54.5 %collective-permute-start.12 = (f32[128,1024]{1,0:T(8,128)S(1)}, f32[128,1024]{1,0:T(8,128)S(1)}, u32[]{:S(2)}, u32[]{:S(2)}) collective-permute-start(f32[128,1024]{1,0:T(8,128)S(1)} %get-tuple-element.30), channel_id=1, source_target_pairs={{0,6},{1,7},{2,4},{3,5},{4,2},{5,3},{6,0},{7,1},{8,14},{9,15},{10,... | collective-permute-start | bytes 1572872 | tf_op jit(solution)/shard_map/ppermute | solution.py:130
  166.9 54.6 %collective-permute-start.13 = (f32[128,1024]{1,0:T(8,128)S(1)}, f32[128,1024]{1,0:T(8,128)S(1)}, u32[]{:S(2)}, u32[]{:S(2)}) collective-permute-start(f32[128,1024]{1,0:T(8,128)S(1)} %get-tuple-element.31), channel_id=1, source_target_pairs={{0,14},{1,15},{2,12},{3,13},{4,10},{5,11},{6,8},{7,9},{8,6},{9,7},... | collective-permute-start | bytes 1572872 | tf_op jit(solution)/shard_map/ppermute | solution.py:130
  170.4 52.6 %collective-permute-start.14 = (f32[128,1024]{1,0:T(8,128)S(1)}, f32[128,1024]{1,0:T(8,128)S(1)}, u32[]{:S(2)}, u32[]{:S(2)}) collective-permute-start(f32[128,1024]{1,0:T(8,128)S(1)} %get-tuple-element.32), channel_id=1, source_target_pairs={{0,7},{1,6},{2,5},{3,4},{4,3},{5,2},{6,1},{7,0},{8,15},{9,14},{10,... | collective-permute-start | bytes 1572872 | tf_op jit(solution)/shard_map/ppermute | solution.py:130
  189.3 42.8 %collective-permute-start.15 = (f32[128,1024]{1,0:T(8,128)S(1)}, f32[128,1024]{1,0:T(8,128)S(1)}, u32[]{:S(2)}, u32[]{:S(2)}) collective-permute-start(f32[128,1024]{1,0:T(8,128)S(1)} %get-tuple-element.33), channel_id=1, source_target_pairs={{0,15},{1,14},{2,13},{3,12},{4,11},{5,10},{6,9},{7,8},{8,7},{9,6},... | collective-permute-start | bytes 1572872 | tf_op jit(solution)/shard_map/ppermute | solution.py:130
  232.2 3.4 %copy-start.17 = (f32[2048,1024]{1,0:T(8,128)}, f32[2048,1024]{1,0:T(8,128)S(1)}, u32[]{:S(2)}) copy-start(f32[2048,1024]{1,0:T(8,128)S(1)} %clamp_dynamic-update-slice_fusion) | copy-start | bytes 25165828
  (3 other events, 2.1 us)

commit v2 on v0

v2 whole, which is shorter than its diff:
```python
import functools

import jax
import jax.numpy as jnp
from jax import lax
from jax.experimental import pallas as pl
from jax.experimental.pallas import tpu as pltpu
from jax.sharding import PartitionSpec as P

eps_value = 1e-06
clip_value = 3.0
payload_rows = 4
window = 4
in_smem, in_vmem = pl.BlockSpec(memory_space=pltpu.SMEM), pl.BlockSpec(memory_space=pltpu.VMEM)
in_hbm, in_any = pl.BlockSpec(memory_space=pltpu.HBM), pl.BlockSpec(memory_space=pl.ANY)


def merge_pair(center_a, spread_a, center_b, spread_b, half):
    gap = center_b - center_a
    return ((center_a + center_b) * 0.5, spread_a + spread_b + gap * gap * half)


def pin(array, space=pltpu.HBM):
    return pltpu.with_memory_space_constraint(array, space)


def lane_order(peers):
    half = peers // 2
    far = list(range(0, half, 2)) + list(range(1, half, 2))
    near = list(range(1, half, 2)) + list(range(2, half, 2)) + [0]
    return [lane for f, n in zip(far, near) for lane in (half + f, n)]


def lane_base(peers):
    return lax.axis_index("inner") ^ ((lax.axis_index("outer") & 1) * (peers // 2))


def first_kernel(lanes, dest_ref, features_ref, inverse_ref, *rest):
    outs, sems = rest[:-1], rest[-1]
    peers, rows = dest_ref.shape[0], outs[0].shape[0]
    base = lane_base(peers)
    for b in range(peers):
        inverse_ref[dest_ref[b] ^ base] = b
    copies = []
    for i, lane in enumerate(lanes):
        start = pl.multiple_of(inverse_ref[lane] * rows, 8)
        copies.append(pltpu.make_async_copy(features_ref.at[pl.ds(start, rows)], outs[i], sems.at[i]))
        copies[-1].start()
    for copy in copies:
        copy.wait()


def pick_first(lanes, dest, features):
    count, (row_count, feats) = len(lanes), features.shape
    rows = row_count // dest.shape[0]
    res = pl.pallas_call(
        functools.partial(first_kernel, lanes),
        out_shape=[jax.ShapeDtypeStruct(dest.shape, jnp.int32)] + [pltpu.VMEM((rows, feats), features.dtype)] * count,
        in_specs=[in_smem, in_hbm],
        out_specs=[in_smem] + [in_vmem] * count,
        scratch_shapes=[pltpu.SemaphoreType.DMA((count,))],
        name="pick_first",
    )(dest, pin(features))
    return res[0], res[1:]


def rest_kernel(lanes, first, inverse_ref, slot_ref, features_ref, payload_ref, *rest):
    outs, (held, in_sems, out_sems) = rest[: len(lanes)], rest[len(lanes) :]
    peers, rows, feats = held.shape
    base = lane_base(peers)
    order = lanes + first
    fetches = []
    for lane in order:
        start = pl.multiple_of(inverse_ref[lane] * rows, 8)
        fetches.append(pltpu.make_async_copy(features_ref.at[pl.ds(start, rows)], held.at[lane], in_sems.at[lane]))
        fetches[-1].start()

    def fold(x):
        return jnp.sum(x.reshape(rows // 8, 8, feats), axis=0)

    stores, parts = [], []
    for i, lane in enumerate(order):
        fetches[i].wait()
        if i < len(lanes):
            stores.append(pltpu.make_async_copy(held.at[lane], outs[i], out_sems.at[i]))
            stores[-1].start()
        center = jnp.sum(fold(held[lane]), axis=0, keepdims=True) / rows
        gap = held[lane] - center
        parts.append((center, jnp.sum(fold(gap * gap), axis=0, keepdims=True)))
    level_count = rows
    while len(parts) > 1:
        parts = [merge_pair(*parts[i], *parts[i + 1], level_count * 0.5) for i in range(0, len(parts), 2)]
        level_count *= 2
    for lane in range(peers):
        mark = jnp.full((payload_rows - 2, feats), slot_ref[inverse_ref[lane]].astype(jnp.float32))
        payload_ref[lane ^ base] = jnp.concatenate(list(parts[0]) + [mark], axis=0)
    for store in stores:
        store.wait()


def pick_rest(lanes, first, inverse, slot, features):
    peers, (row_count, feats) = inverse.shape[0], features.shape
    rows = row_count // peers
    res = pl.pallas_call(
        functools.partial(rest_kernel, lanes, first),
        out_shape=[jax.ShapeDtypeStruct((peers, payload_rows, feats), jnp.float32)] + [pltpu.HBM((rows, feats), features.dtype)] * len(lanes),
        in_specs=[in_smem, in_smem, in_hbm],
        out_specs=[in_vmem] + [in_hbm] * len(lanes),
        scratch_shapes=[
            pltpu.VMEM((peers, rows, feats), jnp.float32),
            pltpu.SemaphoreType.DMA((peers,)),
            pltpu.SemaphoreType.DMA((len(lanes),)),
        ],
        compiler_params=pltpu.CompilerParams(vmem_limit_bytes=32 * 1024 * 1024),
        cost_estimate=pl.CostEstimate(flops=6 * features.size, bytes_accessed=8 * features.size, transcendentals=0),
        name="pick_rest",
    )(inverse, slot, pin(features))
    return res[0], res[1:]


def place_kernel(lanes, near_by, slot_ref, scale_ref, *rest):
    blocks, (out_ref, held, in_sems, out_sems) = rest[: len(lanes)], rest[-4:]
    _, parts, part_rows, _ = held.shape
    plan = []
    for n, lane in enumerate(lanes):
        start = slot_ref[lane] * (parts * part_rows)
        for i in range(parts):
            target = pl.ds(pl.multiple_of(start + i * part_rows, 8), part_rows)
            source = blocks[n].at[pl.ds(i * part_rows, part_rows)]
            fetch = None if near_by else pltpu.make_async_copy(source, held.at[n, i], in_sems.at[n, i])
            if fetch is not None:
                fetch.start()
            plan.append((n, i, source, fetch, pltpu.make_async_copy(held.at[n, i], out_ref.at[target], out_sems.at[n, i])))
    center, factor = scale_ref[0:1], scale_ref[1:2]
    for n, i, source, fetch, store in plan:
        if fetch is not None:
            fetch.wait()
        values = source[...] if fetch is None else held[n, i]
        held[n, i] = jnp.clip((values - center) * factor, -clip_value, clip_value)
        store.start()
    for *_, store in plan:
        store.wait()


def place(lanes, blocks, slots, scale, out, row_count, near_by):
    rows, feats = blocks[0].shape
    count, parts = len(lanes), max(1, rows // 32)
    space, spec = (pltpu.VMEM, in_vmem) if near_by else (pltpu.HBM, in_hbm)
    args = [slots, scale] + [pin(block, space) for block in blocks] + ([] if out is None else [pin(out)])
    return pl.pallas_call(
        functools.partial(place_kernel, lanes, near_by),
        out_shape=pltpu.HBM((row_count, feats), jnp.float32),
        in_specs=[in_smem, in_vmem] + [spec] * count + ([] if out is None else [in_hbm]),
        out_specs=in_hbm,
        scratch_shapes=[
            pltpu.VMEM((count, parts, rows // parts, feats), jnp.float32),
            pltpu.SemaphoreType.DMA((count, parts)),
            pltpu.SemaphoreType.DMA((count, parts)),
        ],
        input_output_aliases={} if out is None else {2 + count: 0},
        compiler_params=pltpu.CompilerParams(vmem_limit_bytes=32 * 1024 * 1024),
        cost_estimate=pl.CostEstimate(flops=4 * count * rows * feats, bytes_accessed=8 * count * rows * feats, transcendentals=0),
        name="place",
    )(*args)


def share_moments(told, row_count):
    peers = told.shape[0]
    outer_count = lax.axis_size("outer")
    slots = told[:, 2, 0].astype(jnp.int32)[lane_base(peers) ^ jnp.arange(peers, dtype=jnp.int32)]
    level_count = row_count
    centers, spreads = told[:, 0], told[:, 1]
    while centers.shape[0] > 1:
        centers, spreads = merge_pair(centers[0::2], spreads[0::2], centers[1::2], spreads[1::2], level_count * 0.5)
        level_count *= 2
    pair = jnp.concatenate([centers, spreads], axis=0)
    for bit in range(outer_count.bit_length() - 1):
        other = lax.ppermute(pair, "outer", [(i, i ^ 1 << bit) for i in range(outer_count)])
        center, spread = merge_pair(pair[0], pair[1], other[0], other[1], level_count * 0.5)
        level_count *= 2
        pair = jnp.stack([center, spread])
    center, variance = pair[0], pair[1] / level_count
    return slots, center, variance, jnp.stack([center, lax.rsqrt(variance + eps_value)])


def body(features, dest, slot):
    row_count, _ = features.shape
    peers, outer_count = dest.shape[0], lax.axis_size("outer")
    order = lane_order(peers)
    inverse, first = pick_first(order[:1], dest, features)
    payload, later = pick_rest(order[1:], order[:1], inverse, slot, features)
    picked, got = list(first) + list(later), []

    def send(block, lane):
        pairs = [(o * peers + i, o * peers + (i ^ lane ^ (o & 1) * (peers // 2))) for o in range(outer_count) for i in range(peers)]
        return lax.ppermute(block, ("outer", "inner"), pairs)

    def place_lanes(begin, end, out):
        return place(order[begin:end], got[begin:end], slots, scale, out, row_count, begin >= peers - window)

    out, placed = None, 0
    for j in range(peers):
        if j >= window:
            k = j - window
            values = [picked[j], got[k]]
            if k == 0:
                values.append(payload)
            elif k == window - 1:
                values.append(told)
            elif k > window and k % window == 0:
                out = place_lanes(placed, k, out)
                placed = k
                values.append(out)
            picked[j], got[k], *extra = lax.optimization_barrier(tuple(values))
            if k == 0:
                told = lax.all_to_all(extra[0], "inner", split_axis=0, concat_axis=0, tiled=True)
            elif k == window - 1:
                slots, center, variance, scale = share_moments(extra[0], row_count)
            elif extra:
                out = extra[0]
        got.append(send(picked[j], order[j]))
    for end in (peers - window, peers - window // 2, peers):
        out = place_lanes(placed, end, out)
        placed = end
    return (out, jnp.stack([center, variance]))


def solution(mesh):
    in_specs = (P(("outer", "inner"), None), P(("outer", "inner")), P(("outer", "inner")))
    out_specs = (P(("outer", "inner"), None), P())
    return jax.shard_map(body, mesh=mesh, in_specs=in_specs, out_specs=out_specs, check_vma=False)
```

time: 244 us -> 205 us (0.84)
  the two profiles are of different devices: /device:TPU:5 before, /device:TPU:8 now
where the time goes in v2:
time: 205 us; the launch traced here: 204 us
  waiting for transfers between devices  115 us (56%)
  starting transfers between devices  64.7 us (32%)
  Pallas kernels  21.3 us (10%)
    ppermute x16, waiting for transfers between devices, send(): return lax.ppermute(block, ('outer', 'inner'), pairs)  115 us
    ppermute x16, starting transfers between devices, send(): return lax.ppermute(block, ('outer', 'inner'), pairs)  54.1 us
    pallas_call x4, Pallas kernels, place(): pl.pallas_call(functools.partial(place_kernel, lanes, near_by), out_shape...  11.5 us
    all_to_all x1, starting transfers between devices, body(): lax.all_to_all(extra[0], 'inner', split_axis=0, concat_axis=0, tiled=True)  9.99 us
    pallas_call x1, Pallas kernels, pick_rest(): pl.pallas_call(functools.partial(rest_kernel, lanes, first), out_shape=[j...  7.45 us
  transfers between devices with their start and end apart: 18, of which 6 were waited for; matrix products, arithmetic and copies ran while one was open for 1% of the time, Pallas kernels for 8%

profile of v2, /device:TPU:8, one launch (start us, length us, event | category | flops | bytes accessed | tf_op | source)
XLA Modules:
  0.0 204.3 jit_solution(6169669063077162207)
XLA Ops:
  0.6 2.4 %pick_first.1 = (s32[16]{0:T(128)}, f32[128,1024]{1,0:T(8,128)S(1)}) custom-call(s32[16]{0:T(128)} %dest_ref.1, f32[2048,1024]{1,0:T(8,128)} %features_ref.3), custom_call_target="tpu_custom_call" | custom-call | tf_op jit(solution)/shard_map/pick_first/pallas_call | solution.py:56
  3.0 4.5 %collective-permute-start.1 = (f32[128,1024]{1,0:T(8,128)S(1)}, f32[128,1024]{1,0:T(8,128)S(1)}, u32[]{:S(2)}, u32[]{:S(2)}) collective-permute-start(f32[128,1024]{1,0:T(8,128)S(1)} %get-tuple-element.51), channel_id=1, source_target_pairs={{0,8},{1,9},{2,10},{3,11},{4,12},{5,13},{6,14},{7,15},{8,0},{9,1},... | collective-permute-start | bytes 1572872 | tf_op jit(solution)/shard_map/ppermute | solution.py:196
  7.6 0.6 copy-done.1
  8.2 7.4 %pick_rest.1 = (f32[16,4,1024]{2,1,0:T(4,128)}, f32[128,1024]{1,0:T(8,128)}, f32[128,1024]{1,0:T(8,128)}, f32[128,1024]{1,0:T(8,128)}, f32[128,1024]{1,0:T(8,128...) custom-call(s32[16]{0:T(128)S(1)} %copy-done.1, ...), custom_call_target="tpu_custom_call" | custom-call | flops 12582912 | bytes 16777216 | tf_op jit(solution)/shard_map/pick_rest/pallas_call | solution.py:104
  15.7 1.4 collective-permute-start.3
  17.0 1.5 collective-permute-start.12
  18.5 0.5 collective-permute-start
  19.0 21.8 %collective-permute-done.1.rest_0_ = f32[128,1024]{1,0:T(8,128)S(1)} collective-permute-done((f32[128,1024]{1,0:T(8,128)S(1)}, f32[128,1024]{1,0:T(8,128)S(1)}, u32[]{:S(2)}, u32[]{:S(2)}) %collective-permute-start.1) | collective-permute-done | bytes 524320 | tf_op jit(solution)/shard_map/ppermute | solution.py:196
  40.8 10.0 %all-to-all-start = ((f32[16,4,1024]{2,1,0:T(4,128)}), f32[16,4,1024]{2,1,0:T(4,128)S(1)}, u32[]{:S(2)}, u32[]{:S(2)}) async-start(f32[16,4,1024]{2,1,0:T(4,128)} %get-tuple-element.53), calls=%async_computation | async-start | bytes 524288 | tf_op jit(solution)/shard_map/all_to_all | solution.py:216
  50.8 1.5 collective-permute-start.10
  52.4 13.9 %collective-permute-start.4 = (f32[128,1024]{1,0:T(8,128)}, f32[128,1024]{1,0:T(8,128)}, u32[]{:S(2)}, u32[]{:S(2)}) collective-permute-start(f32[128,1024]{1,0:T(8,128)} %get-tuple-element.59), channel_id=1, source_target_pairs={{0,14},{1,15},{2,12},{3,13},{4,10},{5,11},{6,8},{7,9},{8,6},{9,7},... | collective-permute-start | bytes 1572872 | tf_op jit(solution)/shard_map/ppermute | solution.py:196
  66.3 6.0 %collective-permute-start.13 = (f32[128,1024]{1,0:T(8,128)}, f32[128,1024]{1,0:T(8,128)}, u32[]{:S(2)}, u32[]{:S(2)}) collective-permute-start(f32[128,1024]{1,0:T(8,128)} %get-tuple-element.79), channel_id=1, source_target_pairs={{0,5},{1,4},{2,7},{3,6},{4,1},{5,0},{6,3},{7,2},{8,13},{9,12},{10,... | collective-permute-start | bytes 1572872 | tf_op jit(solution)/shard_map/ppermute | solution.py:196
  72.3 0.2 copy.10
  72.7 2.1 %collective-permute-start.7 = (f32[128,1024]{1,0:T(8,128)}, f32[128,1024]{1,0:T(8,128)}, u32[]{:S(2)}, u32[]{:S(2)}) collective-permute-start(f32[128,1024]{1,0:T(8,128)} %get-tuple-element.64), channel_id=1, source_target_pairs={{0,7},{1,6},{2,5},{3,4},{4,3},{5,2},{6,1},{7,0},{8,15},{9,14},{10,... | collective-permute-start | bytes 1572872 | tf_op jit(solution)/shard_map/ppermute | solution.py:196
  75.0 10.5 %collective-permute-done.10.rest_4_ = f32[128,1024]{1,0:T(8,128)S(1)} collective-permute-done((f32[128,1024]{1,0:T(8,128)}, f32[128,1024]{1,0:T(8,128)S(1)}, u32[]{:S(2)}, u32[]{:S(2)}) %collective-permute-start.10) | collective-permute-done | bytes 524320 | tf_op jit(solution)/shard_map/ppermute | solution.py:196
  85.5 34.5 %collective-permute-done.4.rest_6_ = f32[128,1024]{1,0:T(8,128)} collective-permute-done((f32[128,1024]{1,0:T(8,128)}, f32[128,1024]{1,0:T(8,128)}, u32[]{:S(2)}, u32[]{:S(2)}) %collective-permute-start.4) | collective-permute-done | bytes 524320 | tf_op jit(solution)/shard_map/ppermute | solution.py:196
  120.1 5.2 %collective-permute-start.8 = (f32[128,1024]{1,0:T(8,128)}, f32[128,1024]{1,0:T(8,128)}, u32[]{:S(2)}, u32[]{:S(2)}) collective-permute-start(f32[128,1024]{1,0:T(8,128)} %get-tuple-element.65), channel_id=1, source_target_pairs={{0,4},{1,5},{2,6},{3,7},{4,0},{5,1},{6,2},{7,3},{8,12},{9,13},{10,... | collective-permute-start | bytes 1572872 | tf_op jit(solution)/shard_map/ppermute | solution.py:196
  125.3 0.6 collective-permute-start.2
  125.8 0.4 convert_reduce_fusion
  126.2 0.7 gather_fusion
  127.0 0.6 pad_maximum_fusion
  127.6 5.0 %place.4.rest_4_ = f32[2048,1024]{1,0:T(8,128)} custom-call(s32[16]{0:T(128)S(1)} %gather_fusion, f32[2,1024]{1,0:T(2,128)S(1)} %get-tuple-element.106.scale_ref, f32[128,1024]{1,0:T(8,128)} %copy-done.2, f32[128,1024]{1,0:T(8,128)} %copy-done.4, f32[128,1024]{1,0:T(8,128)} %copy-done.3, f32[128,1024]{1,0:T(8,128)} %copy-done.5, f32[128,1024]{1,0:T(8,128)} %copy-done.6, ...), custom_call_target="tpu_custom_call" | custom-call | flops 4194304 | bytes 8388608 | tf_op jit(solution)/shard_map/place/pallas_call | solution.py:150
  132.6 15.6 %collective-permute-done.5.rest_2_ = f32[128,1024]{1,0:T(8,128)} collective-permute-done((f32[128,1024]{1,0:T(8,128)}, f32[128,1024]{1,0:T(8,128)}, u32[]{:S(2)}, u32[]{:S(2)}) %collective-permute-start.5) | collective-permute-done | bytes 524320 | tf_op jit(solution)/shard_map/ppermute | solution.py:196
  148.2 10.1 %collective-permute-start.6 = (f32[128,1024]{1,0:T(8,128)S(1)}, f32[128,1024]{1,0:T(8,128)S(1)}, u32[]{:S(2)}, u32[]{:S(2)}) collective-permute-start(f32[128,1024]{1,0:T(8,128)S(1)} %copy-done.8), channel_id=1, source_target_pairs={{0,15},{1,14},{2,13},{3,12},{4,11},{5,10},{6,9},{7,8},{8,7},{9,6},... | collective-permute-start | bytes 1572872 | tf_op jit(solution)/shard_map/ppermute | solution.py:196
  158.3 4.0 %collective-permute-start.16 = (f32[128,1024]{1,0:T(8,128)S(1)}, f32[128,1024]{1,0:T(8,128)S(1)}, u32[]{:S(2)}, u32[]{:S(2)}) collective-permute-start(f32[128,1024]{1,0:T(8,128)S(1)} %copy-done.10), channel_id=1, source_target_pairs={{0,6},{1,7},{2,4},{3,5},{4,2},{5,3},{6,0},{7,1},{8,14},{9,15},{10,... | collective-permute-start | bytes 1572872 | tf_op jit(solution)/shard_map/ppermute | solution.py:196
  162.3 2.8 %collective-permute-start.14 = (f32[128,1024]{1,0:T(8,128)S(1)}, f32[128,1024]{1,0:T(8,128)S(1)}, u32[]{:S(2)}, u32[]{:S(2)}) collective-permute-start(f32[128,1024]{1,0:T(8,128)S(1)} %copy-done.9), channel_id=1, source_target_pairs={{0,13},{1,12},{2,15},{3,14},{4,9},{5,8},{6,11},{7,10},{8,5},{9,4},... | collective-permute-start | bytes 1572872 | tf_op jit(solution)/shard_map/ppermute | solution.py:196
  165.1 0.7 collective-permute-start.9
  165.7 3.1 %place.5.rest_2_ = f32[2048,1024]{1,0:T(8,128)} custom-call(s32[16]{0:T(128)S(1)} %gather_fusion, f32[2,1024]{1,0:T(2,128)S(1)} %get-tuple-element.106.scale_ref, f32[128,1024]{1,0:T(8,128)} %collective-permute-done.11.rest_0_, f32[128,1024]{1,0:T(8,128)} %collective-permute-done.15.rest_1_, ...), custom_call_target="tpu_custom_call", output_to_operand_aliasing={{}: (6, {})} | custom-call | flops 2097152 | bytes 4194304 | tf_op jit(solution)/shard_map/place/pallas_call | solution.py:150
  168.9 17.6 %collective-permute-done.16.rest_1_ = f32[128,1024]{1,0:T(8,128)S(1)} collective-permute-done((f32[128,1024]{1,0:T(8,128)S(1)}, f32[128,1024]{1,0:T(8,128)S(1)}, u32[]{:S(2)}, u32[]{:S(2)}) %collective-permute-start.16) | collective-permute-done | bytes 524320 | tf_op jit(solution)/shard_map/ppermute | solution.py:196
  186.4 14.5 %collective-permute-done.14.rest_0_ = f32[128,1024]{1,0:T(8,128)S(1)} collective-permute-done((f32[128,1024]{1,0:T(8,128)S(1)}, f32[128,1024]{1,0:T(8,128)S(1)}, u32[]{:S(2)}, u32[]{:S(2)}) %collective-permute-start.14) | collective-permute-done | bytes 524320 | tf_op jit(solution)/shard_map/ppermute | solution.py:196
  201.0 1.7 place.6.rest_2_
  202.7 1.7 place.7
  (57 shorter events, 0.5 us)
Async XLA Ops:
  0.6 6.9 %copy-start = (s32[16]{0:T(128)S(1)}, s32[16]{0:T(128)}, u32[]{:S(2)}) copy-start(s32[16]{0:T(128)} %slot_ref.1) | copy-start | bytes 196
  3.0 37.8 %collective-permute-start.1 = (f32[128,1024]{1,0:T(8,128)S(1)}, f32[128,1024]{1,0:T(8,128)S(1)}, u32[]{:S(2)}, u32[]{:S(2)}) collective-permute-start(f32[128,1024]{1,0:T(8,128)S(1)} %get-tuple-element.51), channel_id=1, source_target_pairs={{0,8},{1,9},{2,10},{3,11},{4,12},{5,13},{6,14},{7,15},{8,0},{9,1},... | collective-permute-start | bytes 1572872 | tf_op jit(solution)/shard_map/ppermute | solution.py:196
  7.6 0.7 copy-start.1
  15.7 36.7 %collective-permute-start.3 = (f32[128,1024]{1,0:T(8,128)}, f32[128,1024]{1,0:T(8,128)S(1)}, u32[]{:S(2)}, u32[]{:S(2)}) collective-permute-start(f32[128,1024]{1,0:T(8,128)} %get-tuple-element.58), channel_id=1, source_target_pairs={{0,10},{1,11},{2,8},{3,9},{4,14},{5,15},{6,12},{7,13},{8,2},{9,3},... | collective-permute-start | bytes 1572872 | tf_op jit(solution)/shard_map/ppermute | solution.py:196
  17.0 49.3 %collective-permute-start.12 = (f32[128,1024]{1,0:T(8,128)}, f32[128,1024]{1,0:T(8,128)S(1)}, u32[]{:S(2)}, u32[]{:S(2)}) collective-permute-start(f32[128,1024]{1,0:T(8,128)} %get-tuple-element.73), channel_id=1, source_target_pairs={{0,1},{1,0},{2,3},{3,2},{4,5},{5,4},{6,7},{7,6},{8,9},{9,8},{10,11... | collective-permute-start | bytes 1572872 | tf_op jit(solution)/shard_map/ppermute | solution.py:196
  18.5 53.8 %collective-permute-start = (f32[128,1024]{1,0:T(8,128)}, f32[128,1024]{1,0:T(8,128)S(1)}, u32[]{:S(2)}, u32[]{:S(2)}) collective-permute-start(f32[128,1024]{1,0:T(8,128)} %get-tuple-element.49), channel_id=1, source_target_pairs={{0,3},{1,2},{2,1},{3,0},{4,7},{5,6},{6,5},{7,4},{8,11},{9,10},{10,... | collective-permute-start | bytes 1572872 | tf_op jit(solution)/shard_map/ppermute | solution.py:196
  40.8 86.8 %copy-start.2 = (f32[128,1024]{1,0:T(8,128)}, f32[128,1024]{1,0:T(8,128)S(1)}, u32[]{:S(2)}) copy-start(f32[128,1024]{1,0:T(8,128)S(1)} %collective-permute-done.1.rest_0_) | copy-start | bytes 1572868
  40.8 31.5 %all-to-all-start = ((f32[16,4,1024]{2,1,0:T(4,128)}), f32[16,4,1024]{2,1,0:T(4,128)S(1)}, u32[]{:S(2)}, u32[]{:S(2)}) async-start(f32[16,4,1024]{2,1,0:T(4,128)} %get-tuple-element.53), calls=%async_computation | async-start | bytes 524288 | tf_op jit(solution)/shard_map/all_to_all | solution.py:216
  50.8 34.7 %collective-permute-start.10 = (f32[128,1024]{1,0:T(8,128)}, f32[128,1024]{1,0:T(8,128)S(1)}, u32[]{:S(2)}, u32[]{:S(2)}) collective-permute-start(f32[128,1024]{1,0:T(8,128)} %get-tuple-element.69), channel_id=1, source_target_pairs={{0,12},{1,13},{2,14},{3,15},{4,8},{5,9},{6,10},{7,11},{8,4},{9,5},... | collective-permute-start | bytes 1572872 | tf_op jit(solution)/shard_map/ppermute | solution.py:196
  52.4 75.2 %copy-start.3 = (f32[128,1024]{1,0:T(8,128)}, f32[128,1024]{1,0:T(8,128)S(1)}, u32[]{:S(2)}) copy-start(f32[128,1024]{1,0:T(8,128)S(1)} %collective-permute-done.3.rest_2_) | copy-start | bytes 1572868
  52.4 67.7 %collective-permute-start.4 = (f32[128,1024]{1,0:T(8,128)}, f32[128,1024]{1,0:T(8,128)}, u32[]{:S(2)}, u32[]{:S(2)}) collective-permute-start(f32[128,1024]{1,0:T(8,128)} %get-tuple-element.59), channel_id=1, source_target_pairs={{0,14},{1,15},{2,12},{3,13},{4,10},{5,11},{6,8},{7,9},{8,6},{9,7},... | collective-permute-start | bytes 1572872 | tf_op jit(solution)/shard_map/ppermute | solution.py:196
  66.3 61.3 %copy-start.4 = (f32[128,1024]{1,0:T(8,128)}, f32[128,1024]{1,0:T(8,128)S(1)}, u32[]{:S(2)}) copy-start(f32[128,1024]{1,0:T(8,128)S(1)} %collective-permute-done.12.rest_1_) | copy-start | bytes 1572868
  66.3 53.8 %collective-permute-start.13 = (f32[128,1024]{1,0:T(8,128)}, f32[128,1024]{1,0:T(8,128)}, u32[]{:S(2)}, u32[]{:S(2)}) collective-permute-start(f32[128,1024]{1,0:T(8,128)} %get-tuple-element.79), channel_id=1, source_target_pairs={{0,5},{1,4},{2,7},{3,6},{4,1},{5,0},{6,3},{7,2},{8,13},{9,12},{10,... | collective-permute-start | bytes 1572872 | tf_op jit(solution)/shard_map/ppermute | solution.py:196
  72.3 55.3 %copy-start.5 = (f32[128,1024]{1,0:T(8,128)}, f32[128,1024]{1,0:T(8,128)S(1)}, u32[]{:S(2)}) copy-start(f32[128,1024]{1,0:T(8,128)S(1)} %collective-permute-done.rest_3_) | copy-start | bytes 1572868
  72.7 47.4 %collective-permute-start.7 = (f32[128,1024]{1,0:T(8,128)}, f32[128,1024]{1,0:T(8,128)}, u32[]{:S(2)}, u32[]{:S(2)}) collective-permute-start(f32[128,1024]{1,0:T(8,128)} %get-tuple-element.64), channel_id=1, source_target_pairs={{0,7},{1,6},{2,5},{3,4},{4,3},{5,2},{6,1},{7,0},{8,15},{9,14},{10,... | collective-permute-start | bytes 1572872 | tf_op jit(solution)/shard_map/ppermute | solution.py:196
  85.5 42.1 %copy-start.6 = (f32[128,1024]{1,0:T(8,128)}, f32[128,1024]{1,0:T(8,128)S(1)}, u32[]{:S(2)}) copy-start(f32[128,1024]{1,0:T(8,128)S(1)} %collective-permute-done.10.rest_4_) | copy-start | bytes 1572868
  85.5 76.7 %collective-permute-start.11 = (f32[128,1024]{1,0:T(8,128)}, f32[128,1024]{1,0:T(8,128)}, u32[]{:S(2)}, u32[]{:S(2)}) collective-permute-start(f32[128,1024]{1,0:T(8,128)} %get-tuple-element.70), channel_id=1, source_target_pairs={{0,9},{1,8},{2,11},{3,10},{4,13},{5,12},{6,15},{7,14},{8,1},{9,0},... | collective-permute-start | bytes 1572872 | tf_op jit(solution)/shard_map/ppermute | solution.py:196
  120.1 28.1 %collective-permute-start.5 = (f32[128,1024]{1,0:T(8,128)}, f32[128,1024]{1,0:T(8,128)}, u32[]{:S(2)}, u32[]{:S(2)}) collective-permute-start(f32[128,1024]{1,0:T(8,128)} %get-tuple-element.60), channel_id=1, source_target_pairs={{0,11},{1,10},{2,9},{3,8},{4,15},{5,14},{6,13},{7,12},{8,3},{9,2},... | collective-permute-start | bytes 1572872 | tf_op jit(solution)/shard_map/ppermute | solution.py:196
  120.1 38.2 %collective-permute-start.15 = (f32[128,1024]{1,0:T(8,128)}, f32[128,1024]{1,0:T(8,128)}, u32[]{:S(2)}, u32[]{:S(2)}) collective-permute-start(f32[128,1024]{1,0:T(8,128)} %get-tuple-element.85), channel_id=1, source_target_pairs={{0,2},{1,3},{2,0},{3,1},{4,6},{5,7},{6,4},{7,5},{8,10},{9,11},{10,... | collective-permute-start | bytes 1572872 | tf_op jit(solution)/shard_map/ppermute | solution.py:196
  120.1 45.0 %collective-permute-start.8 = (f32[128,1024]{1,0:T(8,128)}, f32[128,1024]{1,0:T(8,128)}, u32[]{:S(2)}, u32[]{:S(2)}) collective-permute-start(f32[128,1024]{1,0:T(8,128)} %get-tuple-element.65), channel_id=1, source_target_pairs={{0,4},{1,5},{2,6},{3,7},{4,0},{5,1},{6,2},{7,3},{8,12},{9,13},{10,... | collective-permute-start | bytes 1572872 | tf_op jit(solution)/shard_map/ppermute | solution.py:196
  125.3 1.7 collective-permute-start.2
  126.9 21.3 %copy-start.8 = (f32[128,1024]{1,0:T(8,128)S(1)}, f32[128,1024]{1,0:T(8,128)}, u32[]{:S(2)}) copy-start(f32[128,1024]{1,0:T(8,128)} %get-tuple-element.61) | copy-start | bytes 1572868
  126.9 31.4 %copy-start.10 = (f32[128,1024]{1,0:T(8,128)S(1)}, f32[128,1024]{1,0:T(8,128)}, u32[]{:S(2)}) copy-start(f32[128,1024]{1,0:T(8,128)} %get-tuple-element.86) | copy-start | bytes 1572868
  126.9 35.4 %copy-start.9 = (f32[128,1024]{1,0:T(8,128)S(1)}, f32[128,1024]{1,0:T(8,128)}, u32[]{:S(2)}) copy-start(f32[128,1024]{1,0:T(8,128)} %get-tuple-element.83) | copy-start | bytes 1572868
  126.9 38.1 %copy-start.7 = (f32[128,1024]{1,0:T(8,128)S(1)}, f32[128,1024]{1,0:T(8,128)}, u32[]{:S(2)}) copy-start(f32[128,1024]{1,0:T(8,128)} %get-tuple-element.66) | copy-start | bytes 1572868
  148.2 54.4 %collective-permute-start.6 = (f32[128,1024]{1,0:T(8,128)S(1)}, f32[128,1024]{1,0:T(8,128)S(1)}, u32[]{:S(2)}, u32[]{:S(2)}) collective-permute-start(f32[128,1024]{1,0:T(8,128)S(1)} %copy-done.8), channel_id=1, source_target_pairs={{0,15},{1,14},{2,13},{3,12},{4,11},{5,10},{6,9},{7,8},{8,7},{9,6},... | collective-permute-start | bytes 1572872 | tf_op jit(solution)/shard_map/ppermute | solution.py:196
  158.3 28.2 %collective-permute-start.16 = (f32[128,1024]{1,0:T(8,128)S(1)}, f32[128,1024]{1,0:T(8,128)S(1)}, u32[]{:S(2)}, u32[]{:S(2)}) collective-permute-start(f32[128,1024]{1,0:T(8,128)S(1)} %copy-done.10), channel_id=1, source_target_pairs={{0,6},{1,7},{2,4},{3,5},{4,2},{5,3},{6,0},{7,1},{8,14},{9,15},{10,... | collective-permute-start | bytes 1572872 | tf_op jit(solution)/shard_map/ppermute | solution.py:196
  162.3 38.7 %collective-permute-start.14 = (f32[128,1024]{1,0:T(8,128)S(1)}, f32[128,1024]{1,0:T(8,128)S(1)}, u32[]{:S(2)}, u32[]{:S(2)}) collective-permute-start(f32[128,1024]{1,0:T(8,128)S(1)} %copy-done.9), channel_id=1, source_target_pairs={{0,13},{1,12},{2,15},{3,14},{4,9},{5,8},{6,11},{7,10},{8,5},{9,4},... | collective-permute-start | bytes 1572872 | tf_op jit(solution)/shard_map/ppermute | solution.py:196
  165.1 37.6 %collective-permute-start.9 = (f32[128,1024]{1,0:T(8,128)S(1)}, f32[128,1024]{1,0:T(8,128)S(1)}, u32[]{:S(2)}, u32[]{:S(2)}) collective-permute-start(f32[128,1024]{1,0:T(8,128)S(1)} %copy-done.7), channel_id=1, source_target_pairs={{0,0},{1,1},{2,2},{3,3},{4,4},{5,5},{6,6},{7,7},{8,8},{9,9},{10,10... | collective-permute-start | bytes 1572872 | tf_op jit(solution)/shard_map/ppermute | solution.py:196

commit v3 on v2

--- a/solution.py
+++ b/solution.py
@@ -9,8 +9,12 @@
 
 eps_value = 1e-06
 clip_value = 3.0
-payload_rows = 4
+mark_width = 128
 window = 4
+head_count = 2
+tell_step = 1
+told_step = 5
+place_steps = (8,)
 in_smem, in_vmem = pl.BlockSpec(memory_space=pltpu.SMEM), pl.BlockSpec(memory_space=pltpu.VMEM)
 in_hbm, in_any = pl.BlockSpec(memory_space=pltpu.HBM), pl.BlockSpec(memory_space=pl.ANY)
 
@@ -29,6 +33,10 @@
     far = list(range(0, half, 2)) + list(range(1, half, 2))
     near = list(range(1, half, 2)) + list(range(2, half, 2)) + [0]
     return [lane for f, n in zip(far, near) for lane in (half + f, n)]
+
+
+def last_cuts(peers):
+    return (peers - 4,)
 
 
 def lane_base(peers):
@@ -91,9 +99,10 @@
     while len(parts) > 1:
         parts = [merge_pair(*parts[i], *parts[i + 1], level_count * 0.5) for i in range(0, len(parts), 2)]
         level_count *= 2
+    moments = jnp.concatenate(list(parts[0]), axis=1)
     for lane in range(peers):
-        mark = jnp.full((payload_rows - 2, feats), slot_ref[inverse_ref[lane]].astype(jnp.float32))
-        payload_ref[lane ^ base] = jnp.concatenate(list(parts[0]) + [mark], axis=0)
+        mark = jnp.full((1, mark_width), slot_ref[inverse_ref[lane]].astype(jnp.float32))
+        payload_ref[lane ^ base] = jnp.concatenate([moments, mark], axis=1)
     for store in stores:
         store.wait()
 
@@ -103,7 +112,7 @@
     rows = row_count // peers
     res = pl.pallas_call(
         functools.partial(rest_kernel, lanes, first),
-        out_shape=[jax.ShapeDtypeStruct((peers, payload_rows, feats), jnp.float32)] + [pltpu.HBM((rows, feats), features.dtype)] * len(lanes),
+        out_shape=[jax.ShapeDtypeStruct((peers, 1, 2 * feats + mark_width), jnp.float32)] + [pltpu.HBM((rows, feats), features.dtype)] * len(lanes),
         in_specs=[in_smem, in_smem, in_hbm],
         out_specs=[in_vmem] + [in_hbm] * len(lanes),
         scratch_shapes=[
@@ -165,11 +174,11 @@
 
 
 def share_moments(told, row_count):
-    peers = told.shape[0]
+    peers, feats = told.shape[0], (told.shape[2] - mark_width) // 2
     outer_count = lax.axis_size("outer")
-    slots = told[:, 2, 0].astype(jnp.int32)[lane_base(peers) ^ jnp.arange(peers, dtype=jnp.int32)]
+    slots = told[:, 0, 2 * feats].astype(jnp.int32)[lane_base(peers) ^ jnp.arange(peers, dtype=jnp.int32)]
     level_count = row_count
-    centers, spreads = told[:, 0], told[:, 1]
+    centers, spreads = told[:, 0, :feats], told[:, 0, feats : 2 * feats]
     while centers.shape[0] > 1:
         centers, spreads = merge_pair(centers[0::2], spreads[0::2], centers[1::2], spreads[1::2], level_count * 0.5)
         level_count *= 2
@@ -187,41 +196,40 @@
     row_count, _ = features.shape
     peers, outer_count = dest.shape[0], lax.axis_size("outer")
     order = lane_order(peers)
-    inverse, first = pick_first(order[:1], dest, features)
-    payload, later = pick_rest(order[1:], order[:1], inverse, slot, features)
+    inverse, first = pick_first(order[:head_count], dest, features)
+    payload, later = pick_rest(order[head_count:], order[:head_count], inverse, slot, features)
     picked, got = list(first) + list(later), []
 
     def send(block, lane):
         pairs = [(o * peers + i, o * peers + (i ^ lane ^ (o & 1) * (peers // 2))) for o in range(outer_count) for i in range(peers)]
         return lax.ppermute(block, ("outer", "inner"), pairs)
 
-    def place_lanes(begin, end, out):
-        return place(order[begin:end], got[begin:end], slots, scale, out, row_count, begin >= peers - window)
+    def place_lanes(begin, end, out, near_by=False):
+        return place(order[begin:end], got[begin:end], slots, scale, out, row_count, near_by)
 
     out, placed = None, 0
     for j in range(peers):
         if j >= window:
             k = j - window
-            values = [picked[j], got[k]]
-            if k == 0:
-                values.append(payload)
-            elif k == window - 1:
-                values.append(told)
-            elif k > window and k % window == 0:
+            extra = []
+            if k == tell_step:
+                extra = [payload]
+            elif k == told_step:
+                extra = [told]
+            elif k in place_steps:
                 out = place_lanes(placed, k, out)
                 placed = k
-                values.append(out)
-            picked[j], got[k], *extra = lax.optimization_barrier(tuple(values))
-            if k == 0:
+                extra = [out]
+            picked[j], got[k], *extra = lax.optimization_barrier((picked[j], got[k], *extra))
+            if k == tell_step:
                 told = lax.all_to_all(extra[0], "inner", split_axis=0, concat_axis=0, tiled=True)
-            elif k == window - 1:
+            elif k == told_step:
                 slots, center, variance, scale = share_moments(extra[0], row_count)
             elif extra:
                 out = extra[0]
         got.append(send(picked[j], order[j]))
-    for end in (peers - window, peers - window // 2, peers):
-        out = place_lanes(placed, end, out)
-        placed = end
+    for begin, end in zip((placed,) + last_cuts(peers), last_cuts(peers) + (peers,)):
+        out = place_lanes(begin, end, out, begin >= peers - 4)
     return (out, jnp.stack([center, variance]))
 
 

time: 205 us -> 195 us (0.951)
  starting transfers between devices: 64.7 us -> 31.6 us
  waiting for transfers between devices: 115 us -> 139 us
    ppermute x16, starting transfers between devices: 54.1 us -> 25.1 us  [send(): return lax.ppermute(block, ('outer', 'inner'), pairs)]
    ppermute x16, waiting for transfers between devices: 115 us -> 139 us  [send(): return lax.ppermute(block, ('outer', 'inner'), pairs)]
    all_to_all x1, starting transfers between devices: 9.99 us -> 6.41 us  [body(): lax.all_to_all(extra[0], 'inner', split_axis=0, concat_axis=0, tiled=True)]
    pallas_call x4 -> x3, Pallas kernels: 11.5 us -> 10.3 us  [place(): pl.pallas_call(functools.partial(place_kernel, lanes, near_by), out_shape...]
  transfers between devices with their start and end apart: 18 -> 18, of which waited for: 6 -> 8; matrix products, arithmetic and copies ran while one was open for 1% -> 1% of each run, Pallas kernels for 8% -> 8%
where the time goes in v3:
time: 195 us; the launch traced here: 194 us
  waiting for transfers between devices  139 us (71%)
  starting transfers between devices  31.6 us (16%)
  Pallas kernels  20.1 us (10%)
    ppermute x16, waiting for transfers between devices, send(): return lax.ppermute(block, ('outer', 'inner'), pairs)  139 us
    ppermute x16, starting transfers between devices, send(): return lax.ppermute(block, ('outer', 'inner'), pairs)  25.1 us
    pallas_call x3, Pallas kernels, place(): pl.pallas_call(functools.partial(place_kernel, lanes, near_by), out_shape...  10.3 us
    pallas_call x1, Pallas kernels, pick_rest(): pl.pallas_call(functools.partial(rest_kernel, lanes, first), out_shape=[j...  7.28 us
    all_to_all x1, starting transfers between devices, body(): lax.all_to_all(extra[0], 'inner', split_axis=0, concat_axis=0, tiled=True)  6.41 us
  transfers between devices with their start and end apart: 18, of which 8 were waited for; matrix products, arithmetic and copies ran while one was open for 1% of the time, Pallas kernels for 8%

profile of v3, /device:TPU:8, one launch (start us, length us, event | category | flops | bytes accessed | tf_op | source)
XLA Modules:
  0.0 194.2 jit_solution(744236055417568160)
XLA Ops:
  0.6 2.6 %pick_first.1 = (s32[16]{0:T(128)}, f32[128,1024]{1,0:T(8,128)S(1)}, f32[128,1024]{1,0:T(8,128)S(1)}) custom-call(s32[16]{0:T(128)} %dest_ref.1, f32[2048,1024]{1,0:T(8,128)} %features_ref.3), custom_call_target="tpu_custom_call" | custom-call | tf_op jit(solution)/shard_map/pick_first/pallas_call | solution.py:64
  3.2 1.6 collective-permute-start
  4.8 4.5 %collective-permute-start.3 = (f32[128,1024]{1,0:T(8,128)S(1)}, f32[128,1024]{1,0:T(8,128)S(1)}, u32[]{:S(2)}, u32[]{:S(2)}) collective-permute-start(f32[128,1024]{1,0:T(8,128)S(1)} %get-tuple-element.58), channel_id=1, source_target_pairs={{0,8},{1,9},{2,10},{3,11},{4,12},{5,13},{6,14},{7,15},{8,0},{9,1},... | collective-permute-start | bytes 1572872 | tf_op jit(solution)/shard_map/ppermute | solution.py:205
  9.3 0.6 copy-done.1
  9.9 7.3 %pick_rest.1 = (f32[16,1,2176]{2,1,0:T(1,128)}, f32[128,1024]{1,0:T(8,128)}, f32[128,1024]{1,0:T(8,128)}, f32[128,1024]{1,0:T(8,128)}, f32[128,1024]{1,0:T(8,128...) custom-call(s32[16]{0:T(128)S(1)} %copy-done.1, ...), custom_call_target="tpu_custom_call" | custom-call | flops 12582912 | bytes 16777216 | tf_op jit(solution)/shard_map/pick_rest/pallas_call | solution.py:113
  17.2 1.4 collective-permute-start.6
  18.6 0.5 collective-permute-start.7
  19.1 1.4 collective-permute-start.1
  20.4 6.4 %all-to-all-start = ((f32[16,1,2176]{2,1,0:T(1,128)}), f32[16,1,2176]{2,1,0:T(1,128)S(1)}, u32[]{:S(2)}, u32[]{:S(2)}) async-start(f32[16,1,2176]{2,1,0:T(1,128)} %get-tuple-element.53), calls=%async_computation | async-start | bytes 278528 | tf_op jit(solution)/shard_map/all_to_all | solution.py:225
  26.9 14.3 %collective-permute-done.3.rest_0_ = f32[128,1024]{1,0:T(8,128)S(1)} collective-permute-done((f32[128,1024]{1,0:T(8,128)S(1)}, f32[128,1024]{1,0:T(8,128)S(1)}, u32[]{:S(2)}, u32[]{:S(2)}) %collective-permute-start.3) | collective-permute-done | bytes 524320 | tf_op jit(solution)/shard_map/ppermute | solution.py:205
  41.2 0.5 collective-permute-start.4
  41.7 22.8 %collective-permute-done.6.rest_2_ = f32[128,1024]{1,0:T(8,128)S(1)} collective-permute-done((f32[128,1024]{1,0:T(8,128)}, f32[128,1024]{1,0:T(8,128)S(1)}, u32[]{:S(2)}, u32[]{:S(2)}) %collective-permute-start.6) | collective-permute-done | bytes 524320 | tf_op jit(solution)/shard_map/ppermute | solution.py:205
  64.5 1.5 collective-permute-start.8
  66.0 5.1 %collective-permute-start.9 = (f32[128,1024]{1,0:T(8,128)}, f32[128,1024]{1,0:T(8,128)}, u32[]{:S(2)}, u32[]{:S(2)}) collective-permute-start(f32[128,1024]{1,0:T(8,128)} %get-tuple-element.75), channel_id=1, source_target_pairs={{0,7},{1,6},{2,5},{3,4},{4,3},{5,2},{6,1},{7,0},{8,15},{9,14},{10,... | collective-permute-start | bytes 1572872 | tf_op jit(solution)/shard_map/ppermute | solution.py:205
  71.5 17.8 %collective-permute-done.4.rest_4_ = f32[128,1024]{1,0:T(8,128)S(1)} collective-permute-done((f32[128,1024]{1,0:T(8,128)}, f32[128,1024]{1,0:T(8,128)S(1)}, u32[]{:S(2)}, u32[]{:S(2)}) %collective-permute-start.4) | collective-permute-done | bytes 524320 | tf_op jit(solution)/shard_map/ppermute | solution.py:205
  89.3 1.5 collective-permute-start.11
  90.8 28.9 %collective-permute-done.8.rest_6_ = f32[128,1024]{1,0:T(8,128)} collective-permute-done((f32[128,1024]{1,0:T(8,128)}, f32[128,1024]{1,0:T(8,128)}, u32[]{:S(2)}, u32[]{:S(2)}) %collective-permute-start.8) | collective-permute-done | bytes 524320 | tf_op jit(solution)/shard_map/ppermute | solution.py:205
  119.8 1.6 collective-permute-start.15
  121.5 0.4 convert_reduce_fusion
  121.9 0.7 gather_fusion
  122.6 0.1 collective-permute-done.2
  122.7 0.6 pad_maximum_fusion
  123.3 5.0 %place.3.rest_4_ = f32[2048,1024]{1,0:T(8,128)} custom-call(s32[16]{0:T(128)S(1)} %gather_fusion, f32[2,1024]{1,0:T(2,128)S(1)} %get-tuple-element.106.scale_ref, f32[128,1024]{1,0:T(8,128)} %copy-done.3, f32[128,1024]{1,0:T(8,128)} %copy-done.2, f32[128,1024]{1,0:T(8,128)} %copy-done.4, f32[128,1024]{1,0:T(8,128)} %copy-done.5, f32[128,1024]{1,0:T(8,128)} %copy-done.6, ...), custom_call_target="tpu_custom_call" | custom-call | flops 4194304 | bytes 8388608 | tf_op jit(solution)/shard_map/place/pallas_call | solution.py:159
  128.4 1.0 collective-permute-start.12
  129.4 21.5 %collective-permute-done.13.rest_2_ = f32[128,1024]{1,0:T(8,128)} collective-permute-done((f32[128,1024]{1,0:T(8,128)}, f32[128,1024]{1,0:T(8,128)}, u32[]{:S(2)}, u32[]{:S(2)}) %collective-permute-start.13) | collective-permute-done | bytes 524320 | tf_op jit(solution)/shard_map/ppermute | solution.py:205
  150.9 2.6 %collective-permute-start.14 = (f32[128,1024]{1,0:T(8,128)S(1)}, f32[128,1024]{1,0:T(8,128)S(1)}, u32[]{:S(2)}, u32[]{:S(2)}) collective-permute-start(f32[128,1024]{1,0:T(8,128)S(1)} %copy-done.9), channel_id=1, source_target_pairs={{0,15},{1,14},{2,13},{3,12},{4,11},{5,10},{6,9},{7,8},{8,7},{9,6},... | collective-permute-start | bytes 1572872 | tf_op jit(solution)/shard_map/ppermute | solution.py:205
  153.5 0.7 collective-permute-start.16
  154.2 1.3 collective-permute-start.10
  155.6 3.1 %place.4.rest_4_ = f32[2048,1024]{1,0:T(8,128)} custom-call(s32[16]{0:T(128)S(1)} %gather_fusion, f32[2,1024]{1,0:T(2,128)S(1)} %get-tuple-element.106.scale_ref, f32[128,1024]{1,0:T(8,128)} %collective-permute-done.5.rest_0_, f32[128,1024]{1,0:T(8,128)} %collective-permute-done.11.rest_1_, ...), custom_call_target="tpu_custom_call", output_to_operand_aliasing={{}: (6, {})} | custom-call | flops 2097152 | bytes 4194304 | tf_op jit(solution)/shard_map/place/pallas_call | solution.py:159
  158.7 25.7 %collective-permute-done.14.rest_2_ = f32[128,1024]{1,0:T(8,128)S(1)} collective-permute-done((f32[128,1024]{1,0:T(8,128)S(1)}, f32[128,1024]{1,0:T(8,128)S(1)}, u32[]{:S(2)}, u32[]{:S(2)}) %collective-permute-start.14) | collective-permute-done | bytes 524320 | tf_op jit(solution)/shard_map/ppermute | solution.py:205
  184.4 7.6 %collective-permute-done.10.rest_0_ = f32[128,1024]{1,0:T(8,128)S(1)} collective-permute-done((f32[128,1024]{1,0:T(8,128)S(1)}, f32[128,1024]{1,0:T(8,128)S(1)}, u32[]{:S(2)}, u32[]{:S(2)}) %collective-permute-start.10) | collective-permute-done | bytes 524320 | tf_op jit(solution)/shard_map/ppermute | solution.py:205
  192.1 2.1 %place.5 = f32[2048,1024]{1,0:T(8,128)} custom-call(s32[16]{0:T(128)S(1)} %gather_fusion, f32[2,1024]{1,0:T(2,128)S(1)} %get-tuple-element.106.scale_ref, f32[128,1024]{1,0:T(8,128)S(1)} %collective-permute-done.10.rest_0_, f32[128,1024]{1,0:T(8,128)S(1)} %collective-permute-done.12.rest_1_, ...), custom_call_target="tpu_custom_call", output_to_operand_aliasing={{}: (6, {})} | custom-call | flops 2097152 | bytes 4194304 | tf_op jit(solution)/shard_map/place/pallas_call | solution.py:159
  (56 shorter events, 0.6 us)
Async XLA Ops:
  0.6 8.6 %copy-start = (s32[16]{0:T(128)S(1)}, s32[16]{0:T(128)}, u32[]{:S(2)}) copy-start(s32[16]{0:T(128)} %slot_ref.1) | copy-start | bytes 196
  3.2 15.8 %collective-permute-start = (f32[128,1024]{1,0:T(8,128)S(1)}, f32[128,1024]{1,0:T(8,128)S(1)}, u32[]{:S(2)}, u32[]{:S(2)}) collective-permute-start(f32[128,1024]{1,0:T(8,128)S(1)} %get-tuple-element.50), channel_id=1, source_target_pairs={{0,1},{1,0},{2,3},{3,2},{4,5},{5,4},{6,7},{7,6},{8,9},{9,8},{10,11... | collective-permute-start | bytes 1572872 | tf_op jit(solution)/shard_map/ppermute | solution.py:205
  4.8 36.4 %collective-permute-start.3 = (f32[128,1024]{1,0:T(8,128)S(1)}, f32[128,1024]{1,0:T(8,128)S(1)}, u32[]{:S(2)}, u32[]{:S(2)}) collective-permute-start(f32[128,1024]{1,0:T(8,128)S(1)} %get-tuple-element.58), channel_id=1, source_target_pairs={{0,8},{1,9},{2,10},{3,11},{4,12},{5,13},{6,14},{7,15},{8,0},{9,1},... | collective-permute-start | bytes 1572872 | tf_op jit(solution)/shard_map/ppermute | solution.py:205
  9.3 0.7 copy-start.1
  17.2 47.3 %collective-permute-start.6 = (f32[128,1024]{1,0:T(8,128)}, f32[128,1024]{1,0:T(8,128)S(1)}, u32[]{:S(2)}, u32[]{:S(2)}) collective-permute-start(f32[128,1024]{1,0:T(8,128)} %get-tuple-element.64), channel_id=1, source_target_pairs={{0,10},{1,11},{2,8},{3,9},{4,14},{5,15},{6,12},{7,13},{8,2},{9,3},... | collective-permute-start | bytes 1572872 | tf_op jit(solution)/shard_map/ppermute | solution.py:205
  18.6 47.4 %collective-permute-start.7 = (f32[128,1024]{1,0:T(8,128)}, f32[128,1024]{1,0:T(8,128)S(1)}, u32[]{:S(2)}, u32[]{:S(2)}) collective-permute-start(f32[128,1024]{1,0:T(8,128)} %get-tuple-element.67), channel_id=1, source_target_pairs={{0,3},{1,2},{2,1},{3,0},{4,7},{5,6},{6,5},{7,4},{8,11},{9,10},{10,... | collective-permute-start | bytes 1572872 | tf_op jit(solution)/shard_map/ppermute | solution.py:205
  19.1 104.3 %copy-start.2 = (f32[128,1024]{1,0:T(8,128)}, f32[128,1024]{1,0:T(8,128)S(1)}, u32[]{:S(2)}) copy-start(f32[128,1024]{1,0:T(8,128)S(1)} %collective-permute-done.rest_1_) | copy-start | bytes 1572868
  19.1 52.1 %collective-permute-start.1 = (f32[128,1024]{1,0:T(8,128)}, f32[128,1024]{1,0:T(8,128)}, u32[]{:S(2)}, u32[]{:S(2)}) collective-permute-start(f32[128,1024]{1,0:T(8,128)} %get-tuple-element.52), channel_id=1, source_target_pairs={{0,5},{1,4},{2,7},{3,6},{4,1},{5,0},{6,3},{7,2},{8,13},{9,12},{10,... | collective-permute-start | bytes 1572872 | tf_op jit(solution)/shard_map/ppermute | solution.py:205
  20.4 50.7 %all-to-all-start = ((f32[16,1,2176]{2,1,0:T(1,128)}), f32[16,1,2176]{2,1,0:T(1,128)S(1)}, u32[]{:S(2)}, u32[]{:S(2)}) async-start(f32[16,1,2176]{2,1,0:T(1,128)} %get-tuple-element.53), calls=%async_computation | async-start | bytes 278528 | tf_op jit(solution)/shard_map/all_to_all | solution.py:225
  41.2 82.1 %copy-start.3 = (f32[128,1024]{1,0:T(8,128)}, f32[128,1024]{1,0:T(8,128)S(1)}, u32[]{:S(2)}) copy-start(f32[128,1024]{1,0:T(8,128)S(1)} %collective-permute-done.3.rest_0_) | copy-start | bytes 1572868
  41.2 48.1 %collective-permute-start.4 = (f32[128,1024]{1,0:T(8,128)}, f32[128,1024]{1,0:T(8,128)S(1)}, u32[]{:S(2)}, u32[]{:S(2)}) collective-permute-start(f32[128,1024]{1,0:T(8,128)} %get-tuple-element.59), channel_id=1, source_target_pairs={{0,12},{1,13},{2,14},{3,15},{4,8},{5,9},{6,10},{7,11},{8,4},{9,5},... | collective-permute-start | bytes 1572872 | tf_op jit(solution)/shard_map/ppermute | solution.py:205
  64.5 58.8 %copy-start.4 = (f32[128,1024]{1,0:T(8,128)}, f32[128,1024]{1,0:T(8,128)S(1)}, u32[]{:S(2)}) copy-start(f32[128,1024]{1,0:T(8,128)S(1)} %collective-permute-done.6.rest_2_) | copy-start | bytes 1572868
  64.5 55.3 %collective-permute-start.8 = (f32[128,1024]{1,0:T(8,128)}, f32[128,1024]{1,0:T(8,128)}, u32[]{:S(2)}, u32[]{:S(2)}) collective-permute-start(f32[128,1024]{1,0:T(8,128)} %get-tuple-element.72), channel_id=1, source_target_pairs={{0,14},{1,15},{2,12},{3,13},{4,10},{5,11},{6,8},{7,9},{8,6},{9,7},... | collective-permute-start | bytes 1572872 | tf_op jit(solution)/shard_map/ppermute | solution.py:205
  66.0 57.4 %copy-start.5 = (f32[128,1024]{1,0:T(8,128)}, f32[128,1024]{1,0:T(8,128)S(1)}, u32[]{:S(2)}) copy-start(f32[128,1024]{1,0:T(8,128)S(1)} %collective-permute-done.7.rest_3_) | copy-start | bytes 1572868
  66.0 53.8 %collective-permute-start.9 = (f32[128,1024]{1,0:T(8,128)}, f32[128,1024]{1,0:T(8,128)}, u32[]{:S(2)}, u32[]{:S(2)}) collective-permute-start(f32[128,1024]{1,0:T(8,128)} %get-tuple-element.75), channel_id=1, source_target_pairs={{0,7},{1,6},{2,5},{3,4},{4,3},{5,2},{6,1},{7,0},{8,15},{9,14},{10,... | collective-permute-start | bytes 1572872 | tf_op jit(solution)/shard_map/ppermute | solution.py:205
  89.3 32.1 %copy-start.6 = (f32[128,1024]{1,0:T(8,128)}, f32[128,1024]{1,0:T(8,128)S(1)}, u32[]{:S(2)}) copy-start(f32[128,1024]{1,0:T(8,128)S(1)} %collective-permute-done.4.rest_4_) | copy-start | bytes 1572868
  89.3 64.9 %collective-permute-start.5 = (f32[128,1024]{1,0:T(8,128)}, f32[128,1024]{1,0:T(8,128)}, u32[]{:S(2)}, u32[]{:S(2)}) collective-permute-start(f32[128,1024]{1,0:T(8,128)} %get-tuple-element.60), channel_id=1, source_target_pairs={{0,9},{1,8},{2,11},{3,10},{4,13},{5,12},{6,15},{7,14},{8,1},{9,0},... | collective-permute-start | bytes 1572872 | tf_op jit(solution)/shard_map/ppermute | solution.py:205
  89.3 39.0 %collective-permute-start.11 = (f32[128,1024]{1,0:T(8,128)}, f32[128,1024]{1,0:T(8,128)}, u32[]{:S(2)}, u32[]{:S(2)}) collective-permute-start(f32[128,1024]{1,0:T(8,128)} %get-tuple-element.79), channel_id=1, source_target_pairs={{0,2},{1,3},{2,0},{3,1},{4,6},{5,7},{6,4},{7,5},{8,10},{9,11},{10,... | collective-permute-start | bytes 1572872 | tf_op jit(solution)/shard_map/ppermute | solution.py:205
  119.8 31.1 %collective-permute-start.13 = (f32[128,1024]{1,0:T(8,128)}, f32[128,1024]{1,0:T(8,128)}, u32[]{:S(2)}, u32[]{:S(2)}) collective-permute-start(f32[128,1024]{1,0:T(8,128)} %get-tuple-element.82), channel_id=1, source_target_pairs={{0,11},{1,10},{2,9},{3,8},{4,15},{5,14},{6,13},{7,12},{8,3},{9,2},... | collective-permute-start | bytes 1572872 | tf_op jit(solution)/shard_map/ppermute | solution.py:205
  119.8 33.7 %collective-permute-start.15 = (f32[128,1024]{1,0:T(8,128)}, f32[128,1024]{1,0:T(8,128)}, u32[]{:S(2)}, u32[]{:S(2)}) collective-permute-start(f32[128,1024]{1,0:T(8,128)} %get-tuple-element.85), channel_id=1, source_target_pairs={{0,4},{1,5},{2,6},{3,7},{4,0},{5,1},{6,2},{7,3},{8,12},{9,13},{10,... | collective-permute-start | bytes 1572872 | tf_op jit(solution)/shard_map/ppermute | solution.py:205
  121.4 1.2 collective-permute-start.2
  121.9 32.3 %copy-start.7 = (f32[128,1024]{1,0:T(8,128)S(1)}, f32[128,1024]{1,0:T(8,128)}, u32[]{:S(2)}) copy-start(f32[128,1024]{1,0:T(8,128)} %get-tuple-element.77) | copy-start | bytes 1572868
  122.6 5.8 %copy-start.10 = (f32[128,1024]{1,0:T(8,128)S(1)}, f32[128,1024]{1,0:T(8,128)}, u32[]{:S(2)}) copy-start(f32[128,1024]{1,0:T(8,128)} %get-tuple-element.80) | copy-start | bytes 1572868
  122.6 28.4 %copy-start.9 = (f32[128,1024]{1,0:T(8,128)S(1)}, f32[128,1024]{1,0:T(8,128)}, u32[]{:S(2)}) copy-start(f32[128,1024]{1,0:T(8,128)} %get-tuple-element.83) | copy-start | bytes 1572868
  122.6 30.9 %copy-start.8 = (f32[128,1024]{1,0:T(8,128)S(1)}, f32[128,1024]{1,0:T(8,128)}, u32[]{:S(2)}) copy-start(f32[128,1024]{1,0:T(8,128)} %get-tuple-element.86) | copy-start | bytes 1572868
  128.4 30.3 %collective-permute-start.12 = (f32[128,1024]{1,0:T(8,128)S(1)}, f32[128,1024]{1,0:T(8,128)S(1)}, u32[]{:S(2)}, u32[]{:S(2)}) collective-permute-start(f32[128,1024]{1,0:T(8,128)S(1)} %copy-done.10), channel_id=1, source_target_pairs={{0,6},{1,7},{2,4},{3,5},{4,2},{5,3},{6,0},{7,1},{8,14},{9,15},{10,... | collective-permute-start | bytes 1572872 | tf_op jit(solution)/shard_map/ppermute | solution.py:205
  150.9 33.5 %collective-permute-start.14 = (f32[128,1024]{1,0:T(8,128)S(1)}, f32[128,1024]{1,0:T(8,128)S(1)}, u32[]{:S(2)}, u32[]{:S(2)}) collective-permute-start(f32[128,1024]{1,0:T(8,128)S(1)} %copy-done.9), channel_id=1, source_target_pairs={{0,15},{1,14},{2,13},{3,12},{4,11},{5,10},{6,9},{7,8},{8,7},{9,6},... | collective-permute-start | bytes 1572872 | tf_op jit(solution)/shard_map/ppermute | solution.py:205
  153.5 30.9 %collective-permute-start.16 = (f32[128,1024]{1,0:T(8,128)S(1)}, f32[128,1024]{1,0:T(8,128)S(1)}, u32[]{:S(2)}, u32[]{:S(2)}) collective-permute-start(f32[128,1024]{1,0:T(8,128)S(1)} %copy-done.8), channel_id=1, source_target_pairs={{0,0},{1,1},{2,2},{3,3},{4,4},{5,5},{6,6},{7,7},{8,8},{9,9},{10,10... | collective-permute-start | bytes 1572872 | tf_op jit(solution)/shard_map/ppermute | solution.py:205
  154.2 37.9 %collective-permute-start.10 = (f32[128,1024]{1,0:T(8,128)S(1)}, f32[128,1024]{1,0:T(8,128)S(1)}, u32[]{:S(2)}, u32[]{:S(2)}) collective-permute-start(f32[128,1024]{1,0:T(8,128)S(1)} %copy-done.7), channel_id=1, source_target_pairs={{0,13},{1,12},{2,15},{3,14},{4,9},{5,8},{6,11},{7,10},{8,5},{9,4},... | collective-permute-start | bytes 1572872 | tf_op jit(solution)/shard_map/ppermute | solution.py:205

commit v4 on v3

--- a/solution.py
+++ b/solution.py
@@ -9,12 +9,14 @@
 
 eps_value = 1e-06
 clip_value = 3.0
-mark_width = 128
+message_width = 256
 window = 4
 head_count = 2
 tell_step = 1
 told_step = 5
-place_steps = (8,)
+share_step = 7
+shared_step = 9
+place_steps = (10,)
 in_smem, in_vmem = pl.BlockSpec(memory_space=pltpu.SMEM), pl.BlockSpec(memory_space=pltpu.VMEM)
 in_hbm, in_any = pl.BlockSpec(memory_space=pltpu.HBM), pl.BlockSpec(memory_space=pl.ANY)
 
@@ -43,17 +45,25 @@
     return lax.axis_index("inner") ^ ((lax.axis_index("outer") & 1) * (peers // 2))
 
 
-def first_kernel(lanes, dest_ref, features_ref, inverse_ref, *rest):
-    outs, sems = rest[:-1], rest[-1]
-    peers, rows = dest_ref.shape[0], outs[0].shape[0]
+def invert(dest_ref, inverse):
+    peers = dest_ref.shape[0]
     base = lane_base(peers)
     for b in range(peers):
-        inverse_ref[dest_ref[b] ^ base] = b
+        inverse[dest_ref[b] ^ base] = b
+    return base
+
+
+def first_kernel(lanes, dest_ref, features_ref, *rest):
+    outs, (inverse, sems) = rest[:-2], rest[-2:]
+    rows, parts = outs[0].shape[0], sems.shape[1]
+    invert(dest_ref, inverse)
     copies = []
     for i, lane in enumerate(lanes):
-        start = pl.multiple_of(inverse_ref[lane] * rows, 8)
-        copies.append(pltpu.make_async_copy(features_ref.at[pl.ds(start, rows)], outs[i], sems.at[i]))
-        copies[-1].start()
+        for p in range(parts):
+            start = pl.multiple_of(inverse[lane] * rows + p * (rows // parts), 8)
+            target = outs[i].at[pl.ds(p * (rows // parts), rows // parts)]
+            copies.append(pltpu.make_async_copy(features_ref.at[pl.ds(start, rows // parts)], target, sems.at[i, p]))
+            copies[-1].start()
     for copy in copies:
         copy.wait()
 
@@ -61,21 +71,20 @@
 def pick_first(lanes, dest, features):
     count, (row_count, feats) = len(lanes), features.shape
     rows = row_count // dest.shape[0]
-    res = pl.pallas_call(
+    return pl.pallas_call(
         functools.partial(first_kernel, lanes),
-        out_shape=[jax.ShapeDtypeStruct(dest.shape, jnp.int32)] + [pltpu.VMEM((rows, feats), features.dtype)] * count,
+        out_shape=[pltpu.VMEM((rows, feats), features.dtype)] * count,
         in_specs=[in_smem, in_hbm],
-        out_specs=[in_smem] + [in_vmem] * count,
-        scratch_shapes=[pltpu.SemaphoreType.DMA((count,))],
+        out_specs=[in_vmem] * count,
+        scratch_shapes=[pltpu.SMEM(dest.shape, jnp.int32), pltpu.SemaphoreType.DMA((count, max(1, rows // 32)))],
         name="pick_first",
     )(dest, pin(features))
-    return res[0], res[1:]
-
-
-def rest_kernel(lanes, first, inverse_ref, slot_ref, features_ref, payload_ref, *rest):
-    outs, (held, in_sems, out_sems) = rest[: len(lanes)], rest[len(lanes) :]
+
+
+def rest_kernel(lanes, first, dest_ref, slot_ref, features_ref, payload_ref, *rest):
+    outs, (held, inverse_ref, in_sems, out_sems) = rest[: len(lanes)], rest[len(lanes) :]
     peers, rows, feats = held.shape
-    base = lane_base(peers)
+    base = invert(dest_ref, inverse_ref)
     order = lanes + first
     fetches = []
     for lane in order:
@@ -99,31 +108,34 @@
     while len(parts) > 1:
         parts = [merge_pair(*parts[i], *parts[i + 1], level_count * 0.5) for i in range(0, len(parts), 2)]
         level_count *= 2
-    moments = jnp.concatenate(list(parts[0]), axis=1)
-    for lane in range(peers):
-        mark = jnp.full((1, mark_width), slot_ref[inverse_ref[lane]].astype(jnp.float32))
-        payload_ref[lane ^ base] = jnp.concatenate([moments, mark], axis=1)
+    center, spread = parts[0]
+    chunk = feats // peers
+    for peer in range(peers):
+        mark = jnp.full((1, payload_ref.shape[2] - 2 * chunk), slot_ref[inverse_ref[peer ^ base]].astype(jnp.float32))
+        pieces = [x[:, peer * chunk : (peer + 1) * chunk] for x in (center, spread)]
+        payload_ref[peer] = jnp.concatenate(pieces + [mark], axis=1)
     for store in stores:
         store.wait()
 
 
-def pick_rest(lanes, first, inverse, slot, features):
-    peers, (row_count, feats) = inverse.shape[0], features.shape
+def pick_rest(lanes, first, dest, slot, features):
+    peers, (row_count, feats) = dest.shape[0], features.shape
     rows = row_count // peers
     res = pl.pallas_call(
         functools.partial(rest_kernel, lanes, first),
-        out_shape=[jax.ShapeDtypeStruct((peers, 1, 2 * feats + mark_width), jnp.float32)] + [pltpu.HBM((rows, feats), features.dtype)] * len(lanes),
+        out_shape=[jax.ShapeDtypeStruct((peers, 1, message_width), jnp.float32)] + [pltpu.HBM((rows, feats), features.dtype)] * len(lanes),
         in_specs=[in_smem, in_smem, in_hbm],
         out_specs=[in_vmem] + [in_hbm] * len(lanes),
         scratch_shapes=[
             pltpu.VMEM((peers, rows, feats), jnp.float32),
+            pltpu.SMEM((peers,), jnp.int32),
             pltpu.SemaphoreType.DMA((peers,)),
             pltpu.SemaphoreType.DMA((len(lanes),)),
         ],
         compiler_params=pltpu.CompilerParams(vmem_limit_bytes=32 * 1024 * 1024),
         cost_estimate=pl.CostEstimate(flops=6 * features.size, bytes_accessed=8 * features.size, transcendentals=0),
         name="pick_rest",
-    )(inverse, slot, pin(features))
+    )(dest, slot, pin(features))
     return res[0], res[1:]
 
 
@@ -173,12 +185,12 @@
     )(*args)
 
 
-def share_moments(told, row_count):
-    peers, feats = told.shape[0], (told.shape[2] - mark_width) // 2
-    outer_count = lax.axis_size("outer")
-    slots = told[:, 0, 2 * feats].astype(jnp.int32)[lane_base(peers) ^ jnp.arange(peers, dtype=jnp.int32)]
+def merge_chunk(told, row_count, feats):
+    peers, outer_count = told.shape[0], lax.axis_size("outer")
+    chunk = feats // peers
+    slots = told[:, 0, 2 * chunk].astype(jnp.int32)[lane_base(peers) ^ jnp.arange(peers, dtype=jnp.int32)]
     level_count = row_count
-    centers, spreads = told[:, 0, :feats], told[:, 0, feats : 2 * feats]
+    centers, spreads = told[:, 0, :chunk], told[:, 0, chunk : 2 * chunk]
     while centers.shape[0] > 1:
         centers, spreads = merge_pair(centers[0::2], spreads[0::2], centers[1::2], spreads[1::2], level_count * 0.5)
         level_count *= 2
@@ -188,16 +200,22 @@
         center, spread = merge_pair(pair[0], pair[1], other[0], other[1], level_count * 0.5)
         level_count *= 2
         pair = jnp.stack([center, spread])
-    center, variance = pair[0], pair[1] / level_count
-    return slots, center, variance, jnp.stack([center, lax.rsqrt(variance + eps_value)])
+    return slots, jnp.broadcast_to(pair.reshape(1, 1, 2 * chunk), (peers, 1, 2 * chunk))
+
+
+def spread_moments(shares, total_rows):
+    chunk = shares.shape[2] // 2
+    center, variance = shares[:, 0, :chunk].reshape(-1), shares[:, 0, chunk:].reshape(-1) / total_rows
+    return center, variance, jnp.stack([center, lax.rsqrt(variance + eps_value)])
 
 
 def body(features, dest, slot):
-    row_count, _ = features.shape
+    row_count, feats = features.shape
     peers, outer_count = dest.shape[0], lax.axis_size("outer")
     order = lane_order(peers)
-    inverse, first = pick_first(order[:head_count], dest, features)
-    payload, later = pick_rest(order[head_count:], order[:head_count], inverse, slot, features)
+    first = pick_first(order[:head_count], dest, features)
+    dest, slot, *first = lax.optimization_barrier((dest, slot, *first))
+    payload, later = pick_rest(order[head_count:], order[:head_count], dest, slot, features)
     picked, got = list(first) + list(later), []
 
     def send(block, lane):
@@ -216,6 +234,10 @@
                 extra = [payload]
             elif k == told_step:
                 extra = [told]
+            elif k == share_step:
+                extra = [share]
+            elif k == shared_step:
+                extra = [shared]
             elif k in place_steps:
                 out = place_lanes(placed, k, out)
                 placed = k
@@ -224,7 +246,11 @@
             if k == tell_step:
                 told = lax.all_to_all(extra[0], "inner", split_axis=0, concat_axis=0, tiled=True)
             elif k == told_step:
-                slots, center, variance, scale = share_moments(extra[0], row_count)
+                slots, share = merge_chunk(extra[0], row_count, feats)
+            elif k == share_step:
+                shared = lax.all_to_all(extra[0], "inner", split_axis=0, concat_axis=0, tiled=True)
+            elif k == shared_step:
+                center, variance, scale = spread_moments(extra[0], row_count * peers * outer_count)
             elif extra:
                 out = extra[0]
         got.append(send(picked[j], order[j]))

time: 195 us -> 191 us (0.979)
  waiting for transfers between devices: 139 us -> 128 us
  starting transfers between devices: 31.6 us -> 38.3 us
    ppermute x16, waiting for transfers between devices: 139 us -> 102 us  [send(): return lax.ppermute(block, ('outer', 'inner'), pairs)]
    all_to_all x1 -> x2, waiting for transfers between devices: 0.01 us -> 26.1 us  [body(): lax.all_to_all(extra[0], 'inner', split_axis=0, concat_axis=0, tiled=True)]
    all_to_all x1 -> x2, starting transfers between devices: 6.41 us -> 15.6 us  [body(): lax.all_to_all(extra[0], 'inner', split_axis=0, concat_axis=0, tiled=True)]
    ppermute x16, starting transfers between devices: 25.1 us -> 22.7 us  [send(): return lax.ppermute(block, ('outer', 'inner'), pairs)]
  transfers between devices with their start and end apart: 18 -> 19, of which waited for: 8 -> 9; matrix products, arithmetic and copies ran while one was open for 1% -> 2% of each run, Pallas kernels for 8% -> 8%
where the time goes in v4:
time: 191 us; the launch traced here: 190 us
  waiting for transfers between devices  128 us (67%)
  starting transfers between devices  38.3 us (20%)
  Pallas kernels  20.1 us (11%)
    ppermute x16, waiting for transfers between devices, send(): return lax.ppermute(block, ('outer', 'inner'), pairs)  102 us
    all_to_all x2, waiting for transfers between devices, body(): lax.all_to_all(extra[0], 'inner', split_axis=0, concat_axis=0, tiled=True)  26.1 us
    ppermute x16, starting transfers between devices, send(): return lax.ppermute(block, ('outer', 'inner'), pairs)  22.7 us
    all_to_all x2, starting transfers between devices, body(): lax.all_to_all(extra[0], 'inner', split_axis=0, concat_axis=0, tiled=True)  15.6 us
    pallas_call x3, Pallas kernels, place(): pl.pallas_call(functools.partial(place_kernel, lanes, near_by), out_shape...  10.6 us
    pallas_call x1, Pallas kernels, pick_rest(): pl.pallas_call(functools.partial(rest_kernel, lanes, first), out_shape=[j...  7.29 us
  transfers between devices with their start and end apart: 19, of which 9 were waited for; matrix products, arithmetic and copies ran while one was open for 2% of the time, Pallas kernels for 8%

profile of v4, /device:TPU:8, one launch (start us, length us, event | category | flops | bytes accessed | tf_op | source)
XLA Modules:
  0.0 189.9 jit_solution(5464273203141815046)
XLA Ops:
  0.6 2.2 %pick_first.1 = (f32[128,1024]{1,0:T(8,128)S(1)}, f32[128,1024]{1,0:T(8,128)S(1)}) custom-call(s32[16]{0:T(128)} %dest_ref.2, f32[2048,1024]{1,0:T(8,128)} %features_ref.3), custom_call_target="tpu_custom_call" | custom-call | tf_op jit(solution)/shard_map/pick_first/pallas_call | solution.py:74
  2.8 1.6 collective-permute-start
  4.4 4.5 %collective-permute-start.6 = (f32[128,1024]{1,0:T(8,128)S(1)}, f32[128,1024]{1,0:T(8,128)S(1)}, u32[]{:S(2)}, u32[]{:S(2)}) collective-permute-start(f32[128,1024]{1,0:T(8,128)S(1)} %get-tuple-element.74), channel_id=1, source_target_pairs={{0,8},{1,9},{2,10},{3,11},{4,12},{5,13},{6,14},{7,15},{8,0},{9,1},... | collective-permute-start | bytes 1572872 | tf_op jit(solution)/shard_map/ppermute | solution.py:223
  8.9 7.3 %pick_rest.1 = (f32[16,1,256]{2,1,0:T(1,128)}, f32[128,1024]{1,0:T(8,128)}, f32[128,1024]{1,0:T(8,128)}, f32[128,1024]{1,0:T(8,128)}, f32[128,1024]{1,0:T(8,128)...) custom-call(s32[16]{0:T(128)S(1)} %copy-done, ...), custom_call_target="tpu_custom_call" | custom-call | flops 12582912 | bytes 16777216 | tf_op jit(solution)/shard_map/pick_rest/pallas_call | solution.py:124
  16.2 1.6 collective-permute-start.3
  17.8 0.3 collective-permute-start.11
  18.0 1.4 collective-permute-start.1
  19.4 8.1 %all-to-all-start = ((f32[16,1,256]{2,1,0:T(1,128)}), f32[16,1,256]{2,1,0:T(1,128)S(1)}, u32[]{:S(2)}, u32[]{:S(2)}) async-start(f32[16,1,256]{2,1,0:T(1,128)} %get-tuple-element.61), calls=%async_computation | async-start | bytes 32768 | tf_op jit(solution)/shard_map/all_to_all | solution.py:247
  27.5 12.6 %collective-permute-done.6.rest_0_ = f32[128,1024]{1,0:T(8,128)S(1)} collective-permute-done((f32[128,1024]{1,0:T(8,128)S(1)}, f32[128,1024]{1,0:T(8,128)S(1)}, u32[]{:S(2)}, u32[]{:S(2)}) %collective-permute-start.6) | collective-permute-done | bytes 524320 | tf_op jit(solution)/shard_map/ppermute | solution.py:223
  40.1 0.5 collective-permute-start.7
  40.7 5.3 %collective-permute-start.4 = (f32[128,1024]{1,0:T(8,128)}, f32[128,1024]{1,0:T(8,128)}, u32[]{:S(2)}, u32[]{:S(2)}) collective-permute-start(f32[128,1024]{1,0:T(8,128)} %get-tuple-element.68), channel_id=1, source_target_pairs={{0,7},{1,6},{2,5},{3,4},{4,3},{5,2},{6,1},{7,0},{8,15},{9,14},{10,... | collective-permute-start | bytes 1572872 | tf_op jit(solution)/shard_map/ppermute | solution.py:223
  45.9 16.9 %collective-permute-done.11.rest_2_ = f32[128,1024]{1,0:T(8,128)S(1)} collective-permute-done((f32[128,1024]{1,0:T(8,128)}, f32[128,1024]{1,0:T(8,128)S(1)}, u32[]{:S(2)}, u32[]{:S(2)}) %collective-permute-start.11) | collective-permute-done | bytes 524320 | tf_op jit(solution)/shard_map/ppermute | solution.py:223
  62.8 1.5 collective-permute-start.12
  64.3 0.5 all-to-all-done
  65.1 21.2 %collective-permute-done.7.rest_4_ = f32[128,1024]{1,0:T(8,128)S(1)} collective-permute-done((f32[128,1024]{1,0:T(8,128)}, f32[128,1024]{1,0:T(8,128)S(1)}, u32[]{:S(2)}, u32[]{:S(2)}) %collective-permute-start.7) | collective-permute-done | bytes 524320 | tf_op jit(solution)/shard_map/ppermute | solution.py:223
  86.4 1.6 collective-permute-start.2
  88.0 23.4 %collective-permute-done.12.rest_6_ = f32[128,1024]{1,0:T(8,128)} collective-permute-done((f32[128,1024]{1,0:T(8,128)}, f32[128,1024]{1,0:T(8,128)}, u32[]{:S(2)}, u32[]{:S(2)}) %collective-permute-start.12) | collective-permute-done | bytes 524320 | tf_op jit(solution)/shard_map/ppermute | solution.py:223
  111.5 0.6 broadcast_in_dim.9
  112.1 7.5 %all-to-all-start.1 = ((f32[16,1,128]{2,1,0:T(1,128)}), f32[16,1,128]{2,1,0:T(1,128)S(1)}, u32[]{:S(2)}, u32[]{:S(2)}) async-start(f32[16,1,128]{2,1,0:T(1,128)} %broadcast_in_dim.9), calls=%async_computation.1 | async-start | bytes 16384 | tf_op jit(solution)/shard_map/all_to_all | solution.py:251
  119.8 0.4 convert_reduce_fusion
  120.2 0.7 gather_fusion
  120.8 9.7 %collective-permute-done.8.rest_8_ = f32[128,1024]{1,0:T(8,128)} collective-permute-done((f32[128,1024]{1,0:T(8,128)}, f32[128,1024]{1,0:T(8,128)}, u32[]{:S(2)}, u32[]{:S(2)}) %collective-permute-start.8) | collective-permute-done | bytes 524320 | tf_op jit(solution)/shard_map/ppermute | solution.py:223
  130.7 25.6 %all-to-all-done.1 = f32[16,1,128]{2,1,0:T(1,128)S(1)} async-done(((f32[16,1,128]{2,1,0:T(1,128)}), f32[16,1,128]{2,1,0:T(1,128)S(1)}, u32[]{:S(2)}, u32[]{:S(2)}) %all-to-all-start.1) | async-done | bytes 8224 | tf_op jit(solution)/shard_map/all_to_all | solution.py:251
  156.6 0.7 collective-permute-start.10
  157.3 0.6 pad_maximum_fusion
  158.0 5.8 %place.3.rest_2_ = f32[2048,1024]{1,0:T(8,128)} custom-call(s32[16]{0:T(128)S(1)} %gather_fusion, f32[2,1024]{1,0:T(2,128)S(1)} %get-tuple-element.107.scale_ref, f32[128,1024]{1,0:T(8,128)} %copy-done.3, f32[128,1024]{1,0:T(8,128)} %copy-done.2, f32[128,1024]{1,0:T(8,128)} %copy-done.5, f32[128,1024]{1,0:T(8,128)} %copy-done.4, f32[128,1024]{1,0:T(8,128)} %copy-done.7, ...), custom_call_target="tpu_custom_call" | custom-call | flops 5242880 | bytes 10485760 | tf_op jit(solution)/shard_map/place/pallas_call | solution.py:171
  163.8 2.8 %collective-permute-start.14 = (f32[128,1024]{1,0:T(8,128)S(1)}, f32[128,1024]{1,0:T(8,128)S(1)}, u32[]{:S(2)}, u32[]{:S(2)}) collective-permute-start(f32[128,1024]{1,0:T(8,128)S(1)} %copy-done.9), channel_id=1, source_target_pairs={{0,15},{1,14},{2,13},{3,12},{4,11},{5,10},{6,9},{7,8},{8,7},{9,6},... | collective-permute-start | bytes 1572872 | tf_op jit(solution)/shard_map/ppermute | solution.py:223
  166.7 0.7 collective-permute-start.16
  167.4 2.6 %place.4.rest_4_ = f32[2048,1024]{1,0:T(8,128)} custom-call(s32[16]{0:T(128)S(1)} %gather_fusion, f32[2,1024]{1,0:T(2,128)S(1)} %get-tuple-element.107.scale_ref, f32[128,1024]{1,0:T(8,128)} %collective-permute-done.13.rest_0_, f32[128,1024]{1,0:T(8,128)} %collective-permute-done.15.rest_1_, f32[2048,1024]{1,0:T(8,128)} %place.3.rest_2_), custom_call_target="tpu_custom_call", output_to_operand_aliasing={{}: (4, {})} | custom-call | flops 1048576 | bytes 2097152 | tf_op jit(solution)/shard_map/place/pallas_call | solution.py:171
  170.0 6.6 %collective-permute-done.9.rest_0_ = f32[128,1024]{1,0:T(8,128)S(1)} collective-permute-done((f32[128,1024]{1,0:T(8,128)}, f32[128,1024]{1,0:T(8,128)S(1)}, u32[]{:S(2)}, u32[]{:S(2)}) %collective-permute-start.9) | collective-permute-done | bytes 524320 | tf_op jit(solution)/shard_map/ppermute | solution.py:223
  176.7 11.1 %collective-permute-done.14.rest_2_ = f32[128,1024]{1,0:T(8,128)S(1)} collective-permute-done((f32[128,1024]{1,0:T(8,128)S(1)}, f32[128,1024]{1,0:T(8,128)S(1)}, u32[]{:S(2)}, u32[]{:S(2)}) %collective-permute-start.14) | collective-permute-done | bytes 524320 | tf_op jit(solution)/shard_map/ppermute | solution.py:223
  187.7 2.1 %place.5 = f32[2048,1024]{1,0:T(8,128)} custom-call(s32[16]{0:T(128)S(1)} %gather_fusion, f32[2,1024]{1,0:T(2,128)S(1)} %get-tuple-element.107.scale_ref, f32[128,1024]{1,0:T(8,128)S(1)} %collective-permute-done.9.rest_0_, f32[128,1024]{1,0:T(8,128)S(1)} %collective-permute-done.10.rest_1_, ...), custom_call_target="tpu_custom_call", output_to_operand_aliasing={{}: (6, {})} | custom-call | flops 2097152 | bytes 4194304 | tf_op jit(solution)/shard_map/place/pallas_call | solution.py:171
  (64 shorter events, 1.2 us)
Async XLA Ops:
  0.6 8.3 %copy-start = (s32[16]{0:T(128)S(1)}, s32[16]{0:T(128)}, u32[]{:S(2)}) copy-start(s32[16]{0:T(128)} %dest_ref.2) | copy-start | bytes 196
  0.6 8.3 %copy-start.1 = (s32[16]{0:T(128)S(1)}, s32[16]{0:T(128)}, u32[]{:S(2)}) copy-start(s32[16]{0:T(128)} %slot_ref) | copy-start | bytes 196
  2.8 15.2 %collective-permute-start = (f32[128,1024]{1,0:T(8,128)S(1)}, f32[128,1024]{1,0:T(8,128)S(1)}, u32[]{:S(2)}, u32[]{:S(2)}) collective-permute-start(f32[128,1024]{1,0:T(8,128)S(1)} %get-tuple-element.58), channel_id=1, source_target_pairs={{0,1},{1,0},{2,3},{3,2},{4,5},{5,4},{6,7},{7,6},{8,9},{9,8},{10,11... | collective-permute-start | bytes 1572872 | tf_op jit(solution)/shard_map/ppermute | solution.py:223
  4.4 35.7 %collective-permute-start.6 = (f32[128,1024]{1,0:T(8,128)S(1)}, f32[128,1024]{1,0:T(8,128)S(1)}, u32[]{:S(2)}, u32[]{:S(2)}) collective-permute-start(f32[128,1024]{1,0:T(8,128)S(1)} %get-tuple-element.74), channel_id=1, source_target_pairs={{0,8},{1,9},{2,10},{3,11},{4,12},{5,13},{6,14},{7,15},{8,0},{9,1},... | collective-permute-start | bytes 1572872 | tf_op jit(solution)/shard_map/ppermute | solution.py:223
  16.2 24.5 %collective-permute-start.3 = (f32[128,1024]{1,0:T(8,128)}, f32[128,1024]{1,0:T(8,128)S(1)}, u32[]{:S(2)}, u32[]{:S(2)}) collective-permute-start(f32[128,1024]{1,0:T(8,128)} %get-tuple-element.67), channel_id=1, source_target_pairs={{0,3},{1,2},{2,1},{3,0},{4,7},{5,6},{6,5},{7,4},{8,11},{9,10},{10,... | collective-permute-start | bytes 1572872 | tf_op jit(solution)/shard_map/ppermute | solution.py:223
  17.8 45.0 %collective-permute-start.11 = (f32[128,1024]{1,0:T(8,128)}, f32[128,1024]{1,0:T(8,128)S(1)}, u32[]{:S(2)}, u32[]{:S(2)}) collective-permute-start(f32[128,1024]{1,0:T(8,128)} %get-tuple-element.82), channel_id=1, source_target_pairs={{0,10},{1,11},{2,8},{3,9},{4,14},{5,15},{6,12},{7,13},{8,2},{9,3},... | collective-permute-start | bytes 1572872 | tf_op jit(solution)/shard_map/ppermute | solution.py:223
  18.0 139.9 %copy-start.2 = (f32[128,1024]{1,0:T(8,128)}, f32[128,1024]{1,0:T(8,128)S(1)}, u32[]{:S(2)}) copy-start(f32[128,1024]{1,0:T(8,128)S(1)} %collective-permute-done.rest_1_) | copy-start | bytes 1572868
  18.0 46.7 %collective-permute-start.1 = (f32[128,1024]{1,0:T(8,128)}, f32[128,1024]{1,0:T(8,128)S(1)}, u32[]{:S(2)}, u32[]{:S(2)}) collective-permute-start(f32[128,1024]{1,0:T(8,128)} %get-tuple-element.60), channel_id=1, source_target_pairs={{0,5},{1,4},{2,7},{3,6},{4,1},{5,0},{6,3},{7,2},{8,13},{9,12},{10,... | collective-permute-start | bytes 1572872 | tf_op jit(solution)/shard_map/ppermute | solution.py:223
  19.4 45.3 %all-to-all-start = ((f32[16,1,256]{2,1,0:T(1,128)}), f32[16,1,256]{2,1,0:T(1,128)S(1)}, u32[]{:S(2)}, u32[]{:S(2)}) async-start(f32[16,1,256]{2,1,0:T(1,128)} %get-tuple-element.61), calls=%async_computation | async-start | bytes 32768 | tf_op jit(solution)/shard_map/all_to_all | solution.py:247
  40.1 117.8 %copy-start.3 = (f32[128,1024]{1,0:T(8,128)}, f32[128,1024]{1,0:T(8,128)S(1)}, u32[]{:S(2)}) copy-start(f32[128,1024]{1,0:T(8,128)S(1)} %collective-permute-done.6.rest_0_) | copy-start | bytes 1572868
  40.1 46.2 %collective-permute-start.7 = (f32[128,1024]{1,0:T(8,128)}, f32[128,1024]{1,0:T(8,128)S(1)}, u32[]{:S(2)}, u32[]{:S(2)}) collective-permute-start(f32[128,1024]{1,0:T(8,128)} %get-tuple-element.75), channel_id=1, source_target_pairs={{0,12},{1,13},{2,14},{3,15},{4,8},{5,9},{6,10},{7,11},{8,4},{9,5},... | collective-permute-start | bytes 1572872 | tf_op jit(solution)/shard_map/ppermute | solution.py:223
  40.7 117.3 %copy-start.4 = (f32[128,1024]{1,0:T(8,128)}, f32[128,1024]{1,0:T(8,128)S(1)}, u32[]{:S(2)}) copy-start(f32[128,1024]{1,0:T(8,128)S(1)} %collective-permute-done.3.rest_3_) | copy-start | bytes 1572868
  40.7 70.9 %collective-permute-start.4 = (f32[128,1024]{1,0:T(8,128)}, f32[128,1024]{1,0:T(8,128)}, u32[]{:S(2)}, u32[]{:S(2)}) collective-permute-start(f32[128,1024]{1,0:T(8,128)} %get-tuple-element.68), channel_id=1, source_target_pairs={{0,7},{1,6},{2,5},{3,4},{4,3},{5,2},{6,1},{7,0},{8,15},{9,14},{10,... | collective-permute-start | bytes 1572872 | tf_op jit(solution)/shard_map/ppermute | solution.py:223
  62.8 95.2 %copy-start.5 = (f32[128,1024]{1,0:T(8,128)}, f32[128,1024]{1,0:T(8,128)S(1)}, u32[]{:S(2)}) copy-start(f32[128,1024]{1,0:T(8,128)S(1)} %collective-permute-done.11.rest_2_) | copy-start | bytes 1572868
  62.8 48.6 %collective-permute-start.12 = (f32[128,1024]{1,0:T(8,128)}, f32[128,1024]{1,0:T(8,128)}, u32[]{:S(2)}, u32[]{:S(2)}) collective-permute-start(f32[128,1024]{1,0:T(8,128)} %get-tuple-element.83), channel_id=1, source_target_pairs={{0,14},{1,15},{2,12},{3,13},{4,10},{5,11},{6,8},{7,9},{8,6},{9,7},... | collective-permute-start | bytes 1572872 | tf_op jit(solution)/shard_map/ppermute | solution.py:223
  64.8 93.2 %copy-start.6 = (f32[128,1024]{1,0:T(8,128)}, f32[128,1024]{1,0:T(8,128)S(1)}, u32[]{:S(2)}) copy-start(f32[128,1024]{1,0:T(8,128)S(1)} %collective-permute-done.1.rest_5_) | copy-start | bytes 1572868
  86.3 33.3 %copy-start.7 = (f32[128,1024]{1,0:T(8,128)}, f32[128,1024]{1,0:T(8,128)S(1)}, u32[]{:S(2)}) copy-start(f32[128,1024]{1,0:T(8,128)S(1)} %collective-permute-done.7.rest_4_) | copy-start | bytes 1572868
  86.3 44.2 %collective-permute-start.8 = (f32[128,1024]{1,0:T(8,128)}, f32[128,1024]{1,0:T(8,128)}, u32[]{:S(2)}, u32[]{:S(2)}) collective-permute-start(f32[128,1024]{1,0:T(8,128)} %get-tuple-element.76), channel_id=1, source_target_pairs={{0,9},{1,8},{2,11},{3,10},{4,13},{5,12},{6,15},{7,14},{8,1},{9,0},... | collective-permute-start | bytes 1572872 | tf_op jit(solution)/shard_map/ppermute | solution.py:223
  86.4 25.1 %collective-permute-start.5 = (f32[2,64]{1,0:T(2,128)S(1)}, f32[2,64]{1,0:T(2,128)S(1)}, u32[]{:S(2)}, u32[]{:S(2)}) collective-permute-start(f32[2,64]{1,0:T(2,128)S(1)} %pad_maximum_fusion.2), channel_id=1, source_target_pairs={{0,16},{16,0},{1,17},{17,1},{2,18},{18,2},{3,19},{19,3},{4,20},{20... | collective-permute-start | bytes 1544 | tf_op jit(solution)/shard_map/ppermute | solution.py:199
  86.4 69.9 %collective-permute-start.2 = (f32[128,1024]{1,0:T(8,128)}, f32[128,1024]{1,0:T(8,128)}, u32[]{:S(2)}, u32[]{:S(2)}) collective-permute-start(f32[128,1024]{1,0:T(8,128)} %get-tuple-element.64), channel_id=1, source_target_pairs={{0,2},{1,3},{2,0},{3,1},{4,6},{5,7},{6,4},{7,5},{8,10},{9,11},{10,... | collective-permute-start | bytes 1572872 | tf_op jit(solution)/shard_map/ppermute | solution.py:223
  111.4 52.4 %collective-permute-start.13 = (f32[128,1024]{1,0:T(8,128)}, f32[128,1024]{1,0:T(8,128)}, u32[]{:S(2)}, u32[]{:S(2)}) collective-permute-start(f32[128,1024]{1,0:T(8,128)} %get-tuple-element.84), channel_id=1, source_target_pairs={{0,11},{1,10},{2,9},{3,8},{4,15},{5,14},{6,13},{7,12},{8,3},{9,2},... | collective-permute-start | bytes 1572872 | tf_op jit(solution)/shard_map/ppermute | solution.py:223
  112.1 44.2 %all-to-all-start.1 = ((f32[16,1,128]{2,1,0:T(1,128)}), f32[16,1,128]{2,1,0:T(1,128)S(1)}, u32[]{:S(2)}, u32[]{:S(2)}) async-start(f32[16,1,128]{2,1,0:T(1,128)} %broadcast_in_dim.9), calls=%async_computation.1 | async-start | bytes 16384 | tf_op jit(solution)/shard_map/all_to_all | solution.py:251
  119.6 47.1 %collective-permute-start.15 = (f32[128,1024]{1,0:T(8,128)}, f32[128,1024]{1,0:T(8,128)}, u32[]{:S(2)}, u32[]{:S(2)}) collective-permute-start(f32[128,1024]{1,0:T(8,128)} %get-tuple-element.97), channel_id=1, source_target_pairs={{0,4},{1,5},{2,6},{3,7},{4,0},{5,1},{6,2},{7,3},{8,12},{9,13},{10,... | collective-permute-start | bytes 1572872 | tf_op jit(solution)/shard_map/ppermute | solution.py:223
  130.5 46.1 %collective-permute-start.9 = (f32[128,1024]{1,0:T(8,128)}, f32[128,1024]{1,0:T(8,128)S(1)}, u32[]{:S(2)}, u32[]{:S(2)}) collective-permute-start(f32[128,1024]{1,0:T(8,128)} %get-tuple-element.77), channel_id=1, source_target_pairs={{0,13},{1,12},{2,15},{3,14},{4,9},{5,8},{6,11},{7,10},{8,5},{9,4},... | collective-permute-start | bytes 1572872 | tf_op jit(solution)/shard_map/ppermute | solution.py:223
  156.6 7.2 %copy-start.9 = (f32[128,1024]{1,0:T(8,128)S(1)}, f32[128,1024]{1,0:T(8,128)}, u32[]{:S(2)}) copy-start(f32[128,1024]{1,0:T(8,128)} %get-tuple-element.95) | copy-start | bytes 1572868
  156.6 10.1 %copy-start.8 = (f32[128,1024]{1,0:T(8,128)S(1)}, f32[128,1024]{1,0:T(8,128)}, u32[]{:S(2)}) copy-start(f32[128,1024]{1,0:T(8,128)} %get-tuple-element.98) | copy-start | bytes 1572868
  156.6 20.1 %collective-permute-start.10 = (f32[128,1024]{1,0:T(8,128)}, f32[128,1024]{1,0:T(8,128)S(1)}, u32[]{:S(2)}, u32[]{:S(2)}) collective-permute-start(f32[128,1024]{1,0:T(8,128)} %get-tuple-element.78), channel_id=1, source_target_pairs={{0,6},{1,7},{2,4},{3,5},{4,2},{5,3},{6,0},{7,1},{8,14},{9,15},{10,... | collective-permute-start | bytes 1572872 | tf_op jit(solution)/shard_map/ppermute | solution.py:223
  163.8 23.9 %collective-permute-start.14 = (f32[128,1024]{1,0:T(8,128)S(1)}, f32[128,1024]{1,0:T(8,128)S(1)}, u32[]{:S(2)}, u32[]{:S(2)}) collective-permute-start(f32[128,1024]{1,0:T(8,128)S(1)} %copy-done.9), channel_id=1, source_target_pairs={{0,15},{1,14},{2,13},{3,12},{4,11},{5,10},{6,9},{7,8},{8,7},{9,6},... | collective-permute-start | bytes 1572872 | tf_op jit(solution)/shard_map/ppermute | solution.py:223
  166.7 21.1 %collective-permute-start.16 = (f32[128,1024]{1,0:T(8,128)S(1)}, f32[128,1024]{1,0:T(8,128)S(1)}, u32[]{:S(2)}, u32[]{:S(2)}) collective-permute-start(f32[128,1024]{1,0:T(8,128)S(1)} %copy-done.8), channel_id=1, source_target_pairs={{0,0},{1,1},{2,2},{3,3},{4,4},{5,5},{6,6},{7,7},{8,8},{9,9},{10,10... | collective-permute-start | bytes 1572872 | tf_op jit(solution)/shard_map/ppermute | solution.py:223

commit v5 on v4

--- a/solution.py
+++ b/solution.py
@@ -38,7 +38,7 @@
 
 
 def last_cuts(peers):
-    return (peers - 4,)
+    return (peers - 4, peers - 2)
 
 
 def lane_base(peers):
@@ -76,7 +76,7 @@
         out_shape=[pltpu.VMEM((rows, feats), features.dtype)] * count,
         in_specs=[in_smem, in_hbm],
         out_specs=[in_vmem] * count,
-        scratch_shapes=[pltpu.SMEM(dest.shape, jnp.int32), pltpu.SemaphoreType.DMA((count, max(1, rows // 32)))],
+        scratch_shapes=[pltpu.SMEM(dest.shape, jnp.int32), pltpu.SemaphoreType.DMA((count, 1))],
         name="pick_first",
     )(dest, pin(features))
 
@@ -144,7 +144,7 @@
     _, parts, part_rows, _ = held.shape
     plan = []
     for n, lane in enumerate(lanes):
-        start = slot_ref[lane] * (parts * part_rows)
+        start = jnp.max(slot_ref[lane : lane + 1, :]) * (parts * part_rows)
         for i in range(parts):
             target = pl.ds(pl.multiple_of(start + i * part_rows, 8), part_rows)
             source = blocks[n].at[pl.ds(i * part_rows, part_rows)]
@@ -167,11 +167,11 @@
     rows, feats = blocks[0].shape
     count, parts = len(lanes), max(1, rows // 32)
     space, spec = (pltpu.VMEM, in_vmem) if near_by else (pltpu.HBM, in_hbm)
-    args = [slots, scale] + [pin(block, space) for block in blocks] + ([] if out is None else [pin(out)])
+    args = [pin(slots, pltpu.VMEM), pin(scale, pltpu.VMEM)] + [pin(block, space) for block in blocks] + ([] if out is None else [pin(out)])
     return pl.pallas_call(
         functools.partial(place_kernel, lanes, near_by),
         out_shape=pltpu.HBM((row_count, feats), jnp.float32),
-        in_specs=[in_smem, in_vmem] + [spec] * count + ([] if out is None else [in_hbm]),
+        in_specs=[in_vmem, in_vmem] + [spec] * count + ([] if out is None else [in_hbm]),
         out_specs=in_hbm,
         scratch_shapes=[
             pltpu.VMEM((count, parts, rows // parts, feats), jnp.float32),
@@ -188,7 +188,7 @@
 def merge_chunk(told, row_count, feats):
     peers, outer_count = told.shape[0], lax.axis_size("outer")
     chunk = feats // peers
-    slots = told[:, 0, 2 * chunk].astype(jnp.int32)[lane_base(peers) ^ jnp.arange(peers, dtype=jnp.int32)]
+    slots = told[:, 0, message_width - 128 :].astype(jnp.int32)[lane_base(peers) ^ jnp.arange(peers, dtype=jnp.int32)]
     level_count = row_count
     centers, spreads = told[:, 0, :chunk], told[:, 0, chunk : 2 * chunk]
     while centers.shape[0] > 1:

time: 191 us -> 190 us (level)
  waiting for transfers between devices: 128 us -> 124 us
  starting transfers between devices: 38.3 us -> 42.1 us
    ppermute x16, starting transfers between devices: 22.7 us -> 26.4 us  [send(): return lax.ppermute(block, ('outer', 'inner'), pairs)]
    ppermute x16, waiting for transfers between devices: 102 us -> 98.1 us  [send(): return lax.ppermute(block, ('outer', 'inner'), pairs)]
    pallas_call x3 -> x4, Pallas kernels: 10.6 us -> 9.99 us  [place(): pl.pallas_call(functools.partial(place_kernel, lanes, near_by), out_shape...]
  transfers between devices with their start and end apart: 19 -> 19, of which waited for: 9 -> 9; matrix products, arithmetic and copies ran while one was open for 2% -> 1% of each run, Pallas kernels for 8% -> 8%
where the time goes in v5:
time: 190 us; the launch traced here: 189 us
  waiting for transfers between devices  124 us (65%)
  starting transfers between devices  42.1 us (22%)
  Pallas kernels  19.3 us (10%)
    ppermute x16, waiting for transfers between devices, send(): return lax.ppermute(block, ('outer', 'inner'), pairs)  98.1 us
    ppermute x16, starting transfers between devices, send(): return lax.ppermute(block, ('outer', 'inner'), pairs)  26.4 us
    all_to_all x2, waiting for transfers between devices, body(): lax.all_to_all(extra[0], 'inner', split_axis=0, concat_axis=0, tiled=True)  25.9 us
    all_to_all x2, starting transfers between devices, body(): lax.all_to_all(extra[0], 'inner', split_axis=0, concat_axis=0, tiled=True)  15.6 us
    pallas_call x4, Pallas kernels, place(): pl.pallas_call(functools.partial(place_kernel, lanes, near_by), out_shape...  9.99 us
    pallas_call x1, Pallas kernels, pick_rest(): pl.pallas_call(functools.partial(rest_kernel, lanes, first), out_shape=[j...  7.29 us
  transfers between devices with their start and end apart: 19, of which 9 were waited for; matrix products, arithmetic and copies ran while one was open for 1% of the time, Pallas kernels for 8%

profile of v5, /device:TPU:8, one launch (start us, length us, event | category | flops | bytes accessed | tf_op | source)
XLA Modules:
  0.0 188.9 jit_solution(17165928859417388576)
XLA Ops:
  0.6 2.0 %pick_first.1 = (f32[128,1024]{1,0:T(8,128)S(1)}, f32[128,1024]{1,0:T(8,128)S(1)}) custom-call(s32[16]{0:T(128)} %dest_ref.2, f32[2048,1024]{1,0:T(8,128)} %features_ref.3), custom_call_target="tpu_custom_call" | custom-call | tf_op jit(solution)/shard_map/pick_first/pallas_call | solution.py:74
  2.7 1.6 collective-permute-start
  4.3 4.5 %collective-permute-start.9 = (f32[128,1024]{1,0:T(8,128)S(1)}, f32[128,1024]{1,0:T(8,128)S(1)}, u32[]{:S(2)}, u32[]{:S(2)}) collective-permute-start(f32[128,1024]{1,0:T(8,128)S(1)} %get-tuple-element.78), channel_id=1, source_target_pairs={{0,8},{1,9},{2,10},{3,11},{4,12},{5,13},{6,14},{7,15},{8,0},{9,1},... | collective-permute-start | bytes 1572872 | tf_op jit(solution)/shard_map/ppermute | solution.py:223
  8.8 7.3 %pick_rest.1 = (f32[16,1,256]{2,1,0:T(1,128)}, f32[128,1024]{1,0:T(8,128)}, f32[128,1024]{1,0:T(8,128)}, f32[128,1024]{1,0:T(8,128)}, f32[128,1024]{1,0:T(8,128)...) custom-call(s32[16]{0:T(128)S(1)} %copy-done, ...), custom_call_target="tpu_custom_call" | custom-call | flops 12582912 | bytes 16777216 | tf_op jit(solution)/shard_map/pick_rest/pallas_call | solution.py:124
  16.1 1.6 collective-permute-start.3
  17.9 1.4 collective-permute-start.1
  19.3 8.1 %all-to-all-start = ((f32[16,1,256]{2,1,0:T(1,128)}), f32[16,1,256]{2,1,0:T(1,128)S(1)}, u32[]{:S(2)}, u32[]{:S(2)}) async-start(f32[16,1,256]{2,1,0:T(1,128)} %get-tuple-element.61), calls=%async_computation | async-start | bytes 32768 | tf_op jit(solution)/shard_map/all_to_all | solution.py:247
  27.4 12.6 %collective-permute-done.9.rest_0_ = f32[128,1024]{1,0:T(8,128)S(1)} collective-permute-done((f32[128,1024]{1,0:T(8,128)S(1)}, f32[128,1024]{1,0:T(8,128)S(1)}, u32[]{:S(2)}, u32[]{:S(2)}) %collective-permute-start.9) | collective-permute-done | bytes 524320 | tf_op jit(solution)/shard_map/ppermute | solution.py:223
  40.0 0.5 collective-permute-start.10
  40.5 5.3 %collective-permute-start.4 = (f32[128,1024]{1,0:T(8,128)}, f32[128,1024]{1,0:T(8,128)}, u32[]{:S(2)}, u32[]{:S(2)}) collective-permute-start(f32[128,1024]{1,0:T(8,128)} %get-tuple-element.68), channel_id=1, source_target_pairs={{0,7},{1,6},{2,5},{3,4},{4,3},{5,2},{6,1},{7,0},{8,15},{9,14},{10,... | collective-permute-start | bytes 1572872 | tf_op jit(solution)/shard_map/ppermute | solution.py:223
  45.8 16.9 %collective-permute-done.6.rest_2_ = f32[128,1024]{1,0:T(8,128)S(1)} collective-permute-done((f32[128,1024]{1,0:T(8,128)}, f32[128,1024]{1,0:T(8,128)S(1)}, u32[]{:S(2)}, u32[]{:S(2)}) %collective-permute-start.6) | collective-permute-done | bytes 524320 | tf_op jit(solution)/shard_map/ppermute | solution.py:223
  62.7 1.5 collective-permute-start.7
  64.1 0.5 all-to-all-done
  65.0 21.2 %collective-permute-done.10.rest_4_ = f32[128,1024]{1,0:T(8,128)S(1)} collective-permute-done((f32[128,1024]{1,0:T(8,128)}, f32[128,1024]{1,0:T(8,128)S(1)}, u32[]{:S(2)}, u32[]{:S(2)}) %collective-permute-start.10) | collective-permute-done | bytes 524320 | tf_op jit(solution)/shard_map/ppermute | solution.py:223
  86.3 4.7 %collective-permute-start.11 = (f32[128,1024]{1,0:T(8,128)}, f32[128,1024]{1,0:T(8,128)}, u32[]{:S(2)}, u32[]{:S(2)}) collective-permute-start(f32[128,1024]{1,0:T(8,128)} %get-tuple-element.90), channel_id=1, source_target_pairs={{0,9},{1,8},{2,11},{3,10},{4,13},{5,12},{6,15},{7,14},{8,1},{9,0},... | collective-permute-start | bytes 1572872 | tf_op jit(solution)/shard_map/ppermute | solution.py:223
  90.9 0.6 collective-permute-start.2
  91.5 19.7 %collective-permute-done.7.rest_6_ = f32[128,1024]{1,0:T(8,128)} collective-permute-done((f32[128,1024]{1,0:T(8,128)}, f32[128,1024]{1,0:T(8,128)}, u32[]{:S(2)}, u32[]{:S(2)}) %collective-permute-start.7) | collective-permute-done | bytes 524320 | tf_op jit(solution)/shard_map/ppermute | solution.py:223
  111.3 0.6 broadcast_in_dim.9
  111.9 7.5 %all-to-all-start.1 = ((f32[16,1,128]{2,1,0:T(1,128)}), f32[16,1,128]{2,1,0:T(1,128)S(1)}, u32[]{:S(2)}, u32[]{:S(2)}) async-start(f32[16,1,128]{2,1,0:T(1,128)} %broadcast_in_dim.9), calls=%async_computation.1 | async-start | bytes 16384 | tf_op jit(solution)/shard_map/all_to_all | solution.py:251
  119.6 0.6 gather_fusion
  120.1 10.2 %collective-permute-done.11.rest_8_ = f32[128,1024]{1,0:T(8,128)} collective-permute-done((f32[128,1024]{1,0:T(8,128)}, f32[128,1024]{1,0:T(8,128)}, u32[]{:S(2)}, u32[]{:S(2)}) %collective-permute-start.11) | collective-permute-done | bytes 524320 | tf_op jit(solution)/shard_map/ppermute | solution.py:223
  130.7 25.5 %all-to-all-done.1 = f32[16,1,128]{2,1,0:T(1,128)S(1)} async-done(((f32[16,1,128]{2,1,0:T(1,128)}), f32[16,1,128]{2,1,0:T(1,128)S(1)}, u32[]{:S(2)}, u32[]{:S(2)}) %all-to-all-start.1) | async-done | bytes 8224 | tf_op jit(solution)/shard_map/all_to_all | solution.py:251
  156.4 0.6 collective-permute-start.16
  157.0 0.6 pad_maximum_fusion
  157.6 5.3 %place.4.rest_2_ = f32[2048,1024]{1,0:T(8,128)} custom-call(s32[16,128]{1,0:T(8,128)S(1)} %gather_fusion, f32[2,1024]{1,0:T(2,128)S(1)} %get-tuple-element.107.scale_ref, f32[128,1024]{1,0:T(8,128)} %copy-done.5, f32[128,1024]{1,0:T(8,128)} %copy-done.4, f32[128,1024]{1,0:T(8,128)} %copy-done.7, f32[128,1024]{1,0:T(8,128)} %copy-done.6, ...), custom_call_target="tpu_custom_call" | custom-call | flops 5242880 | bytes 10485760 | tf_op jit(solution)/shard_map/place/pallas_call | solution.py:171
  162.9 3.0 %collective-permute-start.12 = (f32[128,1024]{1,0:T(8,128)S(1)}, f32[128,1024]{1,0:T(8,128)S(1)}, u32[]{:S(2)}, u32[]{:S(2)}) collective-permute-start(f32[128,1024]{1,0:T(8,128)S(1)} %copy-done.11), channel_id=1, source_target_pairs={{0,15},{1,14},{2,13},{3,12},{4,11},{5,10},{6,9},{7,8},{8,7},{9,6},... | collective-permute-start | bytes 1572872 | tf_op jit(solution)/shard_map/ppermute | solution.py:223
  165.9 0.7 collective-permute-start.14
  166.7 2.1 %place.5.rest_2_ = f32[2048,1024]{1,0:T(8,128)} custom-call(s32[16,128]{1,0:T(8,128)S(1)} %gather_fusion, f32[2,1024]{1,0:T(2,128)S(1)} %get-tuple-element.107.scale_ref, f32[128,1024]{1,0:T(8,128)} %copy-done.2, f32[128,1024]{1,0:T(8,128)} %copy-done.3, f32[2048,1024]{1,0:T(8,128)} %place.4.rest_2_), custom_call_target="tpu_custom_call", output_to_operand_aliasing={{}: (4, {})} | custom-call | flops 1048576 | bytes 2097152 | tf_op jit(solution)/shard_map/place/pallas_call | solution.py:171
  168.8 7.7 %collective-permute-done.15.rest_0_ = f32[128,1024]{1,0:T(8,128)S(1)} collective-permute-done((f32[128,1024]{1,0:T(8,128)}, f32[128,1024]{1,0:T(8,128)S(1)}, u32[]{:S(2)}, u32[]{:S(2)}) %collective-permute-start.15) | collective-permute-done | bytes 524320 | tf_op jit(solution)/shard_map/ppermute | solution.py:223
  176.5 1.3 place.6.rest_2_
  177.8 9.8 %collective-permute-done.12.rest_0_ = f32[128,1024]{1,0:T(8,128)S(1)} collective-permute-done((f32[128,1024]{1,0:T(8,128)S(1)}, f32[128,1024]{1,0:T(8,128)S(1)}, u32[]{:S(2)}, u32[]{:S(2)}) %collective-permute-start.12) | collective-permute-done | bytes 524320 | tf_op jit(solution)/shard_map/ppermute | solution.py:223
  187.6 1.3 place.7
  (69 shorter events, 1.7 us)
Async XLA Ops:
  0.6 8.1 %copy-start = (s32[16]{0:T(128)S(1)}, s32[16]{0:T(128)}, u32[]{:S(2)}) copy-start(s32[16]{0:T(128)} %dest_ref.2) | copy-start | bytes 196
  0.6 8.1 %copy-start.1 = (s32[16]{0:T(128)S(1)}, s32[16]{0:T(128)}, u32[]{:S(2)}) copy-start(s32[16]{0:T(128)} %slot_ref) | copy-start | bytes 196
  2.7 15.2 %collective-permute-start = (f32[128,1024]{1,0:T(8,128)S(1)}, f32[128,1024]{1,0:T(8,128)S(1)}, u32[]{:S(2)}, u32[]{:S(2)}) collective-permute-start(f32[128,1024]{1,0:T(8,128)S(1)} %get-tuple-element.58), channel_id=1, source_target_pairs={{0,1},{1,0},{2,3},{3,2},{4,5},{5,4},{6,7},{7,6},{8,9},{9,8},{10,11... | collective-permute-start | bytes 1572872 | tf_op jit(solution)/shard_map/ppermute | solution.py:223
  4.3 35.7 %collective-permute-start.9 = (f32[128,1024]{1,0:T(8,128)S(1)}, f32[128,1024]{1,0:T(8,128)S(1)}, u32[]{:S(2)}, u32[]{:S(2)}) collective-permute-start(f32[128,1024]{1,0:T(8,128)S(1)} %get-tuple-element.78), channel_id=1, source_target_pairs={{0,8},{1,9},{2,10},{3,11},{4,12},{5,13},{6,14},{7,15},{8,0},{9,1},... | collective-permute-start | bytes 1572872 | tf_op jit(solution)/shard_map/ppermute | solution.py:223
  16.1 24.5 %collective-permute-start.3 = (f32[128,1024]{1,0:T(8,128)}, f32[128,1024]{1,0:T(8,128)S(1)}, u32[]{:S(2)}, u32[]{:S(2)}) collective-permute-start(f32[128,1024]{1,0:T(8,128)} %get-tuple-element.67), channel_id=1, source_target_pairs={{0,3},{1,2},{2,1},{3,0},{4,7},{5,6},{6,5},{7,4},{8,11},{9,10},{10,... | collective-permute-start | bytes 1572872 | tf_op jit(solution)/shard_map/ppermute | solution.py:223
  17.6 45.0 %collective-permute-start.6 = (f32[128,1024]{1,0:T(8,128)}, f32[128,1024]{1,0:T(8,128)S(1)}, u32[]{:S(2)}, u32[]{:S(2)}) collective-permute-start(f32[128,1024]{1,0:T(8,128)} %get-tuple-element.74), channel_id=1, source_target_pairs={{0,10},{1,11},{2,8},{3,9},{4,14},{5,15},{6,12},{7,13},{8,2},{9,3},... | collective-permute-start | bytes 1572872 | tf_op jit(solution)/shard_map/ppermute | solution.py:223
  17.9 139.7 %copy-start.4 = (f32[128,1024]{1,0:T(8,128)}, f32[128,1024]{1,0:T(8,128)S(1)}, u32[]{:S(2)}) copy-start(f32[128,1024]{1,0:T(8,128)S(1)} %collective-permute-done.rest_1_) | copy-start | bytes 1572868
  17.9 46.7 %collective-permute-start.1 = (f32[128,1024]{1,0:T(8,128)}, f32[128,1024]{1,0:T(8,128)S(1)}, u32[]{:S(2)}, u32[]{:S(2)}) collective-permute-start(f32[128,1024]{1,0:T(8,128)} %get-tuple-element.60), channel_id=1, source_target_pairs={{0,5},{1,4},{2,7},{3,6},{4,1},{5,0},{6,3},{7,2},{8,13},{9,12},{10,... | collective-permute-start | bytes 1572872 | tf_op jit(solution)/shard_map/ppermute | solution.py:223
  19.3 45.3 %all-to-all-start = ((f32[16,1,256]{2,1,0:T(1,128)}), f32[16,1,256]{2,1,0:T(1,128)S(1)}, u32[]{:S(2)}, u32[]{:S(2)}) async-start(f32[16,1,256]{2,1,0:T(1,128)} %get-tuple-element.61), calls=%async_computation | async-start | bytes 32768 | tf_op jit(solution)/shard_map/all_to_all | solution.py:247
  40.0 117.6 %copy-start.5 = (f32[128,1024]{1,0:T(8,128)}, f32[128,1024]{1,0:T(8,128)S(1)}, u32[]{:S(2)}) copy-start(f32[128,1024]{1,0:T(8,128)S(1)} %collective-permute-done.9.rest_0_) | copy-start | bytes 1572868
  40.0 46.2 %collective-permute-start.10 = (f32[128,1024]{1,0:T(8,128)}, f32[128,1024]{1,0:T(8,128)S(1)}, u32[]{:S(2)}, u32[]{:S(2)}) collective-permute-start(f32[128,1024]{1,0:T(8,128)} %get-tuple-element.84), channel_id=1, source_target_pairs={{0,12},{1,13},{2,14},{3,15},{4,8},{5,9},{6,10},{7,11},{8,4},{9,5},... | collective-permute-start | bytes 1572872 | tf_op jit(solution)/shard_map/ppermute | solution.py:223
  40.5 117.1 %copy-start.6 = (f32[128,1024]{1,0:T(8,128)}, f32[128,1024]{1,0:T(8,128)S(1)}, u32[]{:S(2)}) copy-start(f32[128,1024]{1,0:T(8,128)S(1)} %collective-permute-done.3.rest_3_) | copy-start | bytes 1572868
  40.5 70.8 %collective-permute-start.4 = (f32[128,1024]{1,0:T(8,128)}, f32[128,1024]{1,0:T(8,128)}, u32[]{:S(2)}, u32[]{:S(2)}) collective-permute-start(f32[128,1024]{1,0:T(8,128)} %get-tuple-element.68), channel_id=1, source_target_pairs={{0,7},{1,6},{2,5},{3,4},{4,3},{5,2},{6,1},{7,0},{8,15},{9,14},{10,... | collective-permute-start | bytes 1572872 | tf_op jit(solution)/shard_map/ppermute | solution.py:223
  62.7 48.5 %copy-start.7 = (f32[128,1024]{1,0:T(8,128)}, f32[128,1024]{1,0:T(8,128)S(1)}, u32[]{:S(2)}) copy-start(f32[128,1024]{1,0:T(8,128)S(1)} %collective-permute-done.6.rest_2_) | copy-start | bytes 1572868
  62.7 48.5 %collective-permute-start.7 = (f32[128,1024]{1,0:T(8,128)}, f32[128,1024]{1,0:T(8,128)}, u32[]{:S(2)}, u32[]{:S(2)}) collective-permute-start(f32[128,1024]{1,0:T(8,128)} %get-tuple-element.75), channel_id=1, source_target_pairs={{0,14},{1,15},{2,12},{3,13},{4,10},{5,11},{6,8},{7,9},{8,6},{9,7},... | collective-permute-start | bytes 1572872 | tf_op jit(solution)/shard_map/ppermute | solution.py:223
  64.6 46.6 %copy-start.8 = (f32[128,1024]{1,0:T(8,128)}, f32[128,1024]{1,0:T(8,128)S(1)}, u32[]{:S(2)}) copy-start(f32[128,1024]{1,0:T(8,128)S(1)} %collective-permute-done.1.rest_5_) | copy-start | bytes 1572868
  86.2 33.2 %copy-start.9 = (f32[128,1024]{1,0:T(8,128)}, f32[128,1024]{1,0:T(8,128)S(1)}, u32[]{:S(2)}) copy-start(f32[128,1024]{1,0:T(8,128)S(1)} %collective-permute-done.10.rest_4_) | copy-start | bytes 1572868
  86.2 25.0 %collective-permute-start.5 = (f32[2,64]{1,0:T(2,128)S(1)}, f32[2,64]{1,0:T(2,128)S(1)}, u32[]{:S(2)}, u32[]{:S(2)}) collective-permute-start(f32[2,64]{1,0:T(2,128)S(1)} %pad_maximum_fusion.2), channel_id=1, source_target_pairs={{0,16},{16,0},{1,17},{17,1},{2,18},{18,2},{3,19},{19,3},{4,20},{20... | collective-permute-start | bytes 1544 | tf_op jit(solution)/shard_map/ppermute | solution.py:199
  86.3 44.1 %collective-permute-start.11 = (f32[128,1024]{1,0:T(8,128)}, f32[128,1024]{1,0:T(8,128)}, u32[]{:S(2)}, u32[]{:S(2)}) collective-permute-start(f32[128,1024]{1,0:T(8,128)} %get-tuple-element.90), channel_id=1, source_target_pairs={{0,9},{1,8},{2,11},{3,10},{4,13},{5,12},{6,15},{7,14},{8,1},{9,0},... | collective-permute-start | bytes 1572872 | tf_op jit(solution)/shard_map/ppermute | solution.py:223
  90.9 65.2 %collective-permute-start.2 = (f32[128,1024]{1,0:T(8,128)}, f32[128,1024]{1,0:T(8,128)}, u32[]{:S(2)}, u32[]{:S(2)}) collective-permute-start(f32[128,1024]{1,0:T(8,128)} %get-tuple-element.64), channel_id=1, source_target_pairs={{0,2},{1,3},{2,0},{3,1},{4,6},{5,7},{6,4},{7,5},{8,10},{9,11},{10,... | collective-permute-start | bytes 1572872 | tf_op jit(solution)/shard_map/ppermute | solution.py:223
  111.2 51.7 %collective-permute-start.8 = (f32[128,1024]{1,0:T(8,128)}, f32[128,1024]{1,0:T(8,128)S(1)}, u32[]{:S(2)}, u32[]{:S(2)}) collective-permute-start(f32[128,1024]{1,0:T(8,128)} %get-tuple-element.76), channel_id=1, source_target_pairs={{0,11},{1,10},{2,9},{3,8},{4,15},{5,14},{6,13},{7,12},{8,3},{9,2},... | collective-permute-start | bytes 1572872 | tf_op jit(solution)/shard_map/ppermute | solution.py:223
  111.9 44.2 %all-to-all-start.1 = ((f32[16,1,128]{2,1,0:T(1,128)}), f32[16,1,128]{2,1,0:T(1,128)S(1)}, u32[]{:S(2)}, u32[]{:S(2)}) async-start(f32[16,1,128]{2,1,0:T(1,128)} %broadcast_in_dim.9), calls=%async_computation.1 | async-start | bytes 16384 | tf_op jit(solution)/shard_map/all_to_all | solution.py:251
  119.4 46.5 %collective-permute-start.13 = (f32[128,1024]{1,0:T(8,128)}, f32[128,1024]{1,0:T(8,128)S(1)}, u32[]{:S(2)}, u32[]{:S(2)}) collective-permute-start(f32[128,1024]{1,0:T(8,128)} %get-tuple-element.95), channel_id=1, source_target_pairs={{0,4},{1,5},{2,6},{3,7},{4,0},{5,1},{6,2},{7,3},{8,12},{9,13},{10,... | collective-permute-start | bytes 1572872 | tf_op jit(solution)/shard_map/ppermute | solution.py:223
  130.4 46.1 %collective-permute-start.15 = (f32[128,1024]{1,0:T(8,128)}, f32[128,1024]{1,0:T(8,128)S(1)}, u32[]{:S(2)}, u32[]{:S(2)}) collective-permute-start(f32[128,1024]{1,0:T(8,128)} %get-tuple-element.97), channel_id=1, source_target_pairs={{0,13},{1,12},{2,15},{3,14},{4,9},{5,8},{6,11},{7,10},{8,5},{9,4},... | collective-permute-start | bytes 1572872 | tf_op jit(solution)/shard_map/ppermute | solution.py:223
  156.4 6.6 %copy-start.11 = (f32[128,1024]{1,0:T(8,128)S(1)}, f32[128,1024]{1,0:T(8,128)}, u32[]{:S(2)}) copy-start(f32[128,1024]{1,0:T(8,128)} %get-tuple-element.93) | copy-start | bytes 1572868
  156.4 9.5 %copy-start.10 = (f32[128,1024]{1,0:T(8,128)S(1)}, f32[128,1024]{1,0:T(8,128)}, u32[]{:S(2)}) copy-start(f32[128,1024]{1,0:T(8,128)} %get-tuple-element.96) | copy-start | bytes 1572868
  156.4 20.1 %collective-permute-start.16 = (f32[128,1024]{1,0:T(8,128)}, f32[128,1024]{1,0:T(8,128)S(1)}, u32[]{:S(2)}, u32[]{:S(2)}) collective-permute-start(f32[128,1024]{1,0:T(8,128)} %get-tuple-element.98), channel_id=1, source_target_pairs={{0,6},{1,7},{2,4},{3,5},{4,2},{5,3},{6,0},{7,1},{8,14},{9,15},{10,... | collective-permute-start | bytes 1572872 | tf_op jit(solution)/shard_map/ppermute | solution.py:223
  162.9 3.7 %copy-start.2 = (f32[128,1024]{1,0:T(8,128)}, f32[128,1024]{1,0:T(8,128)S(1)}, u32[]{:S(2)}) copy-start(f32[128,1024]{1,0:T(8,128)S(1)} %collective-permute-done.8.rest_0_) | copy-start | bytes 1572868
  162.9 24.7 %collective-permute-start.12 = (f32[128,1024]{1,0:T(8,128)S(1)}, f32[128,1024]{1,0:T(8,128)S(1)}, u32[]{:S(2)}, u32[]{:S(2)}) collective-permute-start(f32[128,1024]{1,0:T(8,128)S(1)} %copy-done.11), channel_id=1, source_target_pairs={{0,15},{1,14},{2,13},{3,12},{4,11},{5,10},{6,9},{7,8},{8,7},{9,6},... | collective-permute-start | bytes 1572872 | tf_op jit(solution)/shard_map/ppermute | solution.py:223
  165.9 0.8 copy-start.3
  165.9 21.7 %collective-permute-start.14 = (f32[128,1024]{1,0:T(8,128)S(1)}, f32[128,1024]{1,0:T(8,128)S(1)}, u32[]{:S(2)}, u32[]{:S(2)}) collective-permute-start(f32[128,1024]{1,0:T(8,128)S(1)} %copy-done.10), channel_id=1, source_target_pairs={{0,0},{1,1},{2,2},{3,3},{4,4},{5,5},{6,6},{7,7},{8,8},{9,9},{10,10... | collective-permute-start | bytes 1572872 | tf_op jit(solution)/shard_map/ppermute | solution.py:223

commit v6 on v5

--- a/solution.py
+++ b/solution.py
@@ -31,10 +31,13 @@
 
 
 def lane_order(peers):
-    half = peers // 2
-    far = list(range(0, half, 2)) + list(range(1, half, 2))
-    near = list(range(1, half, 2)) + list(range(2, half, 2)) + [0]
-    return [lane for f, n in zip(far, near) for lane in (half + f, n)]
+    half, quarter = peers // 2, peers // 4
+    far = [half + k for k in (*range(0, half, 2), *range(1, half, 2))]
+    far[-2:] = far[:-3:-1]
+    near = [*range(1, half, 2), *range(2, half, 2), 0]
+    at = near.index(quarter)
+    near[0], near[at] = quarter, near[0]
+    return [lane for pair in zip(far, near) for lane in pair]
 
 
 def last_cuts(peers):

time: 190 us -> 189 us (level)
    ppermute x16, waiting for transfers between devices: 98.1 us -> 94.7 us  [send(): return lax.ppermute(block, ('outer', 'inner'), pairs)]
    all_to_all x2, waiting for transfers between devices: 25.9 us -> 29 us  [body(): lax.all_to_all(extra[0], 'inner', split_axis=0, concat_axis=0, tiled=True)]
where the time goes in v6:
time: 189 us; the launch traced here: 188 us
  waiting for transfers between devices  124 us (66%)
  starting transfers between devices  41.8 us (22%)
  Pallas kernels  19.3 us (10%)
    ppermute x16, waiting for transfers between devices, send(): return lax.ppermute(block, ('outer', 'inner'), pairs)  94.7 us
    all_to_all x2, waiting for transfers between devices, body(): lax.all_to_all(extra[0], 'inner', split_axis=0, concat_axis=0, tiled=True)  29 us
    ppermute x16, starting transfers between devices, send(): return lax.ppermute(block, ('outer', 'inner'), pairs)  27.5 us
    all_to_all x2, starting transfers between devices, body(): lax.all_to_all(extra[0], 'inner', split_axis=0, concat_axis=0, tiled=True)  14.2 us
    pallas_call x4, Pallas kernels, place(): pl.pallas_call(functools.partial(place_kernel, lanes, near_by), out_shape...  9.99 us
    pallas_call x1, Pallas kernels, pick_rest(): pl.pallas_call(functools.partial(rest_kernel, lanes, first), out_shape=[j...  7.29 us
  transfers between devices with their start and end apart: 19, of which 9 were waited for; matrix products, arithmetic and copies ran while one was open for 1% of the time, Pallas kernels for 8%

profile of v6, /device:TPU:8, one launch (start us, length us, event | category | flops | bytes accessed | tf_op | source)
XLA Modules:
  0.0 188.3 jit_solution(14702892962331213313)
XLA Ops:
  0.6 2.0 %pick_first.1 = (f32[128,1024]{1,0:T(8,128)S(1)}, f32[128,1024]{1,0:T(8,128)S(1)}) custom-call(s32[16]{0:T(128)} %dest_ref.2, f32[2048,1024]{1,0:T(8,128)} %features_ref.3), custom_call_target="tpu_custom_call" | custom-call | tf_op jit(solution)/shard_map/pick_first/pallas_call | solution.py:77
  2.8 4.9 %collective-permute-start.9 = (f32[128,1024]{1,0:T(8,128)S(1)}, f32[128,1024]{1,0:T(8,128)S(1)}, u32[]{:S(2)}, u32[]{:S(2)}) collective-permute-start(f32[128,1024]{1,0:T(8,128)S(1)} %get-tuple-element.78), channel_id=1, source_target_pairs={{0,8},{1,9},{2,10},{3,11},{4,12},{5,13},{6,14},{7,15},{8,0},{9,1},... | collective-permute-start | bytes 1572872 | tf_op jit(solution)/shard_map/ppermute | solution.py:226
  7.7 7.3 %pick_rest.1 = (f32[16,1,256]{2,1,0:T(1,128)}, f32[128,1024]{1,0:T(8,128)}, f32[128,1024]{1,0:T(8,128)}, f32[128,1024]{1,0:T(8,128)}, f32[128,1024]{1,0:T(8,128)...) custom-call(s32[16]{0:T(128)S(1)} %copy-done, ...), custom_call_target="tpu_custom_call" | custom-call | flops 12582912 | bytes 16777216 | tf_op jit(solution)/shard_map/pick_rest/pallas_call | solution.py:127
  15.0 2.5 %collective-permute-start.3 = (f32[128,1024]{1,0:T(8,128)}, f32[128,1024]{1,0:T(8,128)S(1)}, u32[]{:S(2)}, u32[]{:S(2)}) collective-permute-start(f32[128,1024]{1,0:T(8,128)} %get-tuple-element.67), channel_id=1, source_target_pairs={{0,3},{1,2},{2,1},{3,0},{4,7},{5,6},{6,5},{7,4},{8,11},{9,10},{10,... | collective-permute-start | bytes 1572872 | tf_op jit(solution)/shard_map/ppermute | solution.py:226
  17.5 0.3 collective-permute-start.6
  17.8 3.4 %collective-permute-start.1 = (f32[128,1024]{1,0:T(8,128)}, f32[128,1024]{1,0:T(8,128)S(1)}, u32[]{:S(2)}, u32[]{:S(2)}) collective-permute-start(f32[128,1024]{1,0:T(8,128)} %get-tuple-element.60), channel_id=1, source_target_pairs={{0,5},{1,4},{2,7},{3,6},{4,1},{5,0},{6,3},{7,2},{8,13},{9,12},{10,... | collective-permute-start | bytes 1572872 | tf_op jit(solution)/shard_map/ppermute | solution.py:226
  21.2 5.9 %all-to-all-start = ((f32[16,1,256]{2,1,0:T(1,128)}), f32[16,1,256]{2,1,0:T(1,128)S(1)}, u32[]{:S(2)}, u32[]{:S(2)}) async-start(f32[16,1,256]{2,1,0:T(1,128)} %get-tuple-element.61), calls=%async_computation | async-start | bytes 32768 | tf_op jit(solution)/shard_map/all_to_all | solution.py:250
  27.1 19.9 %collective-permute-done.9.rest_0_ = f32[128,1024]{1,0:T(8,128)S(1)} collective-permute-done((f32[128,1024]{1,0:T(8,128)S(1)}, f32[128,1024]{1,0:T(8,128)S(1)}, u32[]{:S(2)}, u32[]{:S(2)}) %collective-permute-start.9) | collective-permute-done | bytes 524320 | tf_op jit(solution)/shard_map/ppermute | solution.py:226
  47.0 6.7 %collective-permute-start.4 = (f32[128,1024]{1,0:T(8,128)}, f32[128,1024]{1,0:T(8,128)}, u32[]{:S(2)}, u32[]{:S(2)}) collective-permute-start(f32[128,1024]{1,0:T(8,128)} %get-tuple-element.68), channel_id=1, source_target_pairs={{0,7},{1,6},{2,5},{3,4},{4,3},{5,2},{6,1},{7,0},{8,15},{9,14},{10,... | collective-permute-start | bytes 1572872 | tf_op jit(solution)/shard_map/ppermute | solution.py:226
  53.7 14.6 %collective-permute-done.6.rest_2_ = f32[128,1024]{1,0:T(8,128)S(1)} collective-permute-done((f32[128,1024]{1,0:T(8,128)}, f32[128,1024]{1,0:T(8,128)S(1)}, u32[]{:S(2)}, u32[]{:S(2)}) %collective-permute-start.6) | collective-permute-done | bytes 524320 | tf_op jit(solution)/shard_map/ppermute | solution.py:226
  68.3 0.2 all-to-all-done
  69.0 17.7 %collective-permute-done.10.rest_4_ = f32[128,1024]{1,0:T(8,128)S(1)} collective-permute-done((f32[128,1024]{1,0:T(8,128)}, f32[128,1024]{1,0:T(8,128)S(1)}, u32[]{:S(2)}, u32[]{:S(2)}) %collective-permute-start.10) | collective-permute-done | bytes 524320 | tf_op jit(solution)/shard_map/ppermute | solution.py:226
  86.9 1.6 collective-permute-start.2
  88.4 22.4 %collective-permute-done.7.rest_6_ = f32[128,1024]{1,0:T(8,128)} collective-permute-done((f32[128,1024]{1,0:T(8,128)}, f32[128,1024]{1,0:T(8,128)}, u32[]{:S(2)}, u32[]{:S(2)}) %collective-permute-start.7) | collective-permute-done | bytes 524320 | tf_op jit(solution)/shard_map/ppermute | solution.py:226
  110.9 0.6 broadcast_in_dim.9
  111.5 8.3 %all-to-all-start.1 = ((f32[16,1,128]{2,1,0:T(1,128)}), f32[16,1,128]{2,1,0:T(1,128)S(1)}, u32[]{:S(2)}, u32[]{:S(2)}) async-start(f32[16,1,128]{2,1,0:T(1,128)} %broadcast_in_dim.9), calls=%async_computation.1 | async-start | bytes 16384 | tf_op jit(solution)/shard_map/all_to_all | solution.py:254
  119.9 1.5 collective-permute-start.13
  121.4 0.6 gather_fusion
  122.0 9.2 %collective-permute-done.11.rest_8_ = f32[128,1024]{1,0:T(8,128)} collective-permute-done((f32[128,1024]{1,0:T(8,128)}, f32[128,1024]{1,0:T(8,128)}, u32[]{:S(2)}, u32[]{:S(2)}) %collective-permute-start.11) | collective-permute-done | bytes 524320 | tf_op jit(solution)/shard_map/ppermute | solution.py:226
  131.2 1.7 collective-permute-start.15
  132.9 28.8 %all-to-all-done.1 = f32[16,1,128]{2,1,0:T(1,128)S(1)} async-done(((f32[16,1,128]{2,1,0:T(1,128)}), f32[16,1,128]{2,1,0:T(1,128)S(1)}, u32[]{:S(2)}, u32[]{:S(2)}) %all-to-all-start.1) | async-done | bytes 8224 | tf_op jit(solution)/shard_map/all_to_all | solution.py:254
  161.7 0.1 multiply_reduce_fusion
  161.9 1.7 collective-permute-start.16
  163.7 0.6 pad_maximum_fusion
  164.3 5.3 %place.4.rest_2_ = f32[2048,1024]{1,0:T(8,128)} custom-call(s32[16,128]{1,0:T(8,128)S(1)} %gather_fusion, f32[2,1024]{1,0:T(2,128)S(1)} %get-tuple-element.107.scale_ref, f32[128,1024]{1,0:T(8,128)} %copy-done.5, f32[128,1024]{1,0:T(8,128)} %copy-done.4, f32[128,1024]{1,0:T(8,128)} %copy-done.7, f32[128,1024]{1,0:T(8,128)} %copy-done.6, ...), custom_call_target="tpu_custom_call" | custom-call | flops 5242880 | bytes 10485760 | tf_op jit(solution)/shard_map/place/pallas_call | solution.py:174
  169.7 2.3 %collective-permute-start.12 = (f32[128,1024]{1,0:T(8,128)S(1)}, f32[128,1024]{1,0:T(8,128)S(1)}, u32[]{:S(2)}, u32[]{:S(2)}) collective-permute-start(f32[128,1024]{1,0:T(8,128)S(1)} %copy-done.11), channel_id=1, source_target_pairs={{0,13},{1,12},{2,15},{3,14},{4,9},{5,8},{6,11},{7,10},{8,5},{9,4},... | collective-permute-start | bytes 1572872 | tf_op jit(solution)/shard_map/ppermute | solution.py:226
  172.0 0.7 collective-permute-start.14
  172.8 2.1 %place.5.rest_2_ = f32[2048,1024]{1,0:T(8,128)} custom-call(s32[16,128]{1,0:T(8,128)S(1)} %gather_fusion, f32[2,1024]{1,0:T(2,128)S(1)} %get-tuple-element.107.scale_ref, f32[128,1024]{1,0:T(8,128)} %copy-done.2, f32[128,1024]{1,0:T(8,128)} %copy-done.3, f32[2048,1024]{1,0:T(8,128)} %place.4.rest_2_), custom_call_target="tpu_custom_call", output_to_operand_aliasing={{}: (4, {})} | custom-call | flops 1048576 | bytes 2097152 | tf_op jit(solution)/shard_map/place/pallas_call | solution.py:174
  174.9 7.0 %collective-permute-done.16.rest_1_ = f32[128,1024]{1,0:T(8,128)S(1)} collective-permute-done((f32[128,1024]{1,0:T(8,128)}, f32[128,1024]{1,0:T(8,128)S(1)}, u32[]{:S(2)}, u32[]{:S(2)}) %collective-permute-start.16) | collective-permute-done | bytes 524320 | tf_op jit(solution)/shard_map/ppermute | solution.py:226
  181.9 1.3 place.6.rest_2_
  183.2 3.8 %collective-permute-done.12.rest_0_ = f32[128,1024]{1,0:T(8,128)S(1)} collective-permute-done((f32[128,1024]{1,0:T(8,128)S(1)}, f32[128,1024]{1,0:T(8,128)S(1)}, u32[]{:S(2)}, u32[]{:S(2)}) %collective-permute-start.12) | collective-permute-done | bytes 524320 | tf_op jit(solution)/shard_map/ppermute | solution.py:226
  187.0 1.3 place.7
  (69 shorter events, 1.0 us)
Async XLA Ops:
  0.6 7.1 %copy-start = (s32[16]{0:T(128)S(1)}, s32[16]{0:T(128)}, u32[]{:S(2)}) copy-start(s32[16]{0:T(128)} %dest_ref.2) | copy-start | bytes 196
  0.6 7.1 %copy-start.1 = (s32[16]{0:T(128)S(1)}, s32[16]{0:T(128)}, u32[]{:S(2)}) copy-start(s32[16]{0:T(128)} %slot_ref) | copy-start | bytes 196
  2.7 15.1 %collective-permute-start = (f32[128,1024]{1,0:T(8,128)S(1)}, f32[128,1024]{1,0:T(8,128)S(1)}, u32[]{:S(2)}, u32[]{:S(2)}) collective-permute-start(f32[128,1024]{1,0:T(8,128)S(1)} %get-tuple-element.58), channel_id=1, source_target_pairs={{0,4},{1,5},{2,6},{3,7},{4,0},{5,1},{6,2},{7,3},{8,12},{9,13},{10,... | collective-permute-start | bytes 1572872 | tf_op jit(solution)/shard_map/ppermute | solution.py:226
  2.8 44.2 %collective-permute-start.9 = (f32[128,1024]{1,0:T(8,128)S(1)}, f32[128,1024]{1,0:T(8,128)S(1)}, u32[]{:S(2)}, u32[]{:S(2)}) collective-permute-start(f32[128,1024]{1,0:T(8,128)S(1)} %get-tuple-element.78), channel_id=1, source_target_pairs={{0,8},{1,9},{2,10},{3,11},{4,12},{5,13},{6,14},{7,15},{8,0},{9,1},... | collective-permute-start | bytes 1572872 | tf_op jit(solution)/shard_map/ppermute | solution.py:226
  15.0 31.9 %collective-permute-start.3 = (f32[128,1024]{1,0:T(8,128)}, f32[128,1024]{1,0:T(8,128)S(1)}, u32[]{:S(2)}, u32[]{:S(2)}) collective-permute-start(f32[128,1024]{1,0:T(8,128)} %get-tuple-element.67), channel_id=1, source_target_pairs={{0,3},{1,2},{2,1},{3,0},{4,7},{5,6},{6,5},{7,4},{8,11},{9,10},{10,... | collective-permute-start | bytes 1572872 | tf_op jit(solution)/shard_map/ppermute | solution.py:226
  17.5 50.8 %collective-permute-start.6 = (f32[128,1024]{1,0:T(8,128)}, f32[128,1024]{1,0:T(8,128)S(1)}, u32[]{:S(2)}, u32[]{:S(2)}) collective-permute-start(f32[128,1024]{1,0:T(8,128)} %get-tuple-element.74), channel_id=1, source_target_pairs={{0,10},{1,11},{2,8},{3,9},{4,14},{5,15},{6,12},{7,13},{8,2},{9,3},... | collective-permute-start | bytes 1572872 | tf_op jit(solution)/shard_map/ppermute | solution.py:226
  17.8 146.5 %copy-start.4 = (f32[128,1024]{1,0:T(8,128)}, f32[128,1024]{1,0:T(8,128)S(1)}, u32[]{:S(2)}) copy-start(f32[128,1024]{1,0:T(8,128)S(1)} %collective-permute-done.rest_1_) | copy-start | bytes 1572868
  17.8 50.8 %collective-permute-start.1 = (f32[128,1024]{1,0:T(8,128)}, f32[128,1024]{1,0:T(8,128)S(1)}, u32[]{:S(2)}, u32[]{:S(2)}) collective-permute-start(f32[128,1024]{1,0:T(8,128)} %get-tuple-element.60), channel_id=1, source_target_pairs={{0,5},{1,4},{2,7},{3,6},{4,1},{5,0},{6,3},{7,2},{8,13},{9,12},{10,... | collective-permute-start | bytes 1572872 | tf_op jit(solution)/shard_map/ppermute | solution.py:226
  21.2 47.4 %all-to-all-start = ((f32[16,1,256]{2,1,0:T(1,128)}), f32[16,1,256]{2,1,0:T(1,128)S(1)}, u32[]{:S(2)}, u32[]{:S(2)}) async-start(f32[16,1,256]{2,1,0:T(1,128)} %get-tuple-element.61), calls=%async_computation | async-start | bytes 32768 | tf_op jit(solution)/shard_map/all_to_all | solution.py:250
  47.0 117.4 %copy-start.5 = (f32[128,1024]{1,0:T(8,128)}, f32[128,1024]{1,0:T(8,128)S(1)}, u32[]{:S(2)}) copy-start(f32[128,1024]{1,0:T(8,128)S(1)} %collective-permute-done.9.rest_0_) | copy-start | bytes 1572868
  47.0 39.7 %collective-permute-start.10 = (f32[128,1024]{1,0:T(8,128)}, f32[128,1024]{1,0:T(8,128)S(1)}, u32[]{:S(2)}, u32[]{:S(2)}) collective-permute-start(f32[128,1024]{1,0:T(8,128)} %get-tuple-element.84), channel_id=1, source_target_pairs={{0,12},{1,13},{2,14},{3,15},{4,8},{5,9},{6,10},{7,11},{8,4},{9,5},... | collective-permute-start | bytes 1572872 | tf_op jit(solution)/shard_map/ppermute | solution.py:226
  47.0 117.4 %copy-start.6 = (f32[128,1024]{1,0:T(8,128)}, f32[128,1024]{1,0:T(8,128)S(1)}, u32[]{:S(2)}) copy-start(f32[128,1024]{1,0:T(8,128)S(1)} %collective-permute-done.3.rest_3_) | copy-start | bytes 1572868
  47.0 64.0 %collective-permute-start.4 = (f32[128,1024]{1,0:T(8,128)}, f32[128,1024]{1,0:T(8,128)}, u32[]{:S(2)}, u32[]{:S(2)}) collective-permute-start(f32[128,1024]{1,0:T(8,128)} %get-tuple-element.68), channel_id=1, source_target_pairs={{0,7},{1,6},{2,5},{3,4},{4,3},{5,2},{6,1},{7,0},{8,15},{9,14},{10,... | collective-permute-start | bytes 1572872 | tf_op jit(solution)/shard_map/ppermute | solution.py:226
  68.3 42.5 %copy-start.7 = (f32[128,1024]{1,0:T(8,128)}, f32[128,1024]{1,0:T(8,128)S(1)}, u32[]{:S(2)}) copy-start(f32[128,1024]{1,0:T(8,128)S(1)} %collective-permute-done.6.rest_2_) | copy-start | bytes 1572868
  68.3 42.5 %collective-permute-start.7 = (f32[128,1024]{1,0:T(8,128)}, f32[128,1024]{1,0:T(8,128)}, u32[]{:S(2)}, u32[]{:S(2)}) collective-permute-start(f32[128,1024]{1,0:T(8,128)} %get-tuple-element.75), channel_id=1, source_target_pairs={{0,14},{1,15},{2,12},{3,13},{4,10},{5,11},{6,8},{7,9},{8,6},{9,7},... | collective-permute-start | bytes 1572872 | tf_op jit(solution)/shard_map/ppermute | solution.py:226
  68.6 42.2 %copy-start.8 = (f32[128,1024]{1,0:T(8,128)}, f32[128,1024]{1,0:T(8,128)S(1)}, u32[]{:S(2)}) copy-start(f32[128,1024]{1,0:T(8,128)S(1)} %collective-permute-done.1.rest_5_) | copy-start | bytes 1572868
  86.7 33.2 %copy-start.9 = (f32[128,1024]{1,0:T(8,128)}, f32[128,1024]{1,0:T(8,128)S(1)}, u32[]{:S(2)}) copy-start(f32[128,1024]{1,0:T(8,128)S(1)} %collective-permute-done.10.rest_4_) | copy-start | bytes 1572868
  86.7 24.1 %collective-permute-start.5 = (f32[2,64]{1,0:T(2,128)S(1)}, f32[2,64]{1,0:T(2,128)S(1)}, u32[]{:S(2)}, u32[]{:S(2)}) collective-permute-start(f32[2,64]{1,0:T(2,128)S(1)} %pad_maximum_fusion.2), channel_id=1, source_target_pairs={{0,16},{16,0},{1,17},{17,1},{2,18},{18,2},{3,19},{19,3},{4,20},{20... | collective-permute-start | bytes 1544 | tf_op jit(solution)/shard_map/ppermute | solution.py:202
  86.8 44.4 %collective-permute-start.11 = (f32[128,1024]{1,0:T(8,128)}, f32[128,1024]{1,0:T(8,128)}, u32[]{:S(2)}, u32[]{:S(2)}) collective-permute-start(f32[128,1024]{1,0:T(8,128)} %get-tuple-element.90), channel_id=1, source_target_pairs={{0,9},{1,8},{2,11},{3,10},{4,13},{5,12},{6,15},{7,14},{8,1},{9,0},... | collective-permute-start | bytes 1572872 | tf_op jit(solution)/shard_map/ppermute | solution.py:226
  86.9 74.8 %collective-permute-start.2 = (f32[128,1024]{1,0:T(8,128)}, f32[128,1024]{1,0:T(8,128)}, u32[]{:S(2)}, u32[]{:S(2)}) collective-permute-start(f32[128,1024]{1,0:T(8,128)} %get-tuple-element.64), channel_id=1, source_target_pairs={{0,2},{1,3},{2,0},{3,1},{4,6},{5,7},{6,4},{7,5},{8,10},{9,11},{10,... | collective-permute-start | bytes 1572872 | tf_op jit(solution)/shard_map/ppermute | solution.py:226
  110.8 58.8 %collective-permute-start.8 = (f32[128,1024]{1,0:T(8,128)}, f32[128,1024]{1,0:T(8,128)S(1)}, u32[]{:S(2)}, u32[]{:S(2)}) collective-permute-start(f32[128,1024]{1,0:T(8,128)} %get-tuple-element.76), channel_id=1, source_target_pairs={{0,11},{1,10},{2,9},{3,8},{4,15},{5,14},{6,13},{7,12},{8,3},{9,2},... | collective-permute-start | bytes 1572872 | tf_op jit(solution)/shard_map/ppermute | solution.py:226
  111.5 50.1 %all-to-all-start.1 = ((f32[16,1,128]{2,1,0:T(1,128)}), f32[16,1,128]{2,1,0:T(1,128)S(1)}, u32[]{:S(2)}, u32[]{:S(2)}) async-start(f32[16,1,128]{2,1,0:T(1,128)} %broadcast_in_dim.9), calls=%async_computation.1 | async-start | bytes 16384 | tf_op jit(solution)/shard_map/all_to_all | solution.py:254
  119.9 52.1 %collective-permute-start.13 = (f32[128,1024]{1,0:T(8,128)}, f32[128,1024]{1,0:T(8,128)S(1)}, u32[]{:S(2)}, u32[]{:S(2)}) collective-permute-start(f32[128,1024]{1,0:T(8,128)} %get-tuple-element.95), channel_id=1, source_target_pairs={{0,1},{1,0},{2,3},{3,2},{4,5},{5,4},{6,7},{7,6},{8,9},{9,8},{10,11... | collective-permute-start | bytes 1572872 | tf_op jit(solution)/shard_map/ppermute | solution.py:226
  131.2 43.7 %collective-permute-start.15 = (f32[128,1024]{1,0:T(8,128)}, f32[128,1024]{1,0:T(8,128)S(1)}, u32[]{:S(2)}, u32[]{:S(2)}) collective-permute-start(f32[128,1024]{1,0:T(8,128)} %get-tuple-element.97), channel_id=1, source_target_pairs={{0,15},{1,14},{2,13},{3,12},{4,11},{5,10},{6,9},{7,8},{8,7},{9,6},... | collective-permute-start | bytes 1572872 | tf_op jit(solution)/shard_map/ppermute | solution.py:226
  161.9 7.7 %copy-start.11 = (f32[128,1024]{1,0:T(8,128)S(1)}, f32[128,1024]{1,0:T(8,128)}, u32[]{:S(2)}) copy-start(f32[128,1024]{1,0:T(8,128)} %get-tuple-element.93) | copy-start | bytes 1572868
  161.9 10.1 %copy-start.10 = (f32[128,1024]{1,0:T(8,128)S(1)}, f32[128,1024]{1,0:T(8,128)}, u32[]{:S(2)}) copy-start(f32[128,1024]{1,0:T(8,128)} %get-tuple-element.96) | copy-start | bytes 1572868
  161.9 20.0 %collective-permute-start.16 = (f32[128,1024]{1,0:T(8,128)}, f32[128,1024]{1,0:T(8,128)S(1)}, u32[]{:S(2)}, u32[]{:S(2)}) collective-permute-start(f32[128,1024]{1,0:T(8,128)} %get-tuple-element.98), channel_id=1, source_target_pairs={{0,6},{1,7},{2,4},{3,5},{4,2},{5,3},{6,0},{7,1},{8,14},{9,15},{10,... | collective-permute-start | bytes 1572872 | tf_op jit(solution)/shard_map/ppermute | solution.py:226
  169.6 3.1 %copy-start.2 = (f32[128,1024]{1,0:T(8,128)}, f32[128,1024]{1,0:T(8,128)S(1)}, u32[]{:S(2)}) copy-start(f32[128,1024]{1,0:T(8,128)S(1)} %collective-permute-done.8.rest_0_) | copy-start | bytes 1572868
  169.7 17.4 %collective-permute-start.12 = (f32[128,1024]{1,0:T(8,128)S(1)}, f32[128,1024]{1,0:T(8,128)S(1)}, u32[]{:S(2)}, u32[]{:S(2)}) collective-permute-start(f32[128,1024]{1,0:T(8,128)S(1)} %copy-done.11), channel_id=1, source_target_pairs={{0,13},{1,12},{2,15},{3,14},{4,9},{5,8},{6,11},{7,10},{8,5},{9,4},... | collective-permute-start | bytes 1572872 | tf_op jit(solution)/shard_map/ppermute | solution.py:226
  172.0 0.8 copy-start.3
  172.0 15.0 %collective-permute-start.14 = (f32[128,1024]{1,0:T(8,128)S(1)}, f32[128,1024]{1,0:T(8,128)S(1)}, u32[]{:S(2)}, u32[]{:S(2)}) collective-permute-start(f32[128,1024]{1,0:T(8,128)S(1)} %copy-done.10), channel_id=1, source_target_pairs={{0,0},{1,1},{2,2},{3,3},{4,4},{5,5},{6,6},{7,7},{8,8},{9,9},{10,10... | collective-permute-start | bytes 1572872 | tf_op jit(solution)/shard_map/ppermute | solution.py:226

commit v7 on v6

--- a/solution.py
+++ b/solution.py
@@ -168,7 +168,7 @@
 
 def place(lanes, blocks, slots, scale, out, row_count, near_by):
     rows, feats = blocks[0].shape
-    count, parts = len(lanes), max(1, rows // 32)
+    count, parts = len(lanes), max(1, rows // 64)
     space, spec = (pltpu.VMEM, in_vmem) if near_by else (pltpu.HBM, in_hbm)
     args = [pin(slots, pltpu.VMEM), pin(scale, pltpu.VMEM)] + [pin(block, space) for block in blocks] + ([] if out is None else [pin(out)])
     return pl.pallas_call(

time: 189 us -> 189 us (level)
  no operation moved by 1% of the time
where the time goes in v7:
time: 189 us; the launch traced here: 188 us
  waiting for transfers between devices  124 us (66%)
  starting transfers between devices  41.8 us (22%)
  Pallas kernels  18.8 us (10%)
    ppermute x16, waiting for transfers between devices, send(): return lax.ppermute(block, ('outer', 'inner'), pairs)  95.2 us
    all_to_all x2, waiting for transfers between devices, body(): lax.all_to_all(extra[0], 'inner', split_axis=0, concat_axis=0, tiled=True)  29 us
    ppermute x16, starting transfers between devices, send(): return lax.ppermute(block, ('outer', 'inner'), pairs)  27.5 us
    all_to_all x2, starting transfers between devices, body(): lax.all_to_all(extra[0], 'inner', split_axis=0, concat_axis=0, tiled=True)  14.2 us
    pallas_call x4, Pallas kernels, place(): pl.pallas_call(functools.partial(place_kernel, lanes, near_by), out_shape...  9.44 us
    pallas_call x1, Pallas kernels, pick_rest(): pl.pallas_call(functools.partial(rest_kernel, lanes, first), out_shape=[j...  7.29 us
  transfers between devices with their start and end apart: 19, of which 9 were waited for; matrix products, arithmetic and copies ran while one was open for 1% of the time, Pallas kernels for 8%

profile of v7, /device:TPU:8, one launch (start us, length us, event | category | flops | bytes accessed | tf_op | source)
XLA Modules:
  0.0 188.3 jit_solution(49022900670284063)
XLA Ops:
  0.6 2.0 %pick_first.1 = (f32[128,1024]{1,0:T(8,128)S(1)}, f32[128,1024]{1,0:T(8,128)S(1)}) custom-call(s32[16]{0:T(128)} %dest_ref.2, f32[2048,1024]{1,0:T(8,128)} %features_ref.3), custom_call_target="tpu_custom_call" | custom-call | tf_op jit(solution)/shard_map/pick_first/pallas_call | solution.py:77
  2.8 4.9 %collective-permute-start.9 = (f32[128,1024]{1,0:T(8,128)S(1)}, f32[128,1024]{1,0:T(8,128)S(1)}, u32[]{:S(2)}, u32[]{:S(2)}) collective-permute-start(f32[128,1024]{1,0:T(8,128)S(1)} %get-tuple-element.78), channel_id=1, source_target_pairs={{0,8},{1,9},{2,10},{3,11},{4,12},{5,13},{6,14},{7,15},{8,0},{9,1},... | collective-permute-start | bytes 1572872 | tf_op jit(solution)/shard_map/ppermute | solution.py:226
  7.7 7.3 %pick_rest.1 = (f32[16,1,256]{2,1,0:T(1,128)}, f32[128,1024]{1,0:T(8,128)}, f32[128,1024]{1,0:T(8,128)}, f32[128,1024]{1,0:T(8,128)}, f32[128,1024]{1,0:T(8,128)...) custom-call(s32[16]{0:T(128)S(1)} %copy-done, ...), custom_call_target="tpu_custom_call" | custom-call | flops 12582912 | bytes 16777216 | tf_op jit(solution)/shard_map/pick_rest/pallas_call | solution.py:127
  15.0 2.5 %collective-permute-start.3 = (f32[128,1024]{1,0:T(8,128)}, f32[128,1024]{1,0:T(8,128)S(1)}, u32[]{:S(2)}, u32[]{:S(2)}) collective-permute-start(f32[128,1024]{1,0:T(8,128)} %get-tuple-element.67), channel_id=1, source_target_pairs={{0,3},{1,2},{2,1},{3,0},{4,7},{5,6},{6,5},{7,4},{8,11},{9,10},{10,... | collective-permute-start | bytes 1572872 | tf_op jit(solution)/shard_map/ppermute | solution.py:226
  17.5 0.3 collective-permute-start.6
  17.8 3.4 %collective-permute-start.1 = (f32[128,1024]{1,0:T(8,128)}, f32[128,1024]{1,0:T(8,128)S(1)}, u32[]{:S(2)}, u32[]{:S(2)}) collective-permute-start(f32[128,1024]{1,0:T(8,128)} %get-tuple-element.60), channel_id=1, source_target_pairs={{0,5},{1,4},{2,7},{3,6},{4,1},{5,0},{6,3},{7,2},{8,13},{9,12},{10,... | collective-permute-start | bytes 1572872 | tf_op jit(solution)/shard_map/ppermute | solution.py:226
  21.2 5.9 %all-to-all-start = ((f32[16,1,256]{2,1,0:T(1,128)}), f32[16,1,256]{2,1,0:T(1,128)S(1)}, u32[]{:S(2)}, u32[]{:S(2)}) async-start(f32[16,1,256]{2,1,0:T(1,128)} %get-tuple-element.61), calls=%async_computation | async-start | bytes 32768 | tf_op jit(solution)/shard_map/all_to_all | solution.py:250
  27.1 19.9 %collective-permute-done.9.rest_0_ = f32[128,1024]{1,0:T(8,128)S(1)} collective-permute-done((f32[128,1024]{1,0:T(8,128)S(1)}, f32[128,1024]{1,0:T(8,128)S(1)}, u32[]{:S(2)}, u32[]{:S(2)}) %collective-permute-start.9) | collective-permute-done | bytes 524320 | tf_op jit(solution)/shard_map/ppermute | solution.py:226
  47.0 6.7 %collective-permute-start.4 = (f32[128,1024]{1,0:T(8,128)}, f32[128,1024]{1,0:T(8,128)}, u32[]{:S(2)}, u32[]{:S(2)}) collective-permute-start(f32[128,1024]{1,0:T(8,128)} %get-tuple-element.68), channel_id=1, source_target_pairs={{0,7},{1,6},{2,5},{3,4},{4,3},{5,2},{6,1},{7,0},{8,15},{9,14},{10,... | collective-permute-start | bytes 1572872 | tf_op jit(solution)/shard_map/ppermute | solution.py:226
  53.7 14.6 %collective-permute-done.6.rest_2_ = f32[128,1024]{1,0:T(8,128)S(1)} collective-permute-done((f32[128,1024]{1,0:T(8,128)}, f32[128,1024]{1,0:T(8,128)S(1)}, u32[]{:S(2)}, u32[]{:S(2)}) %collective-permute-start.6) | collective-permute-done | bytes 524320 | tf_op jit(solution)/shard_map/ppermute | solution.py:226
  68.3 0.2 all-to-all-done
  69.0 17.7 %collective-permute-done.10.rest_4_ = f32[128,1024]{1,0:T(8,128)S(1)} collective-permute-done((f32[128,1024]{1,0:T(8,128)}, f32[128,1024]{1,0:T(8,128)S(1)}, u32[]{:S(2)}, u32[]{:S(2)}) %collective-permute-start.10) | collective-permute-done | bytes 524320 | tf_op jit(solution)/shard_map/ppermute | solution.py:226
  86.9 1.6 collective-permute-start.2
  88.4 22.4 %collective-permute-done.7.rest_6_ = f32[128,1024]{1,0:T(8,128)} collective-permute-done((f32[128,1024]{1,0:T(8,128)}, f32[128,1024]{1,0:T(8,128)}, u32[]{:S(2)}, u32[]{:S(2)}) %collective-permute-start.7) | collective-permute-done | bytes 524320 | tf_op jit(solution)/shard_map/ppermute | solution.py:226
  110.9 0.6 broadcast_in_dim.9
  111.5 8.3 %all-to-all-start.1 = ((f32[16,1,128]{2,1,0:T(1,128)}), f32[16,1,128]{2,1,0:T(1,128)S(1)}, u32[]{:S(2)}, u32[]{:S(2)}) async-start(f32[16,1,128]{2,1,0:T(1,128)} %broadcast_in_dim.9), calls=%async_computation.1 | async-start | bytes 16384 | tf_op jit(solution)/shard_map/all_to_all | solution.py:254
  119.9 1.5 collective-permute-start.13
  121.4 0.6 gather_fusion
  122.0 9.2 %collective-permute-done.11.rest_8_ = f32[128,1024]{1,0:T(8,128)} collective-permute-done((f32[128,1024]{1,0:T(8,128)}, f32[128,1024]{1,0:T(8,128)}, u32[]{:S(2)}, u32[]{:S(2)}) %collective-permute-start.11) | collective-permute-done | bytes 524320 | tf_op jit(solution)/shard_map/ppermute | solution.py:226
  131.2 1.7 collective-permute-start.15
  132.9 28.8 %all-to-all-done.1 = f32[16,1,128]{2,1,0:T(1,128)S(1)} async-done(((f32[16,1,128]{2,1,0:T(1,128)}), f32[16,1,128]{2,1,0:T(1,128)S(1)}, u32[]{:S(2)}, u32[]{:S(2)}) %all-to-all-start.1) | async-done | bytes 8224 | tf_op jit(solution)/shard_map/all_to_all | solution.py:254
  161.7 0.1 multiply_reduce_fusion
  161.9 1.7 collective-permute-start.16
  163.7 0.6 pad_maximum_fusion
  164.3 5.0 %place.4.rest_2_ = f32[2048,1024]{1,0:T(8,128)} custom-call(s32[16,128]{1,0:T(8,128)S(1)} %gather_fusion, f32[2,1024]{1,0:T(2,128)S(1)} %get-tuple-element.107.scale_ref, f32[128,1024]{1,0:T(8,128)} %copy-done.5, f32[128,1024]{1,0:T(8,128)} %copy-done.4, f32[128,1024]{1,0:T(8,128)} %copy-done.7, f32[128,1024]{1,0:T(8,128)} %copy-done.6, ...), custom_call_target="tpu_custom_call" | custom-call | flops 5242880 | bytes 10485760 | tf_op jit(solution)/shard_map/place/pallas_call | solution.py:174
  169.3 2.3 %collective-permute-start.12 = (f32[128,1024]{1,0:T(8,128)S(1)}, f32[128,1024]{1,0:T(8,128)S(1)}, u32[]{:S(2)}, u32[]{:S(2)}) collective-permute-start(f32[128,1024]{1,0:T(8,128)S(1)} %copy-done.11), channel_id=1, source_target_pairs={{0,13},{1,12},{2,15},{3,14},{4,9},{5,8},{6,11},{7,10},{8,5},{9,4},... | collective-permute-start | bytes 1572872 | tf_op jit(solution)/shard_map/ppermute | solution.py:226
  171.7 0.7 collective-permute-start.14
  172.5 2.0 %place.5.rest_2_ = f32[2048,1024]{1,0:T(8,128)} custom-call(s32[16,128]{1,0:T(8,128)S(1)} %gather_fusion, f32[2,1024]{1,0:T(2,128)S(1)} %get-tuple-element.107.scale_ref, f32[128,1024]{1,0:T(8,128)} %copy-done.2, f32[128,1024]{1,0:T(8,128)} %copy-done.3, f32[2048,1024]{1,0:T(8,128)} %place.4.rest_2_), custom_call_target="tpu_custom_call", output_to_operand_aliasing={{}: (4, {})} | custom-call | flops 1048576 | bytes 2097152 | tf_op jit(solution)/shard_map/place/pallas_call | solution.py:174
  174.5 7.4 %collective-permute-done.16.rest_1_ = f32[128,1024]{1,0:T(8,128)S(1)} collective-permute-done((f32[128,1024]{1,0:T(8,128)}, f32[128,1024]{1,0:T(8,128)S(1)}, u32[]{:S(2)}, u32[]{:S(2)}) %collective-permute-start.16) | collective-permute-done | bytes 524320 | tf_op jit(solution)/shard_map/ppermute | solution.py:226
  181.9 1.2 place.6.rest_2_
  183.2 3.8 %collective-permute-done.12.rest_0_ = f32[128,1024]{1,0:T(8,128)S(1)} collective-permute-done((f32[128,1024]{1,0:T(8,128)S(1)}, f32[128,1024]{1,0:T(8,128)S(1)}, u32[]{:S(2)}, u32[]{:S(2)}) %collective-permute-start.12) | collective-permute-done | bytes 524320 | tf_op jit(solution)/shard_map/ppermute | solution.py:226
  187.0 1.2 place.7
  (69 shorter events, 1.0 us)
Async XLA Ops:
  0.6 7.1 %copy-start = (s32[16]{0:T(128)S(1)}, s32[16]{0:T(128)}, u32[]{:S(2)}) copy-start(s32[16]{0:T(128)} %dest_ref.2) | copy-start | bytes 196
  0.6 7.1 %copy-start.1 = (s32[16]{0:T(128)S(1)}, s32[16]{0:T(128)}, u32[]{:S(2)}) copy-start(s32[16]{0:T(128)} %slot_ref) | copy-start | bytes 196
  2.7 15.1 %collective-permute-start = (f32[128,1024]{1,0:T(8,128)S(1)}, f32[128,1024]{1,0:T(8,128)S(1)}, u32[]{:S(2)}, u32[]{:S(2)}) collective-permute-start(f32[128,1024]{1,0:T(8,128)S(1)} %get-tuple-element.58), channel_id=1, source_target_pairs={{0,4},{1,5},{2,6},{3,7},{4,0},{5,1},{6,2},{7,3},{8,12},{9,13},{10,... | collective-permute-start | bytes 1572872 | tf_op jit(solution)/shard_map/ppermute | solution.py:226
  2.8 44.2 %collective-permute-start.9 = (f32[128,1024]{1,0:T(8,128)S(1)}, f32[128,1024]{1,0:T(8,128)S(1)}, u32[]{:S(2)}, u32[]{:S(2)}) collective-permute-start(f32[128,1024]{1,0:T(8,128)S(1)} %get-tuple-element.78), channel_id=1, source_target_pairs={{0,8},{1,9},{2,10},{3,11},{4,12},{5,13},{6,14},{7,15},{8,0},{9,1},... | collective-permute-start | bytes 1572872 | tf_op jit(solution)/shard_map/ppermute | solution.py:226
  15.0 31.9 %collective-permute-start.3 = (f32[128,1024]{1,0:T(8,128)}, f32[128,1024]{1,0:T(8,128)S(1)}, u32[]{:S(2)}, u32[]{:S(2)}) collective-permute-start(f32[128,1024]{1,0:T(8,128)} %get-tuple-element.67), channel_id=1, source_target_pairs={{0,3},{1,2},{2,1},{3,0},{4,7},{5,6},{6,5},{7,4},{8,11},{9,10},{10,... | collective-permute-start | bytes 1572872 | tf_op jit(solution)/shard_map/ppermute | solution.py:226
  17.5 50.8 %collective-permute-start.6 = (f32[128,1024]{1,0:T(8,128)}, f32[128,1024]{1,0:T(8,128)S(1)}, u32[]{:S(2)}, u32[]{:S(2)}) collective-permute-start(f32[128,1024]{1,0:T(8,128)} %get-tuple-element.74), channel_id=1, source_target_pairs={{0,10},{1,11},{2,8},{3,9},{4,14},{5,15},{6,12},{7,13},{8,2},{9,3},... | collective-permute-start | bytes 1572872 | tf_op jit(solution)/shard_map/ppermute | solution.py:226
  17.8 146.5 %copy-start.4 = (f32[128,1024]{1,0:T(8,128)}, f32[128,1024]{1,0:T(8,128)S(1)}, u32[]{:S(2)}) copy-start(f32[128,1024]{1,0:T(8,128)S(1)} %collective-permute-done.rest_1_) | copy-start | bytes 1572868
  17.8 50.8 %collective-permute-start.1 = (f32[128,1024]{1,0:T(8,128)}, f32[128,1024]{1,0:T(8,128)S(1)}, u32[]{:S(2)}, u32[]{:S(2)}) collective-permute-start(f32[128,1024]{1,0:T(8,128)} %get-tuple-element.60), channel_id=1, source_target_pairs={{0,5},{1,4},{2,7},{3,6},{4,1},{5,0},{6,3},{7,2},{8,13},{9,12},{10,... | collective-permute-start | bytes 1572872 | tf_op jit(solution)/shard_map/ppermute | solution.py:226
  21.2 47.4 %all-to-all-start = ((f32[16,1,256]{2,1,0:T(1,128)}), f32[16,1,256]{2,1,0:T(1,128)S(1)}, u32[]{:S(2)}, u32[]{:S(2)}) async-start(f32[16,1,256]{2,1,0:T(1,128)} %get-tuple-element.61), calls=%async_computation | async-start | bytes 32768 | tf_op jit(solution)/shard_map/all_to_all | solution.py:250
  47.0 117.4 %copy-start.5 = (f32[128,1024]{1,0:T(8,128)}, f32[128,1024]{1,0:T(8,128)S(1)}, u32[]{:S(2)}) copy-start(f32[128,1024]{1,0:T(8,128)S(1)} %collective-permute-done.9.rest_0_) | copy-start | bytes 1572868
  47.0 39.7 %collective-permute-start.10 = (f32[128,1024]{1,0:T(8,128)}, f32[128,1024]{1,0:T(8,128)S(1)}, u32[]{:S(2)}, u32[]{:S(2)}) collective-permute-start(f32[128,1024]{1,0:T(8,128)} %get-tuple-element.84), channel_id=1, source_target_pairs={{0,12},{1,13},{2,14},{3,15},{4,8},{5,9},{6,10},{7,11},{8,4},{9,5},... | collective-permute-start | bytes 1572872 | tf_op jit(solution)/shard_map/ppermute | solution.py:226
  47.0 117.4 %copy-start.6 = (f32[128,1024]{1,0:T(8,128)}, f32[128,1024]{1,0:T(8,128)S(1)}, u32[]{:S(2)}) copy-start(f32[128,1024]{1,0:T(8,128)S(1)} %collective-permute-done.3.rest_3_) | copy-start | bytes 1572868
  47.0 64.0 %collective-permute-start.4 = (f32[128,1024]{1,0:T(8,128)}, f32[128,1024]{1,0:T(8,128)}, u32[]{:S(2)}, u32[]{:S(2)}) collective-permute-start(f32[128,1024]{1,0:T(8,128)} %get-tuple-element.68), channel_id=1, source_target_pairs={{0,7},{1,6},{2,5},{3,4},{4,3},{5,2},{6,1},{7,0},{8,15},{9,14},{10,... | collective-permute-start | bytes 1572872 | tf_op jit(solution)/shard_map/ppermute | solution.py:226
  68.3 42.5 %copy-start.7 = (f32[128,1024]{1,0:T(8,128)}, f32[128,1024]{1,0:T(8,128)S(1)}, u32[]{:S(2)}) copy-start(f32[128,1024]{1,0:T(8,128)S(1)} %collective-permute-done.6.rest_2_) | copy-start | bytes 1572868
  68.3 42.5 %collective-permute-start.7 = (f32[128,1024]{1,0:T(8,128)}, f32[128,1024]{1,0:T(8,128)}, u32[]{:S(2)}, u32[]{:S(2)}) collective-permute-start(f32[128,1024]{1,0:T(8,128)} %get-tuple-element.75), channel_id=1, source_target_pairs={{0,14},{1,15},{2,12},{3,13},{4,10},{5,11},{6,8},{7,9},{8,6},{9,7},... | collective-permute-start | bytes 1572872 | tf_op jit(solution)/shard_map/ppermute | solution.py:226
  68.6 42.2 %copy-start.8 = (f32[128,1024]{1,0:T(8,128)}, f32[128,1024]{1,0:T(8,128)S(1)}, u32[]{:S(2)}) copy-start(f32[128,1024]{1,0:T(8,128)S(1)} %collective-permute-done.1.rest_5_) | copy-start | bytes 1572868
  86.7 33.2 %copy-start.9 = (f32[128,1024]{1,0:T(8,128)}, f32[128,1024]{1,0:T(8,128)S(1)}, u32[]{:S(2)}) copy-start(f32[128,1024]{1,0:T(8,128)S(1)} %collective-permute-done.10.rest_4_) | copy-start | bytes 1572868
  86.7 24.1 %collective-permute-start.5 = (f32[2,64]{1,0:T(2,128)S(1)}, f32[2,64]{1,0:T(2,128)S(1)}, u32[]{:S(2)}, u32[]{:S(2)}) collective-permute-start(f32[2,64]{1,0:T(2,128)S(1)} %pad_maximum_fusion.2), channel_id=1, source_target_pairs={{0,16},{16,0},{1,17},{17,1},{2,18},{18,2},{3,19},{19,3},{4,20},{20... | collective-permute-start | bytes 1544 | tf_op jit(solution)/shard_map/ppermute | solution.py:202
  86.8 44.4 %collective-permute-start.11 = (f32[128,1024]{1,0:T(8,128)}, f32[128,1024]{1,0:T(8,128)}, u32[]{:S(2)}, u32[]{:S(2)}) collective-permute-start(f32[128,1024]{1,0:T(8,128)} %get-tuple-element.90), channel_id=1, source_target_pairs={{0,9},{1,8},{2,11},{3,10},{4,13},{5,12},{6,15},{7,14},{8,1},{9,0},... | collective-permute-start | bytes 1572872 | tf_op jit(solution)/shard_map/ppermute | solution.py:226
  86.9 74.8 %collective-permute-start.2 = (f32[128,1024]{1,0:T(8,128)}, f32[128,1024]{1,0:T(8,128)}, u32[]{:S(2)}, u32[]{:S(2)}) collective-permute-start(f32[128,1024]{1,0:T(8,128)} %get-tuple-element.64), channel_id=1, source_target_pairs={{0,2},{1,3},{2,0},{3,1},{4,6},{5,7},{6,4},{7,5},{8,10},{9,11},{10,... | collective-permute-start | bytes 1572872 | tf_op jit(solution)/shard_map/ppermute | solution.py:226
  110.8 58.5 %collective-permute-start.8 = (f32[128,1024]{1,0:T(8,128)}, f32[128,1024]{1,0:T(8,128)S(1)}, u32[]{:S(2)}, u32[]{:S(2)}) collective-permute-start(f32[128,1024]{1,0:T(8,128)} %get-tuple-element.76), channel_id=1, source_target_pairs={{0,11},{1,10},{2,9},{3,8},{4,15},{5,14},{6,13},{7,12},{8,3},{9,2},... | collective-permute-start | bytes 1572872 | tf_op jit(solution)/shard_map/ppermute | solution.py:226
  111.5 50.1 %all-to-all-start.1 = ((f32[16,1,128]{2,1,0:T(1,128)}), f32[16,1,128]{2,1,0:T(1,128)S(1)}, u32[]{:S(2)}, u32[]{:S(2)}) async-start(f32[16,1,128]{2,1,0:T(1,128)} %broadcast_in_dim.9), calls=%async_computation.1 | async-start | bytes 16384 | tf_op jit(solution)/shard_map/all_to_all | solution.py:254
  119.9 51.8 %collective-permute-start.13 = (f32[128,1024]{1,0:T(8,128)}, f32[128,1024]{1,0:T(8,128)S(1)}, u32[]{:S(2)}, u32[]{:S(2)}) collective-permute-start(f32[128,1024]{1,0:T(8,128)} %get-tuple-element.95), channel_id=1, source_target_pairs={{0,1},{1,0},{2,3},{3,2},{4,5},{5,4},{6,7},{7,6},{8,9},{9,8},{10,11... | collective-permute-start | bytes 1572872 | tf_op jit(solution)/shard_map/ppermute | solution.py:226
  131.2 43.3 %collective-permute-start.15 = (f32[128,1024]{1,0:T(8,128)}, f32[128,1024]{1,0:T(8,128)S(1)}, u32[]{:S(2)}, u32[]{:S(2)}) collective-permute-start(f32[128,1024]{1,0:T(8,128)} %get-tuple-element.97), channel_id=1, source_target_pairs={{0,15},{1,14},{2,13},{3,12},{4,11},{5,10},{6,9},{7,8},{8,7},{9,6},... | collective-permute-start | bytes 1572872 | tf_op jit(solution)/shard_map/ppermute | solution.py:226
  161.9 7.4 %copy-start.11 = (f32[128,1024]{1,0:T(8,128)S(1)}, f32[128,1024]{1,0:T(8,128)}, u32[]{:S(2)}) copy-start(f32[128,1024]{1,0:T(8,128)} %get-tuple-element.93) | copy-start | bytes 1572868
  161.9 9.8 %copy-start.10 = (f32[128,1024]{1,0:T(8,128)S(1)}, f32[128,1024]{1,0:T(8,128)}, u32[]{:S(2)}) copy-start(f32[128,1024]{1,0:T(8,128)} %get-tuple-element.96) | copy-start | bytes 1572868
  161.9 20.0 %collective-permute-start.16 = (f32[128,1024]{1,0:T(8,128)}, f32[128,1024]{1,0:T(8,128)S(1)}, u32[]{:S(2)}, u32[]{:S(2)}) collective-permute-start(f32[128,1024]{1,0:T(8,128)} %get-tuple-element.98), channel_id=1, source_target_pairs={{0,6},{1,7},{2,4},{3,5},{4,2},{5,3},{6,0},{7,1},{8,14},{9,15},{10,... | collective-permute-start | bytes 1572872 | tf_op jit(solution)/shard_map/ppermute | solution.py:226
  169.3 3.1 %copy-start.2 = (f32[128,1024]{1,0:T(8,128)}, f32[128,1024]{1,0:T(8,128)S(1)}, u32[]{:S(2)}) copy-start(f32[128,1024]{1,0:T(8,128)S(1)} %collective-permute-done.8.rest_0_) | copy-start | bytes 1572868
  169.3 17.7 %collective-permute-start.12 = (f32[128,1024]{1,0:T(8,128)S(1)}, f32[128,1024]{1,0:T(8,128)S(1)}, u32[]{:S(2)}, u32[]{:S(2)}) collective-permute-start(f32[128,1024]{1,0:T(8,128)S(1)} %copy-done.11), channel_id=1, source_target_pairs={{0,13},{1,12},{2,15},{3,14},{4,9},{5,8},{6,11},{7,10},{8,5},{9,4},... | collective-permute-start | bytes 1572872 | tf_op jit(solution)/shard_map/ppermute | solution.py:226
  171.7 0.8 copy-start.3
  171.7 15.3 %collective-permute-start.14 = (f32[128,1024]{1,0:T(8,128)S(1)}, f32[128,1024]{1,0:T(8,128)S(1)}, u32[]{:S(2)}, u32[]{:S(2)}) collective-permute-start(f32[128,1024]{1,0:T(8,128)S(1)} %copy-done.10), channel_id=1, source_target_pairs={{0,0},{1,1},{2,2},{3,3},{4,4},{5,5},{6,6},{7,7},{8,8},{9,9},{10,10... | collective-permute-start | bytes 1572872 | tf_op jit(solution)/shard_map/ppermute | solution.py:226

commit v8 on v7

--- a/solution.py
+++ b/solution.py
@@ -136,7 +136,6 @@
             pltpu.SemaphoreType.DMA((len(lanes),)),
         ],
         compiler_params=pltpu.CompilerParams(vmem_limit_bytes=32 * 1024 * 1024),
-        cost_estimate=pl.CostEstimate(flops=6 * features.size, bytes_accessed=8 * features.size, transcendentals=0),
         name="pick_rest",
     )(dest, slot, pin(features))
     return res[0], res[1:]

time: 189 us -> 189 us (level)
  no operation moved by 1% of the time
where the time goes in v8:
time: 189 us; the launch traced here: 188 us
  waiting for transfers between devices  124 us (66%)
  starting transfers between devices  41.8 us (22%)
  Pallas kernels  18.8 us (10%)
    ppermute x16, waiting for transfers between devices, send(): return lax.ppermute(block, ('outer', 'inner'), pairs)  95.2 us
    all_to_all x2, waiting for transfers between devices, body(): lax.all_to_all(extra[0], 'inner', split_axis=0, concat_axis=0, tiled=True)  29 us
    ppermute x16, starting transfers between devices, send(): return lax.ppermute(block, ('outer', 'inner'), pairs)  27.5 us
    all_to_all x2, starting transfers between devices, body(): lax.all_to_all(extra[0], 'inner', split_axis=0, concat_axis=0, tiled=True)  14.2 us
    pallas_call x4, Pallas kernels, place(): pl.pallas_call(functools.partial(place_kernel, lanes, near_by), out_shape...  9.44 us
    pallas_call x1, Pallas kernels, pick_rest(): pl.pallas_call(functools.partial(rest_kernel, lanes, first), out_shape=[j...  7.29 us
  transfers between devices with their start and end apart: 19, of which 9 were waited for; matrix products, arithmetic and copies ran while one was open for 1% of the time, Pallas kernels for 8%

profile of v8, /device:TPU:8, one launch (start us, length us, event | category | flops | bytes accessed | tf_op | source)
XLA Modules:
  0.0 188.3 jit_solution(49022900670284063)
XLA Ops:
  0.6 2.0 %pick_first.1 = (f32[128,1024]{1,0:T(8,128)S(1)}, f32[128,1024]{1,0:T(8,128)S(1)}) custom-call(s32[16]{0:T(128)} %dest_ref.2, f32[2048,1024]{1,0:T(8,128)} %features_ref.3), custom_call_target="tpu_custom_call" | custom-call | tf_op jit(solution)/shard_map/pick_first/pallas_call | solution.py:77
  2.8 4.9 %collective-permute-start.9 = (f32[128,1024]{1,0:T(8,128)S(1)}, f32[128,1024]{1,0:T(8,128)S(1)}, u32[]{:S(2)}, u32[]{:S(2)}) collective-permute-start(f32[128,1024]{1,0:T(8,128)S(1)} %get-tuple-element.78), channel_id=1, source_target_pairs={{0,8},{1,9},{2,10},{3,11},{4,12},{5,13},{6,14},{7,15},{8,0},{9,1},... | collective-permute-start | bytes 1572872 | tf_op jit(solution)/shard_map/ppermute | solution.py:225
  7.7 7.3 %pick_rest.1 = (f32[16,1,256]{2,1,0:T(1,128)}, f32[128,1024]{1,0:T(8,128)}, f32[128,1024]{1,0:T(8,128)}, f32[128,1024]{1,0:T(8,128)}, f32[128,1024]{1,0:T(8,128)...) custom-call(s32[16]{0:T(128)S(1)} %copy-done, ...), custom_call_target="tpu_custom_call" | custom-call | tf_op jit(solution)/shard_map/pick_rest/pallas_call | solution.py:127
  15.0 2.5 %collective-permute-start.3 = (f32[128,1024]{1,0:T(8,128)}, f32[128,1024]{1,0:T(8,128)S(1)}, u32[]{:S(2)}, u32[]{:S(2)}) collective-permute-start(f32[128,1024]{1,0:T(8,128)} %get-tuple-element.67), channel_id=1, source_target_pairs={{0,3},{1,2},{2,1},{3,0},{4,7},{5,6},{6,5},{7,4},{8,11},{9,10},{10,... | collective-permute-start | bytes 1572872 | tf_op jit(solution)/shard_map/ppermute | solution.py:225
  17.5 0.3 collective-permute-start.6
  17.8 3.4 %collective-permute-start.1 = (f32[128,1024]{1,0:T(8,128)}, f32[128,1024]{1,0:T(8,128)S(1)}, u32[]{:S(2)}, u32[]{:S(2)}) collective-permute-start(f32[128,1024]{1,0:T(8,128)} %get-tuple-element.60), channel_id=1, source_target_pairs={{0,5},{1,4},{2,7},{3,6},{4,1},{5,0},{6,3},{7,2},{8,13},{9,12},{10,... | collective-permute-start | bytes 1572872 | tf_op jit(solution)/shard_map/ppermute | solution.py:225
  21.2 5.9 %all-to-all-start = ((f32[16,1,256]{2,1,0:T(1,128)}), f32[16,1,256]{2,1,0:T(1,128)S(1)}, u32[]{:S(2)}, u32[]{:S(2)}) async-start(f32[16,1,256]{2,1,0:T(1,128)} %get-tuple-element.61), calls=%async_computation | async-start | bytes 32768 | tf_op jit(solution)/shard_map/all_to_all | solution.py:249
  27.1 19.9 %collective-permute-done.9.rest_0_ = f32[128,1024]{1,0:T(8,128)S(1)} collective-permute-done((f32[128,1024]{1,0:T(8,128)S(1)}, f32[128,1024]{1,0:T(8,128)S(1)}, u32[]{:S(2)}, u32[]{:S(2)}) %collective-permute-start.9) | collective-permute-done | bytes 524320 | tf_op jit(solution)/shard_map/ppermute | solution.py:225
  47.0 6.7 %collective-permute-start.4 = (f32[128,1024]{1,0:T(8,128)}, f32[128,1024]{1,0:T(8,128)}, u32[]{:S(2)}, u32[]{:S(2)}) collective-permute-start(f32[128,1024]{1,0:T(8,128)} %get-tuple-element.68), channel_id=1, source_target_pairs={{0,7},{1,6},{2,5},{3,4},{4,3},{5,2},{6,1},{7,0},{8,15},{9,14},{10,... | collective-permute-start | bytes 1572872 | tf_op jit(solution)/shard_map/ppermute | solution.py:225
  53.7 14.6 %collective-permute-done.6.rest_2_ = f32[128,1024]{1,0:T(8,128)S(1)} collective-permute-done((f32[128,1024]{1,0:T(8,128)}, f32[128,1024]{1,0:T(8,128)S(1)}, u32[]{:S(2)}, u32[]{:S(2)}) %collective-permute-start.6) | collective-permute-done | bytes 524320 | tf_op jit(solution)/shard_map/ppermute | solution.py:225
  68.3 0.2 all-to-all-done
  69.0 17.7 %collective-permute-done.10.rest_4_ = f32[128,1024]{1,0:T(8,128)S(1)} collective-permute-done((f32[128,1024]{1,0:T(8,128)}, f32[128,1024]{1,0:T(8,128)S(1)}, u32[]{:S(2)}, u32[]{:S(2)}) %collective-permute-start.10) | collective-permute-done | bytes 524320 | tf_op jit(solution)/shard_map/ppermute | solution.py:225
  86.9 1.6 collective-permute-start.2
  88.4 22.4 %collective-permute-done.7.rest_6_ = f32[128,1024]{1,0:T(8,128)} collective-permute-done((f32[128,1024]{1,0:T(8,128)}, f32[128,1024]{1,0:T(8,128)}, u32[]{:S(2)}, u32[]{:S(2)}) %collective-permute-start.7) | collective-permute-done | bytes 524320 | tf_op jit(solution)/shard_map/ppermute | solution.py:225
  110.9 0.6 broadcast_in_dim.9
  111.5 8.3 %all-to-all-start.1 = ((f32[16,1,128]{2,1,0:T(1,128)}), f32[16,1,128]{2,1,0:T(1,128)S(1)}, u32[]{:S(2)}, u32[]{:S(2)}) async-start(f32[16,1,128]{2,1,0:T(1,128)} %broadcast_in_dim.9), calls=%async_computation.1 | async-start | bytes 16384 | tf_op jit(solution)/shard_map/all_to_all | solution.py:253
  119.9 1.5 collective-permute-start.13
  121.4 0.6 gather_fusion
  122.0 9.2 %collective-permute-done.11.rest_8_ = f32[128,1024]{1,0:T(8,128)} collective-permute-done((f32[128,1024]{1,0:T(8,128)}, f32[128,1024]{1,0:T(8,128)}, u32[]{:S(2)}, u32[]{:S(2)}) %collective-permute-start.11) | collective-permute-done | bytes 524320 | tf_op jit(solution)/shard_map/ppermute | solution.py:225
  131.2 1.7 collective-permute-start.15
  132.9 28.8 %all-to-all-done.1 = f32[16,1,128]{2,1,0:T(1,128)S(1)} async-done(((f32[16,1,128]{2,1,0:T(1,128)}), f32[16,1,128]{2,1,0:T(1,128)S(1)}, u32[]{:S(2)}, u32[]{:S(2)}) %all-to-all-start.1) | async-done | bytes 8224 | tf_op jit(solution)/shard_map/all_to_all | solution.py:253
  161.7 0.1 multiply_reduce_fusion
  161.9 1.7 collective-permute-start.16
  163.7 0.6 pad_maximum_fusion
  164.3 5.0 %place.4.rest_2_ = f32[2048,1024]{1,0:T(8,128)} custom-call(s32[16,128]{1,0:T(8,128)S(1)} %gather_fusion, f32[2,1024]{1,0:T(2,128)S(1)} %get-tuple-element.107.scale_ref, f32[128,1024]{1,0:T(8,128)} %copy-done.5, f32[128,1024]{1,0:T(8,128)} %copy-done.4, f32[128,1024]{1,0:T(8,128)} %copy-done.7, f32[128,1024]{1,0:T(8,128)} %copy-done.6, ...), custom_call_target="tpu_custom_call" | custom-call | flops 5242880 | bytes 10485760 | tf_op jit(solution)/shard_map/place/pallas_call | solution.py:173
  169.3 2.3 %collective-permute-start.12 = (f32[128,1024]{1,0:T(8,128)S(1)}, f32[128,1024]{1,0:T(8,128)S(1)}, u32[]{:S(2)}, u32[]{:S(2)}) collective-permute-start(f32[128,1024]{1,0:T(8,128)S(1)} %copy-done.11), channel_id=1, source_target_pairs={{0,13},{1,12},{2,15},{3,14},{4,9},{5,8},{6,11},{7,10},{8,5},{9,4},... | collective-permute-start | bytes 1572872 | tf_op jit(solution)/shard_map/ppermute | solution.py:225
  171.7 0.7 collective-permute-start.14
  172.5 2.0 %place.5.rest_2_ = f32[2048,1024]{1,0:T(8,128)} custom-call(s32[16,128]{1,0:T(8,128)S(1)} %gather_fusion, f32[2,1024]{1,0:T(2,128)S(1)} %get-tuple-element.107.scale_ref, f32[128,1024]{1,0:T(8,128)} %copy-done.2, f32[128,1024]{1,0:T(8,128)} %copy-done.3, f32[2048,1024]{1,0:T(8,128)} %place.4.rest_2_), custom_call_target="tpu_custom_call", output_to_operand_aliasing={{}: (4, {})} | custom-call | flops 1048576 | bytes 2097152 | tf_op jit(solution)/shard_map/place/pallas_call | solution.py:173
  174.5 7.4 %collective-permute-done.16.rest_1_ = f32[128,1024]{1,0:T(8,128)S(1)} collective-permute-done((f32[128,1024]{1,0:T(8,128)}, f32[128,1024]{1,0:T(8,128)S(1)}, u32[]{:S(2)}, u32[]{:S(2)}) %collective-permute-start.16) | collective-permute-done | bytes 524320 | tf_op jit(solution)/shard_map/ppermute | solution.py:225
  181.9 1.2 place.6.rest_2_
  183.2 3.8 %collective-permute-done.12.rest_0_ = f32[128,1024]{1,0:T(8,128)S(1)} collective-permute-done((f32[128,1024]{1,0:T(8,128)S(1)}, f32[128,1024]{1,0:T(8,128)S(1)}, u32[]{:S(2)}, u32[]{:S(2)}) %collective-permute-start.12) | collective-permute-done | bytes 524320 | tf_op jit(solution)/shard_map/ppermute | solution.py:225
  187.0 1.2 place.7
  (69 shorter events, 1.0 us)
Async XLA Ops:
  0.6 7.1 %copy-start = (s32[16]{0:T(128)S(1)}, s32[16]{0:T(128)}, u32[]{:S(2)}) copy-start(s32[16]{0:T(128)} %dest_ref.2) | copy-start | bytes 196
  0.6 7.1 %copy-start.1 = (s32[16]{0:T(128)S(1)}, s32[16]{0:T(128)}, u32[]{:S(2)}) copy-start(s32[16]{0:T(128)} %slot_ref) | copy-start | bytes 196
  2.7 15.1 %collective-permute-start = (f32[128,1024]{1,0:T(8,128)S(1)}, f32[128,1024]{1,0:T(8,128)S(1)}, u32[]{:S(2)}, u32[]{:S(2)}) collective-permute-start(f32[128,1024]{1,0:T(8,128)S(1)} %get-tuple-element.58), channel_id=1, source_target_pairs={{0,4},{1,5},{2,6},{3,7},{4,0},{5,1},{6,2},{7,3},{8,12},{9,13},{10,... | collective-permute-start | bytes 1572872 | tf_op jit(solution)/shard_map/ppermute | solution.py:225
  2.8 44.2 %collective-permute-start.9 = (f32[128,1024]{1,0:T(8,128)S(1)}, f32[128,1024]{1,0:T(8,128)S(1)}, u32[]{:S(2)}, u32[]{:S(2)}) collective-permute-start(f32[128,1024]{1,0:T(8,128)S(1)} %get-tuple-element.78), channel_id=1, source_target_pairs={{0,8},{1,9},{2,10},{3,11},{4,12},{5,13},{6,14},{7,15},{8,0},{9,1},... | collective-permute-start | bytes 1572872 | tf_op jit(solution)/shard_map/ppermute | solution.py:225
  15.0 31.9 %collective-permute-start.3 = (f32[128,1024]{1,0:T(8,128)}, f32[128,1024]{1,0:T(8,128)S(1)}, u32[]{:S(2)}, u32[]{:S(2)}) collective-permute-start(f32[128,1024]{1,0:T(8,128)} %get-tuple-element.67), channel_id=1, source_target_pairs={{0,3},{1,2},{2,1},{3,0},{4,7},{5,6},{6,5},{7,4},{8,11},{9,10},{10,... | collective-permute-start | bytes 1572872 | tf_op jit(solution)/shard_map/ppermute | solution.py:225
  17.5 50.8 %collective-permute-start.6 = (f32[128,1024]{1,0:T(8,128)}, f32[128,1024]{1,0:T(8,128)S(1)}, u32[]{:S(2)}, u32[]{:S(2)}) collective-permute-start(f32[128,1024]{1,0:T(8,128)} %get-tuple-element.74), channel_id=1, source_target_pairs={{0,10},{1,11},{2,8},{3,9},{4,14},{5,15},{6,12},{7,13},{8,2},{9,3},... | collective-permute-start | bytes 1572872 | tf_op jit(solution)/shard_map/ppermute | solution.py:225
  17.8 146.5 %copy-start.4 = (f32[128,1024]{1,0:T(8,128)}, f32[128,1024]{1,0:T(8,128)S(1)}, u32[]{:S(2)}) copy-start(f32[128,1024]{1,0:T(8,128)S(1)} %collective-permute-done.rest_1_) | copy-start | bytes 1572868
  17.8 50.8 %collective-permute-start.1 = (f32[128,1024]{1,0:T(8,128)}, f32[128,1024]{1,0:T(8,128)S(1)}, u32[]{:S(2)}, u32[]{:S(2)}) collective-permute-start(f32[128,1024]{1,0:T(8,128)} %get-tuple-element.60), channel_id=1, source_target_pairs={{0,5},{1,4},{2,7},{3,6},{4,1},{5,0},{6,3},{7,2},{8,13},{9,12},{10,... | collective-permute-start | bytes 1572872 | tf_op jit(solution)/shard_map/ppermute | solution.py:225
  21.2 47.4 %all-to-all-start = ((f32[16,1,256]{2,1,0:T(1,128)}), f32[16,1,256]{2,1,0:T(1,128)S(1)}, u32[]{:S(2)}, u32[]{:S(2)}) async-start(f32[16,1,256]{2,1,0:T(1,128)} %get-tuple-element.61), calls=%async_computation | async-start | bytes 32768 | tf_op jit(solution)/shard_map/all_to_all | solution.py:249
  47.0 117.4 %copy-start.5 = (f32[128,1024]{1,0:T(8,128)}, f32[128,1024]{1,0:T(8,128)S(1)}, u32[]{:S(2)}) copy-start(f32[128,1024]{1,0:T(8,128)S(1)} %collective-permute-done.9.rest_0_) | copy-start | bytes 1572868
  47.0 39.7 %collective-permute-start.10 = (f32[128,1024]{1,0:T(8,128)}, f32[128,1024]{1,0:T(8,128)S(1)}, u32[]{:S(2)}, u32[]{:S(2)}) collective-permute-start(f32[128,1024]{1,0:T(8,128)} %get-tuple-element.84), channel_id=1, source_target_pairs={{0,12},{1,13},{2,14},{3,15},{4,8},{5,9},{6,10},{7,11},{8,4},{9,5},... | collective-permute-start | bytes 1572872 | tf_op jit(solution)/shard_map/ppermute | solution.py:225
  47.0 117.4 %copy-start.6 = (f32[128,1024]{1,0:T(8,128)}, f32[128,1024]{1,0:T(8,128)S(1)}, u32[]{:S(2)}) copy-start(f32[128,1024]{1,0:T(8,128)S(1)} %collective-permute-done.3.rest_3_) | copy-start | bytes 1572868
  47.0 64.0 %collective-permute-start.4 = (f32[128,1024]{1,0:T(8,128)}, f32[128,1024]{1,0:T(8,128)}, u32[]{:S(2)}, u32[]{:S(2)}) collective-permute-start(f32[128,1024]{1,0:T(8,128)} %get-tuple-element.68), channel_id=1, source_target_pairs={{0,7},{1,6},{2,5},{3,4},{4,3},{5,2},{6,1},{7,0},{8,15},{9,14},{10,... | collective-permute-start | bytes 1572872 | tf_op jit(solution)/shard_map/ppermute | solution.py:225
  68.3 42.5 %copy-start.7 = (f32[128,1024]{1,0:T(8,128)}, f32[128,1024]{1,0:T(8,128)S(1)}, u32[]{:S(2)}) copy-start(f32[128,1024]{1,0:T(8,128)S(1)} %collective-permute-done.6.rest_2_) | copy-start | bytes 1572868
  68.3 42.5 %collective-permute-start.7 = (f32[128,1024]{1,0:T(8,128)}, f32[128,1024]{1,0:T(8,128)}, u32[]{:S(2)}, u32[]{:S(2)}) collective-permute-start(f32[128,1024]{1,0:T(8,128)} %get-tuple-element.75), channel_id=1, source_target_pairs={{0,14},{1,15},{2,12},{3,13},{4,10},{5,11},{6,8},{7,9},{8,6},{9,7},... | collective-permute-start | bytes 1572872 | tf_op jit(solution)/shard_map/ppermute | solution.py:225
  68.6 42.2 %copy-start.8 = (f32[128,1024]{1,0:T(8,128)}, f32[128,1024]{1,0:T(8,128)S(1)}, u32[]{:S(2)}) copy-start(f32[128,1024]{1,0:T(8,128)S(1)} %collective-permute-done.1.rest_5_) | copy-start | bytes 1572868
  86.7 33.2 %copy-start.9 = (f32[128,1024]{1,0:T(8,128)}, f32[128,1024]{1,0:T(8,128)S(1)}, u32[]{:S(2)}) copy-start(f32[128,1024]{1,0:T(8,128)S(1)} %collective-permute-done.10.rest_4_) | copy-start | bytes 1572868
  86.7 24.1 %collective-permute-start.5 = (f32[2,64]{1,0:T(2,128)S(1)}, f32[2,64]{1,0:T(2,128)S(1)}, u32[]{:S(2)}, u32[]{:S(2)}) collective-permute-start(f32[2,64]{1,0:T(2,128)S(1)} %pad_maximum_fusion.2), channel_id=1, source_target_pairs={{0,16},{16,0},{1,17},{17,1},{2,18},{18,2},{3,19},{19,3},{4,20},{20... | collective-permute-start | bytes 1544 | tf_op jit(solution)/shard_map/ppermute | solution.py:201
  86.8 44.4 %collective-permute-start.11 = (f32[128,1024]{1,0:T(8,128)}, f32[128,1024]{1,0:T(8,128)}, u32[]{:S(2)}, u32[]{:S(2)}) collective-permute-start(f32[128,1024]{1,0:T(8,128)} %get-tuple-element.90), channel_id=1, source_target_pairs={{0,9},{1,8},{2,11},{3,10},{4,13},{5,12},{6,15},{7,14},{8,1},{9,0},... | collective-permute-start | bytes 1572872 | tf_op jit(solution)/shard_map/ppermute | solution.py:225
  86.9 74.8 %collective-permute-start.2 = (f32[128,1024]{1,0:T(8,128)}, f32[128,1024]{1,0:T(8,128)}, u32[]{:S(2)}, u32[]{:S(2)}) collective-permute-start(f32[128,1024]{1,0:T(8,128)} %get-tuple-element.64), channel_id=1, source_target_pairs={{0,2},{1,3},{2,0},{3,1},{4,6},{5,7},{6,4},{7,5},{8,10},{9,11},{10,... | collective-permute-start | bytes 1572872 | tf_op jit(solution)/shard_map/ppermute | solution.py:225
  110.8 58.5 %collective-permute-start.8 = (f32[128,1024]{1,0:T(8,128)}, f32[128,1024]{1,0:T(8,128)S(1)}, u32[]{:S(2)}, u32[]{:S(2)}) collective-permute-start(f32[128,1024]{1,0:T(8,128)} %get-tuple-element.76), channel_id=1, source_target_pairs={{0,11},{1,10},{2,9},{3,8},{4,15},{5,14},{6,13},{7,12},{8,3},{9,2},... | collective-permute-start | bytes 1572872 | tf_op jit(solution)/shard_map/ppermute | solution.py:225
  111.5 50.1 %all-to-all-start.1 = ((f32[16,1,128]{2,1,0:T(1,128)}), f32[16,1,128]{2,1,0:T(1,128)S(1)}, u32[]{:S(2)}, u32[]{:S(2)}) async-start(f32[16,1,128]{2,1,0:T(1,128)} %broadcast_in_dim.9), calls=%async_computation.1 | async-start | bytes 16384 | tf_op jit(solution)/shard_map/all_to_all | solution.py:253
  119.9 51.8 %collective-permute-start.13 = (f32[128,1024]{1,0:T(8,128)}, f32[128,1024]{1,0:T(8,128)S(1)}, u32[]{:S(2)}, u32[]{:S(2)}) collective-permute-start(f32[128,1024]{1,0:T(8,128)} %get-tuple-element.95), channel_id=1, source_target_pairs={{0,1},{1,0},{2,3},{3,2},{4,5},{5,4},{6,7},{7,6},{8,9},{9,8},{10,11... | collective-permute-start | bytes 1572872 | tf_op jit(solution)/shard_map/ppermute | solution.py:225
  131.2 43.3 %collective-permute-start.15 = (f32[128,1024]{1,0:T(8,128)}, f32[128,1024]{1,0:T(8,128)S(1)}, u32[]{:S(2)}, u32[]{:S(2)}) collective-permute-start(f32[128,1024]{1,0:T(8,128)} %get-tuple-element.97), channel_id=1, source_target_pairs={{0,15},{1,14},{2,13},{3,12},{4,11},{5,10},{6,9},{7,8},{8,7},{9,6},... | collective-permute-start | bytes 1572872 | tf_op jit(solution)/shard_map/ppermute | solution.py:225
  161.9 7.4 %copy-start.11 = (f32[128,1024]{1,0:T(8,128)S(1)}, f32[128,1024]{1,0:T(8,128)}, u32[]{:S(2)}) copy-start(f32[128,1024]{1,0:T(8,128)} %get-tuple-element.93) | copy-start | bytes 1572868
  161.9 9.8 %copy-start.10 = (f32[128,1024]{1,0:T(8,128)S(1)}, f32[128,1024]{1,0:T(8,128)}, u32[]{:S(2)}) copy-start(f32[128,1024]{1,0:T(8,128)} %get-tuple-element.96) | copy-start | bytes 1572868
  161.9 20.0 %collective-permute-start.16 = (f32[128,1024]{1,0:T(8,128)}, f32[128,1024]{1,0:T(8,128)S(1)}, u32[]{:S(2)}, u32[]{:S(2)}) collective-permute-start(f32[128,1024]{1,0:T(8,128)} %get-tuple-element.98), channel_id=1, source_target_pairs={{0,6},{1,7},{2,4},{3,5},{4,2},{5,3},{6,0},{7,1},{8,14},{9,15},{10,... | collective-permute-start | bytes 1572872 | tf_op jit(solution)/shard_map/ppermute | solution.py:225
  169.3 3.1 %copy-start.2 = (f32[128,1024]{1,0:T(8,128)}, f32[128,1024]{1,0:T(8,128)S(1)}, u32[]{:S(2)}) copy-start(f32[128,1024]{1,0:T(8,128)S(1)} %collective-permute-done.8.rest_0_) | copy-start | bytes 1572868
  169.3 17.7 %collective-permute-start.12 = (f32[128,1024]{1,0:T(8,128)S(1)}, f32[128,1024]{1,0:T(8,128)S(1)}, u32[]{:S(2)}, u32[]{:S(2)}) collective-permute-start(f32[128,1024]{1,0:T(8,128)S(1)} %copy-done.11), channel_id=1, source_target_pairs={{0,13},{1,12},{2,15},{3,14},{4,9},{5,8},{6,11},{7,10},{8,5},{9,4},... | collective-permute-start | bytes 1572872 | tf_op jit(solution)/shard_map/ppermute | solution.py:225
  171.7 0.8 copy-start.3
  171.7 15.3 %collective-permute-start.14 = (f32[128,1024]{1,0:T(8,128)S(1)}, f32[128,1024]{1,0:T(8,128)S(1)}, u32[]{:S(2)}, u32[]{:S(2)}) collective-permute-start(f32[128,1024]{1,0:T(8,128)S(1)} %copy-done.10), channel_id=1, source_target_pairs={{0,0},{1,1},{2,2},{3,3},{4,4},{5,5},{6,6},{7,7},{8,8},{9,9},{10,10... | collective-permute-start | bytes 1572872 | tf_op jit(solution)/shard_map/ppermute | solution.py:225

commit v9 on v7

--- a/solution.py
+++ b/solution.py
@@ -34,6 +34,7 @@
     half, quarter = peers // 2, peers // 4
     far = [half + k for k in (*range(0, half, 2), *range(1, half, 2))]
     far[-2:] = far[:-3:-1]
+    far[1], far[3] = far[3], far[1]
     near = [*range(1, half, 2), *range(2, half, 2), 0]
     at = near.index(quarter)
     near[0], near[at] = quarter, near[0]

time: 189 us -> 189 us (level)
  waiting for transfers between devices: 124 us -> 121 us
  starting transfers between devices: 41.8 us -> 44.6 us
    ppermute x16, starting transfers between devices: 27.5 us -> 33.9 us  [send(): return lax.ppermute(block, ('outer', 'inner'), pairs)]
    ppermute x16, waiting for transfers between devices: 95.2 us -> 90.8 us  [send(): return lax.ppermute(block, ('outer', 'inner'), pairs)]
    all_to_all x2, starting transfers between devices: 14.2 us -> 10.6 us  [body(): lax.all_to_all(extra[0], 'inner', split_axis=0, concat_axis=0, tiled=True)]
  transfers between devices with their start and end apart: 19 -> 19, of which waited for: 9 -> 10; matrix products, arithmetic and copies ran while one was open for 1% -> 1% of each run, Pallas kernels for 8% -> 8%
where the time goes in v9:
time: 189 us; the launch traced here: 188 us
  waiting for transfers between devices  121 us (64%)
  starting transfers between devices  44.6 us (24%)
  Pallas kernels  18.8 us (10%)
    ppermute x16, waiting for transfers between devices, send(): return lax.ppermute(block, ('outer', 'inner'), pairs)  90.8 us
    ppermute x16, starting transfers between devices, send(): return lax.ppermute(block, ('outer', 'inner'), pairs)  33.9 us
    all_to_all x2, waiting for transfers between devices, body(): lax.all_to_all(extra[0], 'inner', split_axis=0, concat_axis=0, tiled=True)  30.5 us
    all_to_all x2, starting transfers between devices, body(): lax.all_to_all(extra[0], 'inner', split_axis=0, concat_axis=0, tiled=True)  10.6 us
    pallas_call x4, Pallas kernels, place(): pl.pallas_call(functools.partial(place_kernel, lanes, near_by), out_shape...  9.44 us
    pallas_call x1, Pallas kernels, pick_rest(): pl.pallas_call(functools.partial(rest_kernel, lanes, first), out_shape=[j...  7.29 us
  transfers between devices with their start and end apart: 19, of which 10 were waited for; matrix products, arithmetic and copies ran while one was open for 1% of the time, Pallas kernels for 8%

profile of v9, /device:TPU:8, one launch (start us, length us, event | category | flops | bytes accessed | tf_op | source)
XLA Modules:
  0.0 188.2 jit_solution(998815768357410702)
XLA Ops:
  0.6 2.0 %pick_first.1 = (f32[128,1024]{1,0:T(8,128)S(1)}, f32[128,1024]{1,0:T(8,128)S(1)}) custom-call(s32[16]{0:T(128)} %dest_ref.2, f32[2048,1024]{1,0:T(8,128)} %features_ref.3), custom_call_target="tpu_custom_call" | custom-call | tf_op jit(solution)/shard_map/pick_first/pallas_call | solution.py:78
  2.8 4.9 %collective-permute-start.9 = (f32[128,1024]{1,0:T(8,128)S(1)}, f32[128,1024]{1,0:T(8,128)S(1)}, u32[]{:S(2)}, u32[]{:S(2)}) collective-permute-start(f32[128,1024]{1,0:T(8,128)S(1)} %get-tuple-element.78), channel_id=1, source_target_pairs={{0,8},{1,9},{2,10},{3,11},{4,12},{5,13},{6,14},{7,15},{8,0},{9,1},... | collective-permute-start | bytes 1572872 | tf_op jit(solution)/shard_map/ppermute | solution.py:227
  7.7 7.3 %pick_rest.1 = (f32[16,1,256]{2,1,0:T(1,128)}, f32[128,1024]{1,0:T(8,128)}, f32[128,1024]{1,0:T(8,128)}, f32[128,1024]{1,0:T(8,128)}, f32[128,1024]{1,0:T(8,128)...) custom-call(s32[16]{0:T(128)S(1)} %copy-done, ...), custom_call_target="tpu_custom_call" | custom-call | flops 12582912 | bytes 16777216 | tf_op jit(solution)/shard_map/pick_rest/pallas_call | solution.py:128
  15.0 2.5 %collective-permute-start.3 = (f32[128,1024]{1,0:T(8,128)}, f32[128,1024]{1,0:T(8,128)S(1)}, u32[]{:S(2)}, u32[]{:S(2)}) collective-permute-start(f32[128,1024]{1,0:T(8,128)} %get-tuple-element.67), channel_id=1, source_target_pairs={{0,3},{1,2},{2,1},{3,0},{4,7},{5,6},{6,5},{7,4},{8,11},{9,10},{10,... | collective-permute-start | bytes 1572872 | tf_op jit(solution)/shard_map/ppermute | solution.py:227
  17.9 0.6 collective-permute-done.rest_1_
  18.5 4.3 %collective-permute-start.1 = (f32[128,1024]{1,0:T(8,128)}, f32[128,1024]{1,0:T(8,128)S(1)}, u32[]{:S(2)}, u32[]{:S(2)}) collective-permute-start(f32[128,1024]{1,0:T(8,128)} %get-tuple-element.60), channel_id=1, source_target_pairs={{0,5},{1,4},{2,7},{3,6},{4,1},{5,0},{6,3},{7,2},{8,13},{9,12},{10,... | collective-permute-start | bytes 1572872 | tf_op jit(solution)/shard_map/ppermute | solution.py:227
  22.8 6.3 %all-to-all-start = ((f32[16,1,256]{2,1,0:T(1,128)}), f32[16,1,256]{2,1,0:T(1,128)S(1)}, u32[]{:S(2)}, u32[]{:S(2)}) async-start(f32[16,1,256]{2,1,0:T(1,128)} %get-tuple-element.61), calls=%async_computation | async-start | bytes 32768 | tf_op jit(solution)/shard_map/all_to_all | solution.py:251
  29.1 13.0 %collective-permute-done.9.rest_0_ = f32[128,1024]{1,0:T(8,128)S(1)} collective-permute-done((f32[128,1024]{1,0:T(8,128)S(1)}, f32[128,1024]{1,0:T(8,128)S(1)}, u32[]{:S(2)}, u32[]{:S(2)}) %collective-permute-start.9) | collective-permute-done | bytes 524320 | tf_op jit(solution)/shard_map/ppermute | solution.py:227
  42.1 7.2 %collective-permute-start.4 = (f32[128,1024]{1,0:T(8,128)}, f32[128,1024]{1,0:T(8,128)}, u32[]{:S(2)}, u32[]{:S(2)}) collective-permute-start(f32[128,1024]{1,0:T(8,128)} %get-tuple-element.68), channel_id=1, source_target_pairs={{0,7},{1,6},{2,5},{3,4},{4,3},{5,2},{6,1},{7,0},{8,15},{9,14},{10,... | collective-permute-start | bytes 1572872 | tf_op jit(solution)/shard_map/ppermute | solution.py:227
  49.3 17.0 %collective-permute-done.6.rest_2_ = f32[128,1024]{1,0:T(8,128)S(1)} collective-permute-done((f32[128,1024]{1,0:T(8,128)}, f32[128,1024]{1,0:T(8,128)S(1)}, u32[]{:S(2)}, u32[]{:S(2)}) %collective-permute-start.6) | collective-permute-done | bytes 524320 | tf_op jit(solution)/shard_map/ppermute | solution.py:227
  66.4 1.7 all-to-all-done
  68.5 18.2 %collective-permute-done.10.rest_4_ = f32[128,1024]{1,0:T(8,128)S(1)} collective-permute-done((f32[128,1024]{1,0:T(8,128)}, f32[128,1024]{1,0:T(8,128)S(1)}, u32[]{:S(2)}, u32[]{:S(2)}) %collective-permute-start.10) | collective-permute-done | bytes 524320 | tf_op jit(solution)/shard_map/ppermute | solution.py:227
  86.8 1.6 collective-permute-start.2
  88.4 20.7 %collective-permute-done.7.rest_6_ = f32[128,1024]{1,0:T(8,128)} collective-permute-done((f32[128,1024]{1,0:T(8,128)}, f32[128,1024]{1,0:T(8,128)}, u32[]{:S(2)}, u32[]{:S(2)}) %collective-permute-start.7) | collective-permute-done | bytes 524320 | tf_op jit(solution)/shard_map/ppermute | solution.py:227
  109.1 5.2 %collective-permute-start.8 = (f32[128,1024]{1,0:T(8,128)}, f32[128,1024]{1,0:T(8,128)S(1)}, u32[]{:S(2)}, u32[]{:S(2)}) collective-permute-start(f32[128,1024]{1,0:T(8,128)} %get-tuple-element.76), channel_id=1, source_target_pairs={{0,11},{1,10},{2,9},{3,8},{4,15},{5,14},{6,13},{7,12},{8,3},{9,2},... | collective-permute-start | bytes 1572872 | tf_op jit(solution)/shard_map/ppermute | solution.py:227
  114.4 0.6 broadcast_in_dim.9
  115.0 4.3 %all-to-all-start.1 = ((f32[16,1,128]{2,1,0:T(1,128)}), f32[16,1,128]{2,1,0:T(1,128)S(1)}, u32[]{:S(2)}, u32[]{:S(2)}) async-start(f32[16,1,128]{2,1,0:T(1,128)} %broadcast_in_dim.9), calls=%async_computation.1 | async-start | bytes 16384 | tf_op jit(solution)/shard_map/all_to_all | solution.py:255
  119.3 1.5 collective-permute-start.13
  120.9 0.6 gather_fusion
  121.4 10.3 %collective-permute-done.11.rest_8_ = f32[128,1024]{1,0:T(8,128)} collective-permute-done((f32[128,1024]{1,0:T(8,128)}, f32[128,1024]{1,0:T(8,128)}, u32[]{:S(2)}, u32[]{:S(2)}) %collective-permute-start.11) | collective-permute-done | bytes 524320 | tf_op jit(solution)/shard_map/ppermute | solution.py:227
  131.7 1.2 collective-permute-start.15
  132.9 28.8 %all-to-all-done.1 = f32[16,1,128]{2,1,0:T(1,128)S(1)} async-done(((f32[16,1,128]{2,1,0:T(1,128)}), f32[16,1,128]{2,1,0:T(1,128)S(1)}, u32[]{:S(2)}, u32[]{:S(2)}) %all-to-all-start.1) | async-done | bytes 8224 | tf_op jit(solution)/shard_map/all_to_all | solution.py:255
  161.9 1.7 collective-permute-start.16
  163.6 0.6 pad_maximum_fusion
  164.2 5.0 %place.4.rest_2_ = f32[2048,1024]{1,0:T(8,128)} custom-call(s32[16,128]{1,0:T(8,128)S(1)} %gather_fusion, f32[2,1024]{1,0:T(2,128)S(1)} %get-tuple-element.107.scale_ref, f32[128,1024]{1,0:T(8,128)} %copy-done.5, f32[128,1024]{1,0:T(8,128)} %copy-done.4, f32[128,1024]{1,0:T(8,128)} %copy-done.7, f32[128,1024]{1,0:T(8,128)} %copy-done.6, ...), custom_call_target="tpu_custom_call" | custom-call | flops 5242880 | bytes 10485760 | tf_op jit(solution)/shard_map/place/pallas_call | solution.py:175
  169.3 2.6 %collective-permute-start.12 = (f32[128,1024]{1,0:T(8,128)S(1)}, f32[128,1024]{1,0:T(8,128)S(1)}, u32[]{:S(2)}, u32[]{:S(2)}) collective-permute-start(f32[128,1024]{1,0:T(8,128)S(1)} %copy-done.11), channel_id=1, source_target_pairs={{0,13},{1,12},{2,15},{3,14},{4,9},{5,8},{6,11},{7,10},{8,5},{9,4},... | collective-permute-start | bytes 1572872 | tf_op jit(solution)/shard_map/ppermute | solution.py:227
  171.8 0.7 collective-permute-start.14
  172.6 2.0 %place.5.rest_2_ = f32[2048,1024]{1,0:T(8,128)} custom-call(s32[16,128]{1,0:T(8,128)S(1)} %gather_fusion, f32[2,1024]{1,0:T(2,128)S(1)} %get-tuple-element.107.scale_ref, f32[128,1024]{1,0:T(8,128)} %copy-done.2, f32[128,1024]{1,0:T(8,128)} %copy-done.3, f32[2048,1024]{1,0:T(8,128)} %place.4.rest_2_), custom_call_target="tpu_custom_call", output_to_operand_aliasing={{}: (4, {})} | custom-call | flops 1048576 | bytes 2097152 | tf_op jit(solution)/shard_map/place/pallas_call | solution.py:175
  174.6 7.2 %collective-permute-done.16.rest_1_ = f32[128,1024]{1,0:T(8,128)S(1)} collective-permute-done((f32[128,1024]{1,0:T(8,128)}, f32[128,1024]{1,0:T(8,128)S(1)}, u32[]{:S(2)}, u32[]{:S(2)}) %collective-permute-start.16) | collective-permute-done | bytes 524320 | tf_op jit(solution)/shard_map/ppermute | solution.py:227
  181.9 1.2 place.6.rest_2_
  183.1 3.8 %collective-permute-done.12.rest_0_ = f32[128,1024]{1,0:T(8,128)S(1)} collective-permute-done((f32[128,1024]{1,0:T(8,128)S(1)}, f32[128,1024]{1,0:T(8,128)S(1)}, u32[]{:S(2)}, u32[]{:S(2)}) %collective-permute-start.12) | collective-permute-done | bytes 524320 | tf_op jit(solution)/shard_map/ppermute | solution.py:227
  186.9 1.2 place.7
  (69 shorter events, 1.5 us)
Async XLA Ops:
  0.6 7.1 %copy-start = (s32[16]{0:T(128)S(1)}, s32[16]{0:T(128)}, u32[]{:S(2)}) copy-start(s32[16]{0:T(128)} %dest_ref.2) | copy-start | bytes 196
  0.6 7.1 %copy-start.1 = (s32[16]{0:T(128)S(1)}, s32[16]{0:T(128)}, u32[]{:S(2)}) copy-start(s32[16]{0:T(128)} %slot_ref) | copy-start | bytes 196
  2.7 15.8 %collective-permute-start = (f32[128,1024]{1,0:T(8,128)S(1)}, f32[128,1024]{1,0:T(8,128)S(1)}, u32[]{:S(2)}, u32[]{:S(2)}) collective-permute-start(f32[128,1024]{1,0:T(8,128)S(1)} %get-tuple-element.58), channel_id=1, source_target_pairs={{0,4},{1,5},{2,6},{3,7},{4,0},{5,1},{6,2},{7,3},{8,12},{9,13},{10,... | collective-permute-start | bytes 1572872 | tf_op jit(solution)/shard_map/ppermute | solution.py:227
  2.8 39.3 %collective-permute-start.9 = (f32[128,1024]{1,0:T(8,128)S(1)}, f32[128,1024]{1,0:T(8,128)S(1)}, u32[]{:S(2)}, u32[]{:S(2)}) collective-permute-start(f32[128,1024]{1,0:T(8,128)S(1)} %get-tuple-element.78), channel_id=1, source_target_pairs={{0,8},{1,9},{2,10},{3,11},{4,12},{5,13},{6,14},{7,15},{8,0},{9,1},... | collective-permute-start | bytes 1572872 | tf_op jit(solution)/shard_map/ppermute | solution.py:227
  15.0 27.1 %collective-permute-start.3 = (f32[128,1024]{1,0:T(8,128)}, f32[128,1024]{1,0:T(8,128)S(1)}, u32[]{:S(2)}, u32[]{:S(2)}) collective-permute-start(f32[128,1024]{1,0:T(8,128)} %get-tuple-element.67), channel_id=1, source_target_pairs={{0,3},{1,2},{2,1},{3,0},{4,7},{5,6},{6,5},{7,4},{8,11},{9,10},{10,... | collective-permute-start | bytes 1572872 | tf_op jit(solution)/shard_map/ppermute | solution.py:227
  17.5 48.8 %collective-permute-start.6 = (f32[128,1024]{1,0:T(8,128)}, f32[128,1024]{1,0:T(8,128)S(1)}, u32[]{:S(2)}, u32[]{:S(2)}) collective-permute-start(f32[128,1024]{1,0:T(8,128)} %get-tuple-element.74), channel_id=1, source_target_pairs={{0,14},{1,15},{2,12},{3,13},{4,10},{5,11},{6,8},{7,9},{8,6},{9,7},... | collective-permute-start | bytes 1572872 | tf_op jit(solution)/shard_map/ppermute | solution.py:227
  18.5 145.7 %copy-start.4 = (f32[128,1024]{1,0:T(8,128)}, f32[128,1024]{1,0:T(8,128)S(1)}, u32[]{:S(2)}) copy-start(f32[128,1024]{1,0:T(8,128)S(1)} %collective-permute-done.rest_1_) | copy-start | bytes 1572868
  18.5 49.6 %collective-permute-start.1 = (f32[128,1024]{1,0:T(8,128)}, f32[128,1024]{1,0:T(8,128)S(1)}, u32[]{:S(2)}, u32[]{:S(2)}) collective-permute-start(f32[128,1024]{1,0:T(8,128)} %get-tuple-element.60), channel_id=1, source_target_pairs={{0,5},{1,4},{2,7},{3,6},{4,1},{5,0},{6,3},{7,2},{8,13},{9,12},{10,... | collective-permute-start | bytes 1572872 | tf_op jit(solution)/shard_map/ppermute | solution.py:227
  22.8 45.3 %all-to-all-start = ((f32[16,1,256]{2,1,0:T(1,128)}), f32[16,1,256]{2,1,0:T(1,128)S(1)}, u32[]{:S(2)}, u32[]{:S(2)}) async-start(f32[16,1,256]{2,1,0:T(1,128)} %get-tuple-element.61), calls=%async_computation | async-start | bytes 32768 | tf_op jit(solution)/shard_map/all_to_all | solution.py:251
  42.1 122.1 %copy-start.5 = (f32[128,1024]{1,0:T(8,128)}, f32[128,1024]{1,0:T(8,128)S(1)}, u32[]{:S(2)}) copy-start(f32[128,1024]{1,0:T(8,128)S(1)} %collective-permute-done.9.rest_0_) | copy-start | bytes 1572868
  42.1 44.5 %collective-permute-start.10 = (f32[128,1024]{1,0:T(8,128)}, f32[128,1024]{1,0:T(8,128)S(1)}, u32[]{:S(2)}, u32[]{:S(2)}) collective-permute-start(f32[128,1024]{1,0:T(8,128)} %get-tuple-element.84), channel_id=1, source_target_pairs={{0,12},{1,13},{2,14},{3,15},{4,8},{5,9},{6,10},{7,11},{8,4},{9,5},... | collective-permute-start | bytes 1572872 | tf_op jit(solution)/shard_map/ppermute | solution.py:227
  42.1 122.1 %copy-start.6 = (f32[128,1024]{1,0:T(8,128)}, f32[128,1024]{1,0:T(8,128)S(1)}, u32[]{:S(2)}) copy-start(f32[128,1024]{1,0:T(8,128)S(1)} %collective-permute-done.3.rest_3_) | copy-start | bytes 1572868
  42.1 72.3 %collective-permute-start.4 = (f32[128,1024]{1,0:T(8,128)}, f32[128,1024]{1,0:T(8,128)}, u32[]{:S(2)}, u32[]{:S(2)}) collective-permute-start(f32[128,1024]{1,0:T(8,128)} %get-tuple-element.68), channel_id=1, source_target_pairs={{0,7},{1,6},{2,5},{3,4},{4,3},{5,2},{6,1},{7,0},{8,15},{9,14},{10,... | collective-permute-start | bytes 1572872 | tf_op jit(solution)/shard_map/ppermute | solution.py:227
  66.4 42.8 %copy-start.7 = (f32[128,1024]{1,0:T(8,128)}, f32[128,1024]{1,0:T(8,128)S(1)}, u32[]{:S(2)}) copy-start(f32[128,1024]{1,0:T(8,128)S(1)} %collective-permute-done.6.rest_2_) | copy-start | bytes 1572868
  66.4 42.8 %collective-permute-start.7 = (f32[128,1024]{1,0:T(8,128)}, f32[128,1024]{1,0:T(8,128)}, u32[]{:S(2)}, u32[]{:S(2)}) collective-permute-start(f32[128,1024]{1,0:T(8,128)} %get-tuple-element.75), channel_id=1, source_target_pairs={{0,10},{1,11},{2,8},{3,9},{4,14},{5,15},{6,12},{7,13},{8,2},{9,3},... | collective-permute-start | bytes 1572872 | tf_op jit(solution)/shard_map/ppermute | solution.py:227
  68.1 41.0 %copy-start.8 = (f32[128,1024]{1,0:T(8,128)}, f32[128,1024]{1,0:T(8,128)S(1)}, u32[]{:S(2)}) copy-start(f32[128,1024]{1,0:T(8,128)S(1)} %collective-permute-done.1.rest_5_) | copy-start | bytes 1572868
  86.6 32.7 %copy-start.9 = (f32[128,1024]{1,0:T(8,128)}, f32[128,1024]{1,0:T(8,128)S(1)}, u32[]{:S(2)}) copy-start(f32[128,1024]{1,0:T(8,128)S(1)} %collective-permute-done.10.rest_4_) | copy-start | bytes 1572868
  86.7 27.7 %collective-permute-start.5 = (f32[2,64]{1,0:T(2,128)S(1)}, f32[2,64]{1,0:T(2,128)S(1)}, u32[]{:S(2)}, u32[]{:S(2)}) collective-permute-start(f32[2,64]{1,0:T(2,128)S(1)} %pad_maximum_fusion.2), channel_id=1, source_target_pairs={{0,16},{16,0},{1,17},{17,1},{2,18},{18,2},{3,19},{19,3},{4,20},{20... | collective-permute-start | bytes 1544 | tf_op jit(solution)/shard_map/ppermute | solution.py:203
  86.7 44.9 %collective-permute-start.11 = (f32[128,1024]{1,0:T(8,128)}, f32[128,1024]{1,0:T(8,128)}, u32[]{:S(2)}, u32[]{:S(2)}) collective-permute-start(f32[128,1024]{1,0:T(8,128)} %get-tuple-element.90), channel_id=1, source_target_pairs={{0,9},{1,8},{2,11},{3,10},{4,13},{5,12},{6,15},{7,14},{8,1},{9,0},... | collective-permute-start | bytes 1572872 | tf_op jit(solution)/shard_map/ppermute | solution.py:227
  86.8 74.8 %collective-permute-start.2 = (f32[128,1024]{1,0:T(8,128)}, f32[128,1024]{1,0:T(8,128)}, u32[]{:S(2)}, u32[]{:S(2)}) collective-permute-start(f32[128,1024]{1,0:T(8,128)} %get-tuple-element.64), channel_id=1, source_target_pairs={{0,2},{1,3},{2,0},{3,1},{4,6},{5,7},{6,4},{7,5},{8,10},{9,11},{10,... | collective-permute-start | bytes 1572872 | tf_op jit(solution)/shard_map/ppermute | solution.py:227
  109.1 60.1 %collective-permute-start.8 = (f32[128,1024]{1,0:T(8,128)}, f32[128,1024]{1,0:T(8,128)S(1)}, u32[]{:S(2)}, u32[]{:S(2)}) collective-permute-start(f32[128,1024]{1,0:T(8,128)} %get-tuple-element.76), channel_id=1, source_target_pairs={{0,11},{1,10},{2,9},{3,8},{4,15},{5,14},{6,13},{7,12},{8,3},{9,2},... | collective-permute-start | bytes 1572872 | tf_op jit(solution)/shard_map/ppermute | solution.py:227
  115.0 46.6 %all-to-all-start.1 = ((f32[16,1,128]{2,1,0:T(1,128)}), f32[16,1,128]{2,1,0:T(1,128)S(1)}, u32[]{:S(2)}, u32[]{:S(2)}) async-start(f32[16,1,128]{2,1,0:T(1,128)} %broadcast_in_dim.9), calls=%async_computation.1 | async-start | bytes 16384 | tf_op jit(solution)/shard_map/all_to_all | solution.py:255
  119.3 52.5 %collective-permute-start.13 = (f32[128,1024]{1,0:T(8,128)}, f32[128,1024]{1,0:T(8,128)S(1)}, u32[]{:S(2)}, u32[]{:S(2)}) collective-permute-start(f32[128,1024]{1,0:T(8,128)} %get-tuple-element.95), channel_id=1, source_target_pairs={{0,1},{1,0},{2,3},{3,2},{4,5},{5,4},{6,7},{7,6},{8,9},{9,8},{10,11... | collective-permute-start | bytes 1572872 | tf_op jit(solution)/shard_map/ppermute | solution.py:227
  131.7 43.0 %collective-permute-start.15 = (f32[128,1024]{1,0:T(8,128)}, f32[128,1024]{1,0:T(8,128)S(1)}, u32[]{:S(2)}, u32[]{:S(2)}) collective-permute-start(f32[128,1024]{1,0:T(8,128)} %get-tuple-element.97), channel_id=1, source_target_pairs={{0,15},{1,14},{2,13},{3,12},{4,11},{5,10},{6,9},{7,8},{8,7},{9,6},... | collective-permute-start | bytes 1572872 | tf_op jit(solution)/shard_map/ppermute | solution.py:227
  161.9 7.4 %copy-start.11 = (f32[128,1024]{1,0:T(8,128)S(1)}, f32[128,1024]{1,0:T(8,128)}, u32[]{:S(2)}) copy-start(f32[128,1024]{1,0:T(8,128)} %get-tuple-element.93) | copy-start | bytes 1572868
  161.9 9.9 %copy-start.10 = (f32[128,1024]{1,0:T(8,128)S(1)}, f32[128,1024]{1,0:T(8,128)}, u32[]{:S(2)}) copy-start(f32[128,1024]{1,0:T(8,128)} %get-tuple-element.96) | copy-start | bytes 1572868
  161.9 20.0 %collective-permute-start.16 = (f32[128,1024]{1,0:T(8,128)}, f32[128,1024]{1,0:T(8,128)S(1)}, u32[]{:S(2)}, u32[]{:S(2)}) collective-permute-start(f32[128,1024]{1,0:T(8,128)} %get-tuple-element.98), channel_id=1, source_target_pairs={{0,6},{1,7},{2,4},{3,5},{4,2},{5,3},{6,0},{7,1},{8,14},{9,15},{10,... | collective-permute-start | bytes 1572872 | tf_op jit(solution)/shard_map/ppermute | solution.py:227
  169.2 3.3 %copy-start.2 = (f32[128,1024]{1,0:T(8,128)}, f32[128,1024]{1,0:T(8,128)S(1)}, u32[]{:S(2)}) copy-start(f32[128,1024]{1,0:T(8,128)S(1)} %collective-permute-done.8.rest_0_) | copy-start | bytes 1572868
  169.3 17.7 %collective-permute-start.12 = (f32[128,1024]{1,0:T(8,128)S(1)}, f32[128,1024]{1,0:T(8,128)S(1)}, u32[]{:S(2)}, u32[]{:S(2)}) collective-permute-start(f32[128,1024]{1,0:T(8,128)S(1)} %copy-done.11), channel_id=1, source_target_pairs={{0,13},{1,12},{2,15},{3,14},{4,9},{5,8},{6,11},{7,10},{8,5},{9,4},... | collective-permute-start | bytes 1572872 | tf_op jit(solution)/shard_map/ppermute | solution.py:227
  171.8 0.8 copy-start.3
  171.8 15.1 %collective-permute-start.14 = (f32[128,1024]{1,0:T(8,128)S(1)}, f32[128,1024]{1,0:T(8,128)S(1)}, u32[]{:S(2)}, u32[]{:S(2)}) collective-permute-start(f32[128,1024]{1,0:T(8,128)S(1)} %copy-done.10), channel_id=1, source_target_pairs={{0,0},{1,1},{2,2},{3,3},{4,4},{5,5},{6,6},{7,7},{8,8},{9,9},{10,10... | collective-permute-start | bytes 1572872 | tf_op jit(solution)/shard_map/ppermute | solution.py:227
